TPU v7x, 32 devices: a whole 2x2x4 slice. The times are simulated.
32 devices in a mesh: wide: 8 (over z, y), narrow: 4 (over x, core).
Axes of the slice: x: 2, y: 2, z: 4, core: 2. Of those that a mesh axis runs over, the one named last changes fastest.
Arguments:
- tag_states: bfloat16 [96, 512, 512], P(('wide', 'narrow')), may hold values from -6 to 6
- image_memory: bfloat16 [96, 784, 512], P(('wide', 'narrow')), may hold values from -6 to 6
- tag_lengths: int32 [96], P(('wide', 'narrow')), may hold values from 20 to 512, as said below
- w_self: bfloat16 [512, 1536], P(('wide', 'narrow')), may hold values from -0.25 to 0.25
- w_cross: bfloat16 [512, 1536], P(('wide', 'narrow')), may hold values from -0.25 to 0.25
- w_proj: bfloat16 [2, 512, 512], P(None, ('wide', 'narrow')), may hold values from -1 to 1
- w_in: bfloat16 [512, 1024], P(('wide', 'narrow')), may hold values from -0.25 to 0.25
- b_in: bfloat16 [1024], P(('wide', 'narrow')), may hold values from -1.75 to 1.75
- w_out: bfloat16 [1024, 512], P(('wide', 'narrow')), may hold values from -0.1875 to 0.1875
- ln_gains: bfloat16 [3, 512], P(None, ('wide', 'narrow')), may hold values from 0.099609375 to 1.8984375
- biases: bfloat16 [10, 512], P(None, ('wide', 'narrow')), may hold values from -1.75 to 1.75
- out_grad: bfloat16 [96, 512, 512], P(('wide', 'narrow')), may hold values from -6 to 6
Outputs:
- layer_out: bfloat16 [96, 512, 512], P(('wide', 'narrow'))
- grad_tags: float32 [96, 512, 512], P(('wide', 'narrow'))
- grad_memory: float32 [96, 784, 512], P(('wide', 'narrow'))
- grad_w_self: float32 [512, 1536], P(('wide', 'narrow'))
- grad_w_cross: float32 [512, 1536], P(('wide', 'narrow'))
- grad_w_proj: float32 [2, 512, 512], P(None, ('wide', 'narrow'))
- grad_w_in: float32 [512, 1024], P(('wide', 'narrow'))
- grad_b_in: float32 [1024], P(('wide', 'narrow'))
- grad_w_out: float32 [1024, 512], P(('wide', 'narrow'))
- grad_gains: float32 [3, 512], P(None, ('wide', 'narrow'))
- grad_biases: float32 [10, 512], P(None, ('wide', 'narrow'))
Inputs may be any that keep to these rules, and one draw needn't show every extreme that they name: `tag_lengths`: each image's number of tags; some image has exactly 512 and some exactly 20.
All inputs are finite; a program needn't handle non-finite values.
Results may differ from a plain program's by a relative error of at most 0.02.
Values may be sent and summed in bfloat16 or wider, within the bound.
A program may use at most 256 MiB of HBM per device.

v0:
```python
import jax
import jax.numpy as jnp
from jax import lax
from jax.sharding import PartitionSpec as P

HEADS = 8
HEAD_DIM = 64


epsilon = 1e-05
masked_fill = -1000000000.0


def matmul(left, right):
    return jnp.dot(left, right, preferred_element_type=jnp.float32)


def left_t(left, right):
    return lax.dot_general(
        left, right, (((0,), (0,)), ((), ())), preferred_element_type=jnp.float32
    )


def right_t(left, right):
    return lax.dot_general(
        left, right, (((1,), (1,)), ((), ())), preferred_element_type=jnp.float32
    )


def layer_norm(resid, gain, shift):
    centred = resid - jnp.mean(resid, -1, keepdims=True)
    spread = jnp.mean(centred * centred, -1, keepdims=True)
    return centred * lax.rsqrt(spread + epsilon) * gain + shift


def split_heads(rows):
    return rows.reshape(rows.shape[0], HEADS, HEAD_DIM)


def head_scores(queries, key_rows, allowed):
    scores = jnp.einsum(
        "qhd,khd->hqk",
        split_heads(queries),
        split_heads(key_rows),
        preferred_element_type=jnp.float32,
    ) * HEAD_DIM ** (-0.5)
    return jnp.where(allowed[None], scores, masked_fill)


def attend(queries, key_rows, value_rows, allowed):
    scores = head_scores(queries, key_rows, allowed)
    row_max = jnp.max(scores, -1, keepdims=True)
    expsum = jnp.exp(scores - row_max)
    summed = jnp.sum(expsum, -1, keepdims=True)
    softmax_w = (expsum / summed).astype(jnp.bfloat16)
    mixed_out = jnp.einsum(
        "hqk,khd->qhd", softmax_w, split_heads(value_rows), preferred_element_type=jnp.float32
    )
    return (mixed_out.reshape(queries.shape[0], HEADS * HEAD_DIM), row_max + jnp.log(summed))


def attend_back(queries, key_rows, value_rows, allowed, log_total, grad_mixed):
    scores = head_scores(queries, key_rows, allowed)
    softmax_w = jnp.where(allowed[None], jnp.exp(scores - log_total), 0.0)
    grad_heads = split_heads(grad_mixed)
    grad_probs = jnp.einsum(
        "qhd,khd->hqk", grad_heads, split_heads(value_rows), preferred_element_type=jnp.float32
    )
    grad_values = jnp.einsum(
        "hqk,qhd->khd",
        softmax_w.astype(jnp.bfloat16),
        grad_heads,
        preferred_element_type=jnp.float32,
    )
    inner_sum = jnp.sum(grad_probs * softmax_w, -1, keepdims=True)
    grad_scores = (softmax_w * (grad_probs - inner_sum)).astype(jnp.bfloat16)
    head_scale = HEAD_DIM ** (-0.5)
    grad_queries = (
        jnp.einsum(
            "hqk,khd->qhd", grad_scores, split_heads(key_rows), preferred_element_type=jnp.float32
        )
        * head_scale
    )
    grad_keys = (
        jnp.einsum(
            "hqk,qhd->khd", grad_scores, split_heads(queries), preferred_element_type=jnp.float32
        )
        * head_scale
    )
    width_all = HEADS * HEAD_DIM
    return (
        grad_queries.reshape(queries.shape[0], width_all),
        grad_keys.reshape(key_rows.shape[0], width_all),
        grad_values.reshape(key_rows.shape[0], width_all),
    )


def per_device(
    tag_states,
    image_memory,
    tag_lengths,
    w_self,
    w_cross,
    w_proj,
    w_in,
    b_in,
    w_out,
    ln_gains,
    biases,
    out_grad,
):
    gathered = (
        lax.all_gather(w_self, ("wide", "narrow"), axis=0, tiled=True),
        lax.all_gather(w_cross, ("wide", "narrow"), axis=0, tiled=True),
        lax.all_gather(w_proj, ("wide", "narrow"), axis=1, tiled=True),
        lax.all_gather(w_in, ("wide", "narrow"), axis=0, tiled=True),
        lax.all_gather(b_in, ("wide", "narrow"), axis=0, tiled=True),
        lax.all_gather(w_out, ("wide", "narrow"), axis=0, tiled=True),
        lax.all_gather(ln_gains, ("wide", "narrow"), axis=1, tiled=True),
        lax.all_gather(biases, ("wide", "narrow"), axis=1, tiled=True),
    )
    images, tag_len, model_width = tag_states.shape
    memory_len = image_memory.shape[1]
    query_pos = lax.broadcasted_iota(jnp.int32, (tag_len, tag_len), 0)
    key_pos = lax.broadcasted_iota(jnp.int32, (tag_len, tag_len), 1)
    allowed_self = (key_pos <= query_pos)[None] & (key_pos[None] < tag_lengths[:, None, None])
    valid_rows = (
        (query_pos[:, 0][None] < tag_lengths[:, None])
        .astype(jnp.float32)
        .reshape(images * tag_len, 1)
    )
    all_pairs = jnp.ones((tag_len, memory_len), bool)
    zero_row = jnp.zeros((model_width,), jnp.float32)
    fw_self, fw_cross, fw_proj, fw_in, fb_in, fw_out, f_gains, f_biases = gathered
    gain_f = f_gains.astype(jnp.float32)
    bias_f = f_biases.astype(jnp.float32)
    tag_rows = tag_states.reshape(images * tag_len, model_width)
    mem_rows = image_memory.reshape(images * memory_len, model_width)
    self_bias = jnp.concatenate([bias_f[0], zero_row, bias_f[1]])
    qkv_rows = (
        (matmul(tag_rows, fw_self) + self_bias)
        .astype(jnp.bfloat16)
        .reshape(images, tag_len, 3 * model_width)
    )

    def self_one(pieces):
        proj_block, allowed = pieces
        return attend(
            proj_block[:, :model_width],
            proj_block[:, model_width : 2 * model_width],
            proj_block[:, 2 * model_width :],
            allowed,
        )

    self_mix, self_total = lax.map(self_one, (qkv_rows, allowed_self))
    self_mix = self_mix.reshape(images * tag_len, model_width).astype(jnp.bfloat16)
    resid_one = tag_rows.astype(jnp.float32) + matmul(self_mix, fw_proj[0]) + bias_f[2]
    normed_one = layer_norm(resid_one, gain_f[0], bias_f[6])
    normed_one_bf = normed_one.astype(jnp.bfloat16)
    cross_q = (
        (matmul(normed_one_bf, fw_cross[:, :model_width]) + bias_f[3])
        .astype(jnp.bfloat16)
        .reshape(images, tag_len, model_width)
    )
    cross_kv = (
        (matmul(mem_rows, fw_cross[:, model_width:]) + jnp.concatenate([zero_row, bias_f[4]]))
        .astype(jnp.bfloat16)
        .reshape(images, memory_len, 2 * model_width)
    )

    def cross_one(pieces):
        query_block, kv_block = pieces
        return attend(query_block, kv_block[:, :model_width], kv_block[:, model_width:], all_pairs)

    cross_mix, cross_total = lax.map(cross_one, (cross_q, cross_kv))
    cross_mix = cross_mix.reshape(images * tag_len, model_width).astype(jnp.bfloat16)
    resid_two = normed_one + matmul(cross_mix, fw_proj[1]) + bias_f[5]
    normed_two = layer_norm(resid_two, gain_f[1], bias_f[7])
    normed_two_bf = normed_two.astype(jnp.bfloat16)
    inner_pre = matmul(normed_two_bf, fw_in) + fb_in.astype(jnp.float32)
    activated = jax.nn.gelu(inner_pre).astype(jnp.bfloat16)
    resid_three = normed_two + matmul(activated, fw_out) + bias_f[9]
    layer_rows = layer_norm(resid_three, gain_f[2], bias_f[8]) * valid_rows
    weights_back = (
        lax.all_gather(w_self, ("wide", "narrow"), axis=0, tiled=True),
        lax.all_gather(w_cross, ("wide", "narrow"), axis=0, tiled=True),
        lax.all_gather(w_proj, ("wide", "narrow"), axis=1, tiled=True),
        lax.all_gather(w_in, ("wide", "narrow"), axis=0, tiled=True),
        lax.all_gather(b_in, ("wide", "narrow"), axis=0, tiled=True),
        lax.all_gather(w_out, ("wide", "narrow"), axis=0, tiled=True),
        lax.all_gather(ln_gains, ("wide", "narrow"), axis=1, tiled=True),
        lax.all_gather(biases, ("wide", "narrow"), axis=1, tiled=True),
    )
    bw_self, bw_cross, bw_proj, bw_in, bb_in, bw_out, b_gains, b_biases = weights_back
    gain_b = b_gains.astype(jnp.float32)
    bias_b = b_biases.astype(jnp.float32)
    grad_rows = out_grad.reshape(images * tag_len, model_width).astype(jnp.float32) * valid_rows
    _, pull_three = jax.vjp(layer_norm, resid_three, gain_b[2], bias_b[8])
    grad_r3, grad_g3, grad_n3 = pull_three(grad_rows)
    grad_f_bf = grad_r3.astype(jnp.bfloat16)
    grad_bout = jnp.sum(grad_f_bf.astype(jnp.float32), 0)
    grad_w_out = left_t(activated, grad_f_bf)
    grad_act = right_t(grad_f_bf, bw_out)
    _, gelu_pull = jax.vjp(jax.nn.gelu, inner_pre)
    grad_inner_bf = gelu_pull(grad_act)[0].astype(jnp.bfloat16)
    grad_b_in = jnp.sum(grad_inner_bf.astype(jnp.float32), 0)
    grad_w_in = left_t(normed_two_bf, grad_inner_bf)
    grad_n2 = grad_r3 + right_t(grad_inner_bf, bw_in)
    _, pull_two = jax.vjp(layer_norm, resid_two, gain_b[1], bias_b[7])
    grad_r2, grad_g2, grad_ln2 = pull_two(grad_n2)
    grad_c_bf = grad_r2.astype(jnp.bfloat16)
    grad_bo_c = jnp.sum(grad_c_bf.astype(jnp.float32), 0)
    grad_wo_c = left_t(cross_mix, grad_c_bf)
    grad_cm = (
        right_t(grad_c_bf, bw_proj[1]).astype(jnp.bfloat16).reshape(images, tag_len, model_width)
    )

    def cross_back(pieces):
        query_block, kv_block, log_total, grad_block = pieces
        return attend_back(
            query_block,
            kv_block[:, :model_width],
            kv_block[:, model_width:],
            all_pairs,
            log_total,
            grad_block,
        )

    grad_cq, grad_ck, grad_cv = lax.map(cross_back, (cross_q, cross_kv, cross_total, grad_cm))
    grad_cq_bf = grad_cq.reshape(images * tag_len, model_width).astype(jnp.bfloat16)
    grad_ckv_bf = (
        jnp.concatenate([grad_ck, grad_cv], -1)
        .reshape(images * memory_len, 2 * model_width)
        .astype(jnp.bfloat16)
    )
    grad_bq_c = jnp.sum(grad_cq_bf.astype(jnp.float32), 0)
    grad_bv_c = jnp.sum(grad_ckv_bf[:, model_width:].astype(jnp.float32), 0)
    grad_w_cross = jnp.concatenate(
        [left_t(normed_one_bf, grad_cq_bf), left_t(mem_rows, grad_ckv_bf)], 1
    )
    grad_memory = right_t(grad_ckv_bf, bw_cross[:, model_width:])
    grad_n1 = grad_r2 + right_t(grad_cq_bf, bw_cross[:, :model_width])
    _, pull_one = jax.vjp(layer_norm, resid_one, gain_b[0], bias_b[6])
    grad_r1, grad_g1, grad_ln1 = pull_one(grad_n1)
    grad_a_bf = grad_r1.astype(jnp.bfloat16)
    grad_bo_s = jnp.sum(grad_a_bf.astype(jnp.float32), 0)
    grad_wo_s = left_t(self_mix, grad_a_bf)
    grad_sm = (
        right_t(grad_a_bf, bw_proj[0]).astype(jnp.bfloat16).reshape(images, tag_len, model_width)
    )

    def self_back(pieces):
        proj_block, allowed, log_total, grad_block = pieces
        grads_qkv = attend_back(
            proj_block[:, :model_width],
            proj_block[:, model_width : 2 * model_width],
            proj_block[:, 2 * model_width :],
            allowed,
            log_total,
            grad_block,
        )
        return jnp.concatenate(grads_qkv, -1)

    grad_qkv_bf = (
        lax.map(self_back, (qkv_rows, allowed_self, self_total, grad_sm))
        .reshape(images * tag_len, 3 * model_width)
        .astype(jnp.bfloat16)
    )
    grad_bq_s = jnp.sum(grad_qkv_bf[:, :model_width].astype(jnp.float32), 0)
    grad_bv_s = jnp.sum(grad_qkv_bf[:, 2 * model_width :].astype(jnp.float32), 0)
    grad_w_self = left_t(tag_rows, grad_qkv_bf)
    grad_tags = grad_r1 + right_t(grad_qkv_bf, bw_self)
    grad_w_proj = jnp.stack([grad_wo_s, grad_wo_c])
    grad_gains = jnp.stack([grad_g1, grad_g2, grad_g3])
    grad_biases = jnp.stack(
        [
            grad_bq_s,
            grad_bv_s,
            grad_bo_s,
            grad_bq_c,
            grad_bv_c,
            grad_bo_c,
            grad_ln1,
            grad_ln2,
            grad_n3,
            grad_bout,
        ]
    )
    every_share = (
        lax.psum_scatter(grad_w_self, ("wide", "narrow"), scatter_dimension=0, tiled=True),
        lax.psum_scatter(grad_w_cross, ("wide", "narrow"), scatter_dimension=0, tiled=True),
        lax.psum_scatter(grad_w_proj, ("wide", "narrow"), scatter_dimension=1, tiled=True),
        lax.psum_scatter(grad_w_in, ("wide", "narrow"), scatter_dimension=0, tiled=True),
        lax.psum_scatter(grad_b_in, ("wide", "narrow"), scatter_dimension=0, tiled=True),
        lax.psum_scatter(grad_w_out, ("wide", "narrow"), scatter_dimension=0, tiled=True),
        lax.psum_scatter(grad_gains, ("wide", "narrow"), scatter_dimension=1, tiled=True),
        lax.psum_scatter(grad_biases, ("wide", "narrow"), scatter_dimension=1, tiled=True),
    )
    (
        share_self,
        share_cross,
        share_proj,
        share_w_in,
        share_b_in,
        share_w_out,
        share_gains,
        share_biases,
    ) = every_share
    layer_out = layer_rows.astype(jnp.bfloat16).reshape(images, tag_len, model_width)
    return (
        layer_out,
        grad_tags.reshape(images, tag_len, model_width),
        grad_memory.reshape(images, memory_len, model_width),
        share_self,
        share_cross,
        share_proj,
        share_w_in,
        share_b_in,
        share_w_out,
        share_gains,
        share_biases,
    )


def solution(mesh):
    placed = (
        P(("wide", "narrow"), None, None),
        P(("wide", "narrow"), None, None),
        P(("wide", "narrow")),
        P(("wide", "narrow"), None),
        P(("wide", "narrow"), None),
        P(None, ("wide", "narrow"), None),
        P(("wide", "narrow"), None),
        P(("wide", "narrow")),
        P(("wide", "narrow"), None),
        P(None, ("wide", "narrow")),
        P(None, ("wide", "narrow")),
        P(("wide", "narrow"), None, None),
    )
    return jax.shard_map(
        per_device,
        mesh=mesh,
        in_specs=placed,
        out_specs=(
            P(("wide", "narrow"), None, None),
            P(("wide", "narrow"), None, None),
            P(("wide", "narrow"), None, None),
            P(("wide", "narrow"), None),
            P(("wide", "narrow"), None),
            P(None, ("wide", "narrow"), None),
            P(("wide", "narrow"), None),
            P(("wide", "narrow")),
            P(("wide", "narrow"), None),
            P(None, ("wide", "narrow")),
            P(None, ("wide", "narrow")),
        ),
        check_vma=False,
    )
```

profile of v0, /device:TPU:0, one launch (start us, length us, event | category | flops | bytes accessed | tf_op | source)
XLA Modules:
  0.0 1364.9 jit_solution(14104537942483306924)
XLA Ops:
  11.6 42.1 %all-reduce.1 = bf16[1024]{0:T(1024)(128)(2,1)S(1)} all-reduce(bf16[1024]{0:T(1024)(128)(2,1)S(1)} %dynamic-update-slice), channel_id=1, replica_groups=mesh['wide'=8,'narrow'=4] {'wide','narrow'}, use_global_device_ids=true, to_apply=%add.1 | all-reduce | flops 1024 | bytes 4096
  58.8 40.5 %all-gather = bf16[32,16,3]{1,2,0:T(4,128)(2,1)S(1)} all-gather(bf16[1,16,3]{1,2,0:T(4,128)(2,1)} %bitcast.389), channel_id=1, replica_groups=mesh['wide'=8,'narrow'=4] {'wide','narrow'}, dimensions={0}, use_global_device_ids=true | all-gather | bytes 3168 | tf_op jit(solution)/shard_map/all_gather | solution.py:119
  100.1 37.1 %all_gather.31 = bf16[10,512]{0,1:T(8,128)(2,1)S(1)} all-gather(bf16[10,16]{0,1:T(8,128)(2,1)S(1)} %copy.111), channel_id=1, replica_groups=mesh['wide'=8,'narrow'=4] {'wide','narrow'}, dimensions={1}, use_global_device_ids=true | all-gather | bytes 10560 | tf_op jit(solution)/shard_map/all_gather | solution.py:120
  141.3 6.7 add_convert_fusion.1
  147.9 6.9 copy.112
  156.2 28.3 %while.48 = (s32[]{:T(128)}, bf16[3,512,512]{2,1,0:T(8,128)(2,1)}, f32[3,8,512,1]{2,1,3,0:T(8,128)S(1)}, bf16[3,512,1536]{1,2,0:T(8,128)(2,1)}, pred[3,512,512]{1,2,0:T(8,128)(4,1)}, /*index=5*/s32[]{:T(128)}) while((s32[]{:T(128)}, bf16[3,512,512]{2,1,0:T(8,128)(2,1)}, f32[3,8,512,1]{2,1,3,0:T(8,128)S(1)}, bf16[3,512,1536]{1,2,0:T(8,128)(2,1)}, ...), condition=%wide.region_3.4_spmd, body=%wide.region_0.3_spmd.sunk | while | flops 562032640 | bytes 37093468 | solution.py:155
  203.0 7.6 copy.116
  211.9 33.4 %while.49 = (s32[]{:T(128)}, bf16[3,512,512]{2,1,0:T(8,128)(2,1)}, f32[3,8,512,1]{2,1,3,0:T(8,128)S(1)}, bf16[3,784,1024]{1,2,0:T(8,128)(2,1)}, bf16[3,512,512]{1,2,0:T(8,128)(2,1)}, /*index=5*/s32[]{:T(128)}) while((s32[]{:T(128)}, bf16[3,512,512]{2,1,0:T(8,128)(2,1)}, f32[3,8,512,1]{2,1,3,0:T(8,128)S(1)}, bf16[3,784,1024]{1,2,0:T(8,128)(2,1)}, ...), condition=%wide.region_9.10_spmd, body=%wide.region_6.9_spmd.sunk | while | flops 850980864 | bytes 50888796 | solution.py:175
  251.7 7.7 multiply_convert_fusion.2
  259.4 32.3 %all-gather.15.cloned.1.call-done = bf16[1024,512]{1,0:T(8,128)(2,1)} async-done(((bf16[32,512]{1,0:T(8,128)(2,1)}), bf16[1024,512]{1,0:T(8,128)(2,1)}) %all-gather.15.cloned.1.call-update) | async-done | bytes 1048592 | tf_op jit(solution)/shard_map/all_gather | solution.py:118
  305.2 6.4 convert_reduce_fusion
  322.4 140.1 %while.50 = (s32[]{:T(128)}, bf16[3,512,512]{2,1,0:T(8,128)(2,1)}, bf16[3,784,512]{2,1,0:T(8,128)(2,1)}, bf16[3,784,512]{2,1,0:T(8,128)(2,1)}, bf16[3,784,1024]{...) while((s32[]{:T(128)}, bf16[3,512,512]{2,1,0:T(8,128)(2,1)}, ...), condition=%wide.region_20.21_spmd, body=%wide.region_18.20_spmd.sunk | while | flops 2082222080 | bytes 221675856 | solution.py:229
  340.1 11.9 multiply_reduce_fusion.17
  352.1 6.9 multiply_convert_fusion.6
  386.6 11.9 multiply_reduce_fusion.17
  398.6 6.9 multiply_convert_fusion.6
  433.2 11.9 multiply_reduce_fusion.17
  445.2 6.9 multiply_convert_fusion.6
  481.1 105.1 %while.51 = (s32[]{:T(128)}, bf16[3,512,1536]{2,1,0:T(8,128)(2,1)}, bf16[3,512,1536]{1,2,0:T(8,128)(2,1)}, pred[3,512,512]{1,2,0:T(8,128)(4,1)}, f32[3,8,512,1]{...) while((s32[]{:T(128)}, bf16[3,512,1536]{2,1,0:T(8,128)(2,1)}, bf16[3,512,1536]{1,2,0:T(8,128)(2,1)}, ...), condition=%wide.region_25.26_spmd, body=%wide.region_23.25_spmd.sunk | while | flops 1368911872 | bytes 129843472 | solution.py:265
  498.3 8.1 multiply_convert_fusion.7
  533.3 8.1 multiply_convert_fusion.7
  568.3 8.1 multiply_convert_fusion.7
  590.0 6.2 fusion.36
  621.1 7.2 convolution_bitcast_fusion
  632.5 39.6 %all-reduce.2 = f32[1024]{0:T(1024)S(1)} all-reduce(f32[1024]{0:T(1024)S(1)} %copy-done.59), channel_id=6, replica_groups=mesh['wide'=8,'narrow'=4] {'wide','narrow'}, use_global_device_ids=true, to_apply=%region_31.32.clone | all-reduce | flops 1024 | bytes 8192
  672.7 7.8 fusion.27
  686.2 53.6 %reduce-scatter.28.cloned.1.call-done = f32[16,10]{1,0:T(8,128)} async-done(((f32[512,10]{1,0:T(8,128)}), f32[16,10]{1,0:T(8,128)}) %reduce-scatter.28.cloned.1.call-update) | async-done | bytes 656
  741.1 134.2 %reduce-scatter.18.cloned.1.call-done = f32[16,1024]{1,0:T(8,128)} async-done(((f32[512,1024]{1,0:T(8,128)}), f32[16,1024]{1,0:T(8,128)}) %reduce-scatter.18.cloned.1.call-update) | async-done | bytes 65552 | tf_op jit(solution)/shard_map/reduce_scatter | solution.py:293
  875.4 135.5 %reduce-scatter.20.cloned.1.call-done = f32[32,512]{1,0:T(8,128)} async-done(((f32[1024,512]{1,0:T(8,128)}), f32[32,512]{1,0:T(8,128)}) %reduce-scatter.20.cloned.1.call-update) | async-done | bytes 65552 | tf_op jit(solution)/shard_map/reduce_scatter | solution.py:295
  1010.9 135.3 %reduce-scatter.16.cloned.1.call-done = f32[2,16,512]{2,1,0:T(8,128)} async-done(((f32[2,512,512]{2,1,0:T(8,128)}), f32[2,16,512]{2,1,0:T(8,128)}) %reduce-scatter.16.cloned.1.call-update) | async-done | bytes 65552 | tf_op jit(solution)/shard_map/reduce_scatter | solution.py:292
  1146.2 104.3 %reduce-scatter.24.cloned.1.call-done = f32[16,1536]{1,0:T(8,128)} async-done(((f32[512,1536]{1,0:T(8,128)}), f32[16,1536]{1,0:T(8,128)}) %reduce-scatter.24.cloned.1.call-update) | async-done | bytes 98320
  1250.5 107.3 %reduce-scatter.22.cloned.1.call-done = f32[16,1536]{1,0:T(8,128)} async-done(((f32[512,1536]{1,0:T(8,128)}), f32[16,1536]{1,0:T(8,128)}) %reduce-scatter.22.cloned.1.call-update) | async-done | bytes 98320
  (474 shorter events, 348.6 us)
Async XLA Ops:
  7.2 190.3 %copy-start = (bf16[3,784,512]{2,1,0:T(8,128)(2,1)S(1)}, bf16[3,784,512]{2,1,0:T(8,128)(2,1)}, u32[]{:S(2)}) copy-start(bf16[3,784,512]{2,1,0:T(8,128)(2,1)} %param.21) | copy-start | bytes 7225348
  7.2 132.0 %copy-start.63 = (s32[3]{0:T(128)S(1)}, s32[3]{0:T(128)}, u32[]{:S(2)}) copy-start(s32[3]{0:T(128)} %param.22) | copy-start | bytes 40
  7.2 134.0 %all-gather.7.cloned.1.call-start = ((), (), s32[]{:S(2)}) async-start(), calls=%async_computation.7 | async-start | bytes 1622016 | tf_op jit(solution)/shard_map/all_gather | solution.py:113
  7.9 176.6 %all-gather.9.cloned.1.call-start = ((), (), s32[]{:S(2)}) async-start(), calls=%async_computation.8 | async-start | bytes 1081344 | tf_op jit(solution)/shard_map/all_gather | solution.py:115
  8.7 182.5 %all-gather.11.cloned.1.call-start = ((), (), s32[]{:S(2)}) async-start(), calls=%async_computation.9 | async-start | bytes 1622016 | tf_op jit(solution)/shard_map/all_gather | solution.py:114
  9.4 242.2 %all-gather.13.cloned.1.call-start = ((), (), s32[]{:S(2)}) async-start(), calls=%async_computation.10 | async-start | bytes 1081344 | tf_op jit(solution)/shard_map/all_gather | solution.py:116
  10.0 281.6 %all-gather.15.cloned.1.call-start = ((), (), s32[]{:S(2)}) async-start(), calls=%async_computation.11 | async-start | bytes 1081344 | tf_op jit(solution)/shard_map/all_gather | solution.py:118
  10.6 674.2 %reduce-scatter.26.cloned.1.call-start = ((), (), s32[]{:S(2)}) async-start(), calls=%async_computation.17 | async-start | bytes 270336
  187.8 57.5 %copy-start.34 = (f32[1536]{0:T(1024)}, f32[1536]{0:T(1024)S(1)}, u32[]{:S(2)}) copy-start(f32[1536]{0:T(1024)S(1)} %broadcast_multiply_fusion.2) | copy-start | bytes 18436
  189.4 55.9 %copy-start.36 = (f32[1536]{0:T(1024)}, f32[1536]{0:T(1024)S(1)}, u32[]{:S(2)}) copy-start(f32[1536]{0:T(1024)S(1)} %fusion.33) | copy-start | bytes 18436
  249.4 65.9 %copy-start.29 = (f32[1536]{0:T(1024)}, f32[1536]{0:T(1024)S(1)}, u32[]{:S(2)}) copy-start(f32[1536]{0:T(1024)S(1)} %broadcast_multiply_fusion.1) | copy-start | bytes 18436
  251.6 63.7 %copy-start.32 = (f32[1536]{0:T(1024)}, f32[1536]{0:T(1024)S(1)}, u32[]{:S(2)}) copy-start(f32[1536]{0:T(1024)S(1)} %fusion.34) | copy-start | bytes 18436
  251.7 40.0 %copy-start.61 = (f32[512]{0:T(512)S(1)}, f32[512]{0:T(512)}, u32[]{:S(2)}) copy-start(f32[512]{0:T(512)} %get-tuple-element.337) | copy-start | bytes 6148
  337.9 14.1 %slice-start = ((s8[12845056]{0:T(1024)(128)(4,1)}), s8[262144]{0:T(1024)(128)(4,1)S(1)}, s32[]{:S(2)}) async-start(s8[12845056]{0:T(1024)(128)(4,1)} %bitcast.312), calls=%async_computation.19 | async-start | bytes 524288 | tf_op jit(solution)/shard_map/while
  340.1 11.9 slice-start.1
  340.1 11.9 slice-start.2
  340.1 11.9 slice-start.3
  384.4 14.1 %slice-start = ((s8[12845056]{0:T(1024)(128)(4,1)}), s8[262144]{0:T(1024)(128)(4,1)S(1)}, s32[]{:S(2)}) async-start(s8[12845056]{0:T(1024)(128)(4,1)} %bitcast.312), calls=%async_computation.19 | async-start | bytes 524288 | tf_op jit(solution)/shard_map/while
  386.6 11.9 slice-start.1
  386.6 11.9 slice-start.2
  386.6 11.9 slice-start.3
  431.0 14.1 %slice-start = ((s8[12845056]{0:T(1024)(128)(4,1)}), s8[262144]{0:T(1024)(128)(4,1)S(1)}, s32[]{:S(2)}) async-start(s8[12845056]{0:T(1024)(128)(4,1)} %bitcast.312), calls=%async_computation.19 | async-start | bytes 524288 | tf_op jit(solution)/shard_map/while
  433.2 11.9 slice-start.1
  433.2 11.9 slice-start.2
  433.2 11.9 slice-start.3
  475.4 264.4 %reduce-scatter.28.cloned.1.call-start = ((), (), s32[]{:S(2)}) async-start(), calls=%async_computation.18 | async-start | bytes 270336
  590.0 285.4 %reduce-scatter.18.cloned.1.call-start = ((), (), s32[]{:S(2)}) async-start(), calls=%async_computation.13 | async-start | bytes 2162688 | tf_op jit(solution)/shard_map/reduce_scatter | solution.py:293
  596.3 414.6 %reduce-scatter.20.cloned.1.call-start = ((), (), s32[]{:S(2)}) async-start(), calls=%async_computation.14 | async-start | bytes 2162688 | tf_op jit(solution)/shard_map/reduce_scatter | solution.py:295
  602.0 544.2 %reduce-scatter.16.cloned.1.call-start = ((), (), s32[]{:S(2)}) async-start(), calls=%async_computation.12 | async-start | bytes 2162688 | tf_op jit(solution)/shard_map/reduce_scatter | solution.py:292
  607.7 642.8 %reduce-scatter.24.cloned.1.call-start = ((), (), s32[]{:S(2)}) async-start(), calls=%async_computation.16 | async-start | bytes 3244032
  621.1 736.7 %reduce-scatter.22.cloned.1.call-start = ((), (), s32[]{:S(2)}) async-start(), calls=%async_computation.15 | async-start | bytes 3244032
  631.8 48.6 %slice-start.4 = ((s8[4718592]{0:T(1024)(128)(4,1)}), s8[524288]{0:T(1024)(128)(4,1)S(1)}, s32[]{:S(2)}) async-start(s8[4718592]{0:T(1024)(128)(4,1)} %bitcast.354), calls=%async_computation.23 | async-start | bytes 1048576
  (89 other events, 291.9 us)
Sparse Core Ops, SparseCore 0:
  10.9 57.6 all-gather.6
  71.5 52.4 all-gather.8
  126.9 53.9 all-gather.10
  183.7 52.5 all-gather.12
  239.0 52.6 all-gather.14
  475.5 132.3 reduce-scatter.25
  610.3 129.4 reduce-scatter.27
  742.6 132.7 reduce-scatter.17
  878.3 132.5 reduce-scatter.19
  1013.6 132.5 reduce-scatter.15
  1153.1 97.3 reduce-scatter.23
  1257.3 100.4 reduce-scatter.21
where the time goes:
time: 1370 us; the launch traced here: 1360 us
  waiting for transfers between devices  706 us (52%)
  matrix products  230 us (17%)
  local copies, waits for them, and re-layouts  160 us (12%)
  blocking collectives  159 us (12%)
  other arithmetic  92.4 us (7%)
  between operations  15.3 us (1%)
    unnamed x16, waiting for transfers between devices  268 us
    reduce_scatter x1, waiting for transfers between devices, per_device(): lax.psum_scatter(grad_w_out, ('wide', 'narrow'), scatter_dimension=0, til...  136 us
    reduce_scatter x1, waiting for transfers between devices, per_device(): lax.psum_scatter(grad_w_proj, ('wide', 'narrow'), scatter_dimension=1, ti...  135 us
    reduce_scatter x1, waiting for transfers between devices, per_device(): lax.psum_scatter(grad_w_in, ('wide', 'narrow'), scatter_dimension=0, tile...  134 us
    unnamed x2, blocking collectives  81.7 us
    dot_general x6, matrix products, attend_back(): jnp.einsum('qhd,khd->hqk', grad_heads, split_heads(value_rows), preferred...  49.4 us
    convert_element_type x6, other arithmetic, attend_back(): grad_scores = (softmax_w * (grad_probs - inner_sum)).astype(jnp.bfloat16)  45.1 us
    all_gather x1, blocking collectives, per_device(): lax.all_gather(ln_gains, ('wide', 'narrow'), axis=1, tiled=True)  40.5 us
  transfers between devices with their start and end apart: 12, of which 7 were waited for; matrix products, arithmetic and copies ran while one was open for 21% of the time, Pallas kernels for 0%

commit v1 on v0

v1 whole, which is shorter than its diff:
```python
import functools

import jax
import jax.numpy as jnp
from jax import lax
from jax.experimental import pallas as pl
from jax.experimental.pallas import tpu as pltpu
from jax.sharding import PartitionSpec as P


MESH = pl.DeviceIdType.MESH
f32, bf16 = jnp.float32, jnp.bfloat16


def grid_of(mesh_wide, mesh_narrow):
    outer = 4
    return outer, mesh_wide // outer, mesh_narrow // 2


def place(dims):
    outer, inner, across = dims
    wide, narrow = lax.axis_index("wide"), lax.axis_index("narrow")
    return wide // inner, lax.rem(wide, inner), narrow // 2, lax.rem(narrow, 2)


def device(dims, a, b, x, c):
    return {"wide": a * dims[1] + b, "narrow": x * 2 + c}


def greet(dims, me):
    a, b, x, c = me
    outer, inner, across = dims
    barrier = pltpu.get_barrier_semaphore()
    peers = [(lax.rem(a + k, outer), b, x, c) for k in range(1, outer)]
    peers += [(a, lax.rem(b + k, inner), x, c) for k in range(1, inner)]
    peers += [(a, b, lax.rem(x + k, across), c) for k in range(1, across)]
    peers += [(a, b, x, 1 - c)]
    for peer in peers:
        pl.semaphore_signal(barrier, inc=1, device_id=device(dims, *peer), device_id_type=MESH)
    pl.semaphore_wait(barrier, len(peers))


ALL = slice(None)


def gather_kernel(dims, leads, *refs):
    count = len(leads)
    shards, outs = refs[:count], refs[count : 2 * count]
    local_sem, send_sem, recv_sem = refs[2 * count :]
    outer, inner, across = dims
    me = place(dims)
    a, b, x, c = me
    greet(dims, me)

    def cell(ref, lead, *index):
        return ref.at[(ALL,) * lead + index]

    def remote(g, slot, src, dst, peer):
        return pltpu.make_async_remote_copy(
            src_ref=src, dst_ref=dst, send_sem=send_sem.at[g, slot], recv_sem=recv_sem.at[g, slot],
            device_id=device(dims, *peer), device_id_type=MESH)

    n_in, n_ac = inner - 1, across - 1

    def first(g):
        lead = leads[g]
        mine = cell(outs[g], lead, a, b, x, c)
        return [remote(g, k - 1, shards[g], mine, (lax.rem(a + k, outer), b, x, c)) for k in range(1, outer)]

    def keep(g):
        return pltpu.make_async_copy(shards[g], cell(outs[g], leads[g], a, b, x, c), local_sem.at[g])

    base = outer - 1

    def via_inner(g, core):
        lead = leads[g]
        column = ALL if core == 0 else x
        piece = cell(outs[g], lead, ALL, b, column, c)
        return [remote(g, base + k - 1, piece, piece, (a, lax.rem(b + k, inner), x, c)) for k in range(1, inner)]

    def via_across(g, core):
        lead = leads[g]
        row = b if core == 0 else ALL
        piece = cell(outs[g], lead, ALL, row, x, c)
        return [remote(g, base + n_in + k - 1, piece, piece, (a, b, lax.rem(x + k, across), c)) for k in range(1, across)]

    share = base + n_in + n_ac

    def to_partner(g, core, holder):
        lead = leads[g]
        def piece(slot, row, column):
            ref = cell(outs[g], lead, ALL, row, column, holder)
            return remote(g, share + slot, ref, ref, (a, b, x, 1 - c))
        own = [piece(0, b, x)]
        by_inner = [piece(1 + k - 1, lax.rem(b + k, inner), ALL if core == 0 else x) for k in range(1, inner)]
        by_across = [piece(1 + n_in + k - 1, b if core == 0 else ALL, lax.rem(x + k, across)) for k in range(1, across)]
        return (own, by_across, by_inner) if core == 0 else (own, by_inner, by_across)

    def start(copies):
        for copy in copies:
            copy.start()

    def arrived(copies):
        for copy in copies:
            copy.wait_recv()

    for g in range(count):
        keep(g).start()
        start(first(g))

    def body(core):
        second, third = (via_across, via_inner) if core == 0 else (via_inner, via_across)
        for step in range(count + 2):
            g = step
            if g < count:
                keep(g).wait()
                arrived(first(g))
                start(second(g, core))
                start(to_partner(g, core, c)[0])
            g = step - 1
            if 0 <= g < count:
                arrived(second(g, core))
                start(third(g, core))
                start(to_partner(g, core, c)[1])
            g = step - 2
            if 0 <= g < count:
                arrived(third(g, core))
                start(to_partner(g, core, c)[2])
        for g in range(count):
            for group in to_partner(g, 1 - core, 1 - c):
                arrived(group)
        for g in range(count):
            for copy in first(g) + second(g, core) + third(g, core):
                copy.wait_send()
            for group in to_partner(g, core, c):
                for copy in group:
                    copy.wait_send()

    @pl.when(c == 0)
    def _():
        body(0)

    @pl.when(c == 1)
    def _():
        body(1)


def gather(dims, shards, leads):
    outer, inner, across = dims
    def shape(s, lead):
        return jax.ShapeDtypeStruct(s.shape[:lead] + (outer, inner, across, 2) + s.shape[lead:], s.dtype)
    slots = (outer - 1) + 2 * (inner - 1) + 2 * (across - 1) + 1
    n = len(shards)
    return pl.pallas_call(
        functools.partial(gather_kernel, dims, leads),
        out_shape=[shape(s, l) for s, l in zip(shards, leads)],
        in_specs=[pl.BlockSpec(memory_space=pl.ANY)] * n,
        out_specs=[pl.BlockSpec(memory_space=pl.ANY)] * n,
        scratch_shapes=[pltpu.SemaphoreType.DMA((n,)), pltpu.SemaphoreType.DMA((n, slots)), pltpu.SemaphoreType.DMA((n, slots))],
        compiler_params=pltpu.CompilerParams(collective_id=0, has_side_effects=True),
        name="gather_weights",
    )(*shards)


def scatter_kernel(dims, leads, *refs):
    count = len(leads)
    grads, outs = refs[:count], refs[count : 2 * count]
    rest = refs[2 * count :]
    r0, r1i, r1a, r2a, r2i, r3 = (rest[k * count : (k + 1) * count] for k in range(6))
    send_sem, recv_sem = rest[6 * count :]
    outer, inner, across = dims
    me = place(dims)
    a, b, x, c = me
    greet(dims, me)
    n_in, n_ac = inner - 1, across - 1

    def cell(ref, lead, *index):
        return ref.at[(ALL,) * lead + index]

    def remote(g, slot, src, dst, peer):
        return pltpu.make_async_remote_copy(
            src_ref=src, dst_ref=dst, send_sem=send_sem.at[g, slot], recv_sem=recv_sem.at[g, slot],
            device_id=device(dims, *peer), device_id_type=MESH)

    def swap(g):
        return [remote(g, 0, cell(grads[g], leads[g], ALL, ALL, ALL, 1 - c), r0[g], (a, b, x, 1 - c))]

    def via_inner(g, core):
        lead = leads[g]
        res = []
        for k in range(1, inner):
            peer = lax.rem(b + k, inner)
            if core == 0:
                src, dst = cell(r0[g], lead, ALL, peer), r1i[g].at[k - 1]
            else:
                src, dst = cell(r1a[g].at[0], lead, ALL, peer), r2i[g].at[k - 1]
            res.append(remote(g, k, src, dst, (a, peer, x, c)))
        return res

    def via_across(g, core):
        lead = leads[g]
        res = []
        for k in range(1, across):
            peer = lax.rem(x + k, across)
            if core == 1:
                src, dst = cell(r0[g], lead, ALL, ALL, peer), r1a[g].at[k - 1]
            else:
                src, dst = cell(r1i[g].at[0], lead, ALL, peer), r2a[g].at[k - 1]
            res.append(remote(g, 1 + n_in + k - 1, src, dst, (a, b, peer, c)))
        return res

    def last(g, core):
        lead = leads[g]
        held = (r2a if core == 0 else r2i)[g].at[0]
        res = []
        for k in range(1, outer):
            peer = lax.rem(a + k, outer)
            res.append(remote(g, 1 + n_in + n_ac + k - 1, cell(held, lead, peer), r3[g].at[k - 1], (peer, b, x, c)))
        return res

    def start(copies):
        for copy in copies:
            copy.start()

    def arrived(copies):
        for copy in copies:
            copy.wait_recv()

    def up(v):
        return v.astype(f32)

    for g in range(count):
        start(swap(g))

    def body(core):
        second, third = (via_inner, via_across) if core == 0 else (via_across, via_inner)
        def at(lead, *index):
            return (ALL,) * lead + index
        for step in range(count + 3):
            g = step
            if g < count:
                arrived(swap(g))
                lead = leads[g]
                r0[g][...] = (up(grads[g][at(lead, ALL, ALL, ALL, c)]) + up(r0[g][...])).astype(bf16)
                start(second(g, core))
            g = step - 1
            if 0 <= g < count:
                arrived(second(g, core))
                lead = leads[g]
                if core == 0:
                    total = up(r0[g][at(lead, ALL, b)])
                    held = r1i[g]
                else:
                    total = up(r0[g][at(lead, ALL, ALL, x)])
                    held = r1a[g]
                for k in range(held.shape[0]):
                    total = total + up(held[k])
                held[0] = total.astype(bf16)
                start(third(g, core))
            g = step - 2
            if 0 <= g < count:
                arrived(third(g, core))
                lead = leads[g]
                if core == 0:
                    total = up(r1i[g][(0,) + at(lead, ALL, x)])
                    held = r2a[g]
                else:
                    total = up(r1a[g][(0,) + at(lead, ALL, b)])
                    held = r2i[g]
                for k in range(held.shape[0]):
                    total = total + up(held[k])
                held[0] = total.astype(bf16)
                start(last(g, core))
            g = step - 3
            if 0 <= g < count:
                arrived(last(g, core))
                lead = leads[g]
                held = (r2a if core == 0 else r2i)[g]
                total = up(held[(0,) + at(lead, a)])
                for k in range(outer - 1):
                    total = total + up(r3[g][k])
                outs[g][...] = total
        for g in range(count):
            for copy in swap(g) + second(g, core) + third(g, core) + last(g, core):
                copy.wait_send()

    @pl.when(c == 0)
    def _():
        body(0)

    @pl.when(c == 1)
    def _():
        body(1)


def scatter(dims, grads, leads):
    outer, inner, across = dims
    n = len(grads)
    outs, shapes = [], [[] for _ in range(6)]
    for g, lead in zip(grads, leads):
        head, tail = g.shape[:lead], g.shape[lead + 4 :]
        outs.append(jax.ShapeDtypeStruct(head + tail, f32))
        shapes[0].append(head + (outer, inner, across) + tail)
        shapes[1].append((inner - 1,) + head + (outer, across) + tail)
        shapes[2].append((across - 1,) + head + (outer, inner) + tail)
        shapes[3].append((across - 1,) + head + (outer,) + tail)
        shapes[4].append((inner - 1,) + head + (outer,) + tail)
        shapes[5].append((outer - 1,) + head + tail)
    slots = 1 + (inner - 1) + (across - 1) + (outer - 1)
    return pl.pallas_call(
        functools.partial(scatter_kernel, dims, leads),
        out_shape=outs,
        in_specs=[pl.BlockSpec(memory_space=pltpu.VMEM)] * n,
        out_specs=[pl.BlockSpec(memory_space=pltpu.VMEM)] * n,
        scratch_shapes=[pltpu.VMEM(s, bf16) for group in shapes for s in group]
        + [pltpu.SemaphoreType.DMA((n, slots)), pltpu.SemaphoreType.DMA((n, slots))],
        compiler_params=pltpu.CompilerParams(collective_id=1, has_side_effects=True, vmem_limit_bytes=48 * 2**20),
        name="scatter_grads",
    )(*grads)

HEADS, HEAD_DIM = 8, 64
EPS = 1e-5
MASKED = -1e9
MIB = 2**20


def dot(left, right, left_dim, right_dim):
    return lax.dot_general(left, right, (((left_dim,), (right_dim,)), ((), ())), preferred_element_type=f32)


def full(shape):
    return pl.BlockSpec(shape, lambda i: (0,) * len(shape))


def image(shape):
    return pl.BlockSpec((1,) + shape, lambda i: (i,) + (0,) * len(shape))


def with_ones(rows):
    return jnp.concatenate([rows, jnp.ones((16, rows.shape[1]), bf16)], 0)


def with_delta(rows, delta):
    high = delta.astype(bf16).astype(f32)
    low = delta - high
    at = lax.broadcasted_iota(jnp.int32, (16, rows.shape[1]), 0)
    extra = jnp.where(at == 0, -high, jnp.where(at == 1, -low, 0.0))
    return jnp.concatenate([rows, extra.astype(bf16)], 0)


def self_forward(lens, x_ref, mem_ref, w_self, w_cross, bias_qkv, bias_kv,
                 qkv_ref, ckv_ref, near_ref, far_ref, inv_ref, mix_ref, wt_self, wt_cross):
    width = x_ref.shape[2]
    tags = x_ref.shape[1]
    half = tags // 2
    i = pl.program_id(0)

    @pl.when(i == 0)
    def _():
        wt_self[...] = w_self[...].T
        wt_cross[...] = w_cross[...].T

    ckv = dot(wt_cross[width:], mem_ref[0], 1, 1) + bias_kv[...]
    ckv_ref[0] = ckv.astype(bf16).reshape(ckv_ref.shape[1:])
    qkv = dot(wt_self[...], x_ref[0], 1, 1) + bias_qkv[...]
    q = qkv[:width].astype(bf16) * bf16(HEAD_DIM ** -0.5)
    qkv_ref[0, :HEADS] = q.reshape(HEADS, HEAD_DIM, tags)
    qkv_ref[0, HEADS:] = qkv[width:].astype(bf16).reshape(2 * HEADS, HEAD_DIM, tags)
    last = lens[i] - 1

    def head(h, _):
        qt, kt, vt = qkv_ref[0, h], qkv_ref[0, HEADS + h], with_ones(qkv_ref[0, 2 * HEADS + h])

        def part(keys, first, out):
            s = dot(kt[:, :keys], qt[:, first : first + half], 0, 0)
            key_at = lax.broadcasted_iota(jnp.int32, (keys, half), 0)
            query_at = lax.broadcasted_iota(jnp.int32, (1, half), 1) + first
            s = jnp.where(key_at <= jnp.minimum(query_at, last), s, MASKED)
            e = jnp.exp(s - jnp.max(s, 0, keepdims=True)).astype(bf16)
            out[0, h] = e
            mixed = dot(vt[:, :keys], e, 1, 0)
            inv = 1.0 / mixed[HEAD_DIM : HEAD_DIM + 1]
            inv_ref[0, pl.ds(h, 1), first : first + half] = inv
            mix_ref[0, h, :, first : first + half] = (mixed[:HEAD_DIM] * inv).astype(bf16)

        part(half, 0, near_ref)
        part(tags, half, far_ref)
        return 0

    lax.fori_loop(0, HEADS, head, 0)


def run_self_forward(lens, x, mem, w_self, w_cross, bias_qkv, bias_kv):
    images, tags, width = x.shape
    cells = mem.shape[1]
    half = tags // 2
    sds = jax.ShapeDtypeStruct
    return pl.pallas_call(
        self_forward,
        grid_spec=pltpu.PrefetchScalarGridSpec(
            num_scalar_prefetch=1,
            grid=(images,),
            in_specs=[pl.BlockSpec((1, tags, width), lambda i, n: (i, 0, 0)), pl.BlockSpec((1, cells, width), lambda i, n: (i, 0, 0))]
            + [pl.BlockSpec(v.shape, lambda i, n: (0, 0)) for v in (w_self, w_cross, bias_qkv, bias_kv)],
            out_specs=[
                pl.BlockSpec((1, 3 * HEADS, HEAD_DIM, tags), lambda i, n: (i, 0, 0, 0)),
                pl.BlockSpec((1, 2 * HEADS, HEAD_DIM, cells), lambda i, n: (i, 0, 0, 0)),
                pl.BlockSpec((1, HEADS, half, half), lambda i, n: (i, 0, 0, 0)),
                pl.BlockSpec((1, HEADS, tags, half), lambda i, n: (i, 0, 0, 0)),
                pl.BlockSpec((1, HEADS, tags), lambda i, n: (i, 0, 0)),
                pl.BlockSpec((1, HEADS, HEAD_DIM, tags), lambda i, n: (i, 0, 0, 0)),
                pl.BlockSpec((3 * width, width), lambda i, n: (0, 0)),
                pl.BlockSpec((3 * width, width), lambda i, n: (0, 0)),
            ],
        ),
        out_shape=[
            sds((images, 3 * HEADS, HEAD_DIM, tags), bf16),
            sds((images, 2 * HEADS, HEAD_DIM, cells), bf16),
            sds((images, HEADS, half, half), bf16),
            sds((images, HEADS, tags, half), bf16),
            sds((images, HEADS, tags), f32),
            sds((images, HEADS, HEAD_DIM, tags), bf16),
            sds((3 * width, width), bf16),
            sds((3 * width, width), bf16),
        ],
        compiler_params=pltpu.CompilerParams(vmem_limit_bytes=58 * MIB),
        name="self_forward",
    )(lens, x, mem, w_self, w_cross, bias_qkv, bias_kv)


def norm(resid):
    centred = resid - jnp.mean(resid, -1, keepdims=True)
    scale = lax.rsqrt(jnp.mean(centred * centred, -1, keepdims=True) + EPS)
    return centred * scale, scale


def norm_back(grad, normed, scale, gain):
    scaled = grad * gain
    mean_one = jnp.mean(scaled, -1, keepdims=True)
    mean_two = jnp.mean(scaled * normed, -1, keepdims=True)
    return scale * (scaled - mean_one - normed * mean_two)


def column_sums(rows):
    return jnp.sum(rows, 0, keepdims=True)


def lane_groups(rows):
    total = rows[:, :128]
    for k in range(1, rows.shape[1] // 128):
        total = total + rows[:, 128 * k : 128 * (k + 1)]
    return total


def middle(lens, x_ref, mem_ref, gout_ref, mix_one, ckv_ref, wt_q, w_proj, w_in, w_out, bias_q, vectors, b_in,
           out_ref, g_resid, g_mix, dkv_ref, gw_cross, gw_proj, gw_in, gw_out, g_vec, g_bin,
           e_ref, q_ref, inv_ref, mix_two, gmix_two, dq_ref, acc_cross, acc_proj, acc_in, acc_out, acc_vec, acc_bin, acc_col,
           n_one, n_two):
    tags, width = x_ref.shape[1:]
    cells = mem_ref.shape[1]
    i = pl.program_id(0)
    count = pl.num_programs(0)

    @pl.when(i == 0)
    def _():
        for ref in (acc_cross, acc_proj, acc_in, acc_out, acc_vec, acc_bin, acc_col):
            ref[...] = jnp.zeros_like(ref)

    def vec(k):
        return vectors[k : k + 1, :]

    def add(k, value):
        acc_vec[k : k + 1, :] += value

    mix_one_t = mix_one[0].reshape(width, tags)
    resid = x_ref[0].astype(f32) + dot(mix_one_t, w_proj[0], 0, 0) + vec(2)
    normed, scale_one = norm(resid)
    n_one[...] = normed
    one = normed * vec(10) + vec(6)
    one_low = one.astype(bf16)
    cq = (dot(wt_q[...], one_low, 1, 1) + bias_q[...]).astype(bf16) * bf16(HEAD_DIM ** -0.5)
    q_ref[...] = cq.reshape(q_ref.shape)

    def forward(h, _):
        s = dot(ckv_ref[0, h], q_ref[h], 0, 0)
        e = jnp.exp(s - jnp.max(s, 0, keepdims=True)).astype(bf16)
        e_ref[h] = e
        mixed = dot(with_ones(ckv_ref[0, HEADS + h]), e, 1, 0)
        inv = 1.0 / mixed[HEAD_DIM : HEAD_DIM + 1]
        inv_ref[pl.ds(h, 1), :] = inv
        mix_two[h] = (mixed[:HEAD_DIM] * inv).astype(bf16)
        return 0

    lax.fori_loop(0, HEADS, forward, 0)
    mix_two_t = mix_two[...].reshape(width, tags)
    resid = one + dot(mix_two_t, w_proj[1], 0, 0) + vec(5)
    normed, scale_two = norm(resid)
    n_two[...] = normed
    two = normed * vec(11) + vec(7)
    two_low = two.astype(bf16)
    inner = dot(two_low, w_in[...], 1, 0) + b_in[...]
    root = 0.7978845608028654
    square = inner * inner
    tanh = jnp.tanh(root * inner * (1.0 + 0.044715 * square))
    act = (0.5 * inner * (1.0 + tanh)).astype(bf16)
    slope = 0.5 * (1.0 + tanh) + 0.5 * inner * (1.0 - tanh * tanh) * (root * (1.0 + 3 * 0.044715 * square))
    resid = two + dot(act, w_out[...], 1, 0) + vec(9)
    three, scale_three = norm(resid)
    valid = lax.broadcasted_iota(jnp.int32, (tags, 1), 0) < lens[i]
    out_ref[0] = jnp.where(valid, three * vec(12) + vec(8), 0.0).astype(bf16)

    grad = jnp.where(valid, gout_ref[0].astype(f32), 0.0)
    add(12, column_sums(grad * three))
    add(8, column_sums(grad))
    g_three = norm_back(grad, three, scale_three, vec(12))
    g_low = g_three.astype(bf16)
    add(9, column_sums(g_three))
    acc_out[...] += dot(act, g_low, 0, 0)
    g_inner = dot(g_low, w_out[...], 1, 1) * slope
    acc_bin[...] += column_sums(g_inner)
    g_inner = g_inner.astype(bf16)
    acc_in[...] += dot(two_low, g_inner, 0, 0)
    g_two = g_three + dot(g_inner, w_in[...], 1, 1)
    add(11, column_sums(g_two * n_two[...]))
    add(7, column_sums(g_two))
    g_two = norm_back(g_two, n_two[...], scale_two, vec(11))
    add(5, column_sums(g_two))
    g_low = g_two.astype(bf16)
    acc_proj[1] += dot(mix_two_t, g_low, 1, 0)
    gmix_two[...] = dot(w_proj[1], g_low, 1, 1).astype(bf16).reshape(gmix_two.shape)

    def backward(h, _):
        grad = gmix_two[h].astype(f32)
        inv = inv_ref[pl.ds(h, 1), :]
        delta = jnp.sum(grad * mix_two[h].astype(f32), 0, keepdims=True) * inv
        grad = (grad * inv).astype(bf16)
        e = e_ref[h]
        dp = dot(with_ones(ckv_ref[0, HEADS + h]), with_delta(grad, delta), 0, 0)
        ds = e * dp.astype(bf16)
        dkv_ref[0, HEADS + h] = dot(grad, e, 1, 1).astype(bf16)
        dkv_ref[0, h] = dot(q_ref[h], ds, 1, 1).astype(bf16)
        dq_ref[h] = (dot(ckv_ref[0, h], ds, 1, 0) * HEAD_DIM ** -0.5).astype(bf16)
        return 0

    lax.fori_loop(0, HEADS, backward, 0)
    dq = dq_ref[...].reshape(width, tags)
    dkv = dkv_ref[0].reshape(2 * width, cells)
    acc_col[0] += lane_groups(dq.astype(f32))
    body = cells // 128 * 128
    dv = dkv[width:].astype(f32)
    acc_col[1] += lane_groups(dv[:, :body])
    if body < cells:
        acc_col[1, :, : cells - body] += dv[:, body:]
    acc_cross[:width] += dot(dq, one_low, 1, 0)
    acc_cross[width:] += dot(dkv, mem_ref[0], 1, 0)
    g_one = g_two + dot(dq, wt_q[...], 0, 0)
    add(10, column_sums(g_one * n_one[...]))
    add(6, column_sums(g_one))
    g_one = norm_back(g_one, n_one[...], scale_one, vec(10))
    add(2, column_sums(g_one))
    g_resid[0] = g_one
    g_low = g_one.astype(bf16)
    acc_proj[0] += dot(mix_one_t, g_low, 1, 0)
    g_mix[0] = dot(w_proj[0], g_low, 1, 1).astype(bf16).reshape(g_mix.shape[1:])

    @pl.when(i == count - 1)
    def _():
        gw_cross[...] = acc_cross[...].astype(bf16).T
        gw_proj[...] = acc_proj[...].astype(bf16)
        gw_in[...] = acc_in[...].astype(bf16)
        gw_out[...] = acc_out[...].astype(bf16)
        add(3, column_sums(acc_col[0].T))
        add(4, column_sums(acc_col[1].T))
        g_vec[...] = acc_vec[...]
        g_bin[...] = acc_bin[...]


def run_middle(lens, x, mem, gout, mix_one, ckv, wt_cross, w_proj, w_in, w_out, bias_q, vectors, b_in):
    images, tags, width = x.shape
    cells = mem.shape[1]
    hidden = w_in.shape[1]
    sds = jax.ShapeDtypeStruct

    def per(*shape):
        return pl.BlockSpec((1,) + shape, lambda i, n: (i,) + (0,) * len(shape))

    def one(*shape):
        return pl.BlockSpec(shape, lambda i, n: (0,) * len(shape))

    return pl.pallas_call(
        middle,
        grid_spec=pltpu.PrefetchScalarGridSpec(
            num_scalar_prefetch=1,
            grid=(images,),
            in_specs=[
                per(tags, width), per(cells, width), per(tags, width), per(HEADS, HEAD_DIM, tags), per(2 * HEADS, HEAD_DIM, cells),
                one(width, width), one(2, width, width), one(width, hidden), one(hidden, width), one(width, 1), one(16, width), one(1, hidden),
            ],
            out_specs=[
                per(tags, width), per(tags, width), per(HEADS, HEAD_DIM, tags), per(2 * HEADS, HEAD_DIM, cells),
                one(width, 3 * width), one(2, width, width), one(width, hidden), one(hidden, width), one(16, width), one(1, hidden),
            ],
            scratch_shapes=[
                pltpu.VMEM((HEADS, cells, tags), bf16),
                pltpu.VMEM((HEADS, HEAD_DIM, tags), bf16),
                pltpu.VMEM((HEADS, tags), f32),
                pltpu.VMEM((HEADS, HEAD_DIM, tags), bf16),
                pltpu.VMEM((HEADS, HEAD_DIM, tags), bf16),
                pltpu.VMEM((HEADS, HEAD_DIM, tags), bf16),
                pltpu.VMEM((3 * width, width), f32),
                pltpu.VMEM((2, width, width), f32),
                pltpu.VMEM((width, hidden), f32),
                pltpu.VMEM((hidden, width), f32),
                pltpu.VMEM((16, width), f32),
                pltpu.VMEM((1, hidden), f32),
                pltpu.VMEM((2, width, 128), f32),
                pltpu.VMEM((tags, width), f32),
                pltpu.VMEM((tags, width), f32),
            ],
        ),
        out_shape=[
            sds((images, tags, width), bf16), sds((images, tags, width), f32), sds((images, HEADS, HEAD_DIM, tags), bf16),
            sds((images, 2 * HEADS, HEAD_DIM, cells), bf16),
            sds((width, 3 * width), bf16), sds((2, width, width), bf16), sds((width, hidden), bf16), sds((hidden, width), bf16),
            sds((16, width), f32), sds((1, hidden), f32),
        ],
        compiler_params=pltpu.CompilerParams(vmem_limit_bytes=62 * MIB),
        name="middle",
    )(lens, x, mem, gout, mix_one, ckv, wt_cross, w_proj, w_in, w_out, bias_q, vectors, b_in)


def self_backward(x_ref, qkv_ref, near_ref, far_ref, inv_ref, mix_ref, gmix_ref, g_resid, dkv_ref, wt_self, wt_cross,
                  g_tags, g_mem, gw_self, g_col, d_ref, acc, acc_col):
    tags, width = x_ref.shape[1:]
    half = tags // 2
    i = pl.program_id(0)

    @pl.when(i == 0)
    def _():
        acc[...] = jnp.zeros_like(acc)
        acc_col[...] = jnp.zeros_like(acc_col)

    def head(h, _):
        grad = gmix_ref[0, h].astype(f32)
        inv = inv_ref[0, pl.ds(h, 1), :]
        delta = jnp.sum(grad * mix_ref[0, h].astype(f32), 0, keepdims=True) * inv
        grad = (grad * inv).astype(bf16)
        ext = with_delta(grad, delta)
        qt, kt, vt = qkv_ref[0, h], qkv_ref[0, HEADS + h], with_ones(qkv_ref[0, 2 * HEADS + h])
        near, far = near_ref[0, h], far_ref[0, h]
        ds_near = near * dot(vt[:, :half], ext[:, :half], 0, 0).astype(bf16)
        ds_far = far * dot(vt, ext[:, half:], 0, 0).astype(bf16)
        dv = dot(grad[:, half:], far, 1, 1)
        dk = dot(qt[:, half:], ds_far, 1, 1)
        d_ref[2 * HEADS + h, :, half:] = dv[:, half:].astype(bf16)
        d_ref[2 * HEADS + h, :, :half] = (dv[:, :half] + dot(grad[:, :half], near, 1, 1)).astype(bf16)
        d_ref[HEADS + h, :, half:] = dk[:, half:].astype(bf16)
        d_ref[HEADS + h, :, :half] = (dk[:, :half] + dot(qt[:, :half], ds_near, 1, 1)).astype(bf16)
        d_ref[h, :, :half] = (dot(kt[:, :half], ds_near, 1, 0) * HEAD_DIM ** -0.5).astype(bf16)
        d_ref[h, :, half:] = (dot(kt, ds_far, 1, 0) * HEAD_DIM ** -0.5).astype(bf16)
        return 0

    lax.fori_loop(0, HEADS, head, 0)
    d = d_ref[...].reshape(3 * width, tags)
    acc_col[0] += lane_groups(d[:width].astype(f32))
    acc_col[1] += lane_groups(d[2 * width :].astype(f32))
    acc[...] += dot(d, x_ref[0], 1, 0)
    g_tags[0] = g_resid[0] + dot(d, wt_self[...], 0, 0)
    g_mem[0] = dot(dkv_ref[0].reshape(2 * width, -1), wt_cross[width:], 0, 0)

    @pl.when(i == pl.num_programs(0) - 1)
    def _():
        gw_self[...] = acc[...].astype(bf16).T
        g_col[0:1] = column_sums(acc_col[0].T)
        g_col[1:2] = column_sums(acc_col[1].T)


def run_self_backward(x, qkv, near, far, inv, mix, gmix, g_resid, dkv, wt_self, wt_cross):
    images, tags, width = x.shape
    cells = dkv.shape[3]
    half = tags // 2
    sds = jax.ShapeDtypeStruct

    def per(*shape):
        return pl.BlockSpec((1,) + shape, lambda i: (i,) + (0,) * len(shape))

    def one(*shape):
        return pl.BlockSpec(shape, lambda i: (0,) * len(shape))

    return pl.pallas_call(
        self_backward,
        grid=(images,),
        in_specs=[per(tags, width), per(3 * HEADS, HEAD_DIM, tags), per(HEADS, half, half), per(HEADS, tags, half), per(HEADS, tags),
                  per(HEADS, HEAD_DIM, tags), per(HEADS, HEAD_DIM, tags), per(tags, width), per(2 * HEADS, HEAD_DIM, cells),
                  one(3 * width, width), one(3 * width, width)],
        out_specs=[per(tags, width), per(cells, width), one(width, 3 * width), one(8, width)],
        out_shape=[sds((images, tags, width), f32), sds((images, cells, width), f32), sds((width, 3 * width), bf16), sds((8, width), f32)],
        scratch_shapes=[pltpu.VMEM((3 * HEADS, HEAD_DIM, tags), bf16), pltpu.VMEM((3 * width, width), f32), pltpu.VMEM((2, width, 128), f32)],
        compiler_params=pltpu.CompilerParams(vmem_limit_bytes=60 * MIB),
        name="self_backward",
    )(x, qkv, near, far, inv, mix, gmix, g_resid, dkv, wt_self, wt_cross)


def layer(lens, x, mem, gout, w_self, w_cross, w_proj, w_in, w_out, vectors, b_in):
    width = x.shape[2]
    zero = jnp.zeros((width,), f32)
    bias_qkv = jnp.concatenate([vectors[0], zero, vectors[1]])[:, None]
    bias_kv = jnp.concatenate([zero, vectors[4]])[:, None]
    bias_q = vectors[3][:, None]
    qkv, ckv, near, far, inv, mix, wt_self, wt_cross = run_self_forward(lens, x, mem, w_self, w_cross, bias_qkv, bias_kv)
    out, g_resid, gmix, dkv, gw_cross, gw_proj, gw_in, gw_out, g_vec, g_bin = run_middle(
        lens, x, mem, gout, mix, ckv, wt_cross, w_proj, w_in, w_out, bias_q, vectors, b_in)
    g_tags, g_mem, gw_self, g_col = run_self_backward(x, qkv, near, far, inv, mix, gmix, g_resid, dkv, wt_self, wt_cross)
    g_vec = g_vec.at[0:2].set(g_col[0:2])
    return out, g_tags, g_mem, gw_self, gw_cross, gw_proj, gw_in, gw_out, g_vec, g_bin


AXES = ("wide", "narrow")
LEADS = (0, 0, 1, 0, 0, 0)


def fold(block, rows, columns):
    if rows % 16 == 0:
        return block
    return block.reshape(block.shape[:-2] + (16, rows * columns // 16))


def per_device(dims, tag_states, image_memory, tag_lengths, w_self, w_cross, w_proj, w_in, b_in, w_out, ln_gains, biases, out_grad):
    cells = dims + (2,)
    devices = dims[0] * dims[1] * dims[2] * 2
    width = tag_states.shape[2]
    lanes, hidden_lanes = biases.shape[1], b_in.shape[0]
    small = jnp.concatenate(
        [
            jnp.pad(jnp.concatenate([biases, ln_gains]), ((0, 0), (0, 128 - lanes))),
            jnp.pad(b_in[None], ((0, 2), (0, 128 - hidden_lanes))),
        ]
    )
    shards = (w_self, w_cross, w_proj, w_in, w_out, small)
    gathered = gather(dims, [fold(s, *s.shape[-2:]) for s in shards], LEADS)

    def whole(held, shard):
        lead = shard.shape[:-2]
        rows, columns = shard.shape[-2:]
        return held.reshape(lead + (devices * rows, columns))

    full_self, full_cross, full_proj, full_in, full_out, full_small = [whole(h, s) for h, s in zip(gathered, shards)]
    by_device = full_small.reshape(devices, 16, 128)
    vectors = by_device[:, :, :lanes].transpose(1, 0, 2).reshape(16, width).astype(f32)
    hidden_bias = by_device[:, 13, :hidden_lanes].reshape(1, -1).astype(f32)
    layer_out, grad_tags, grad_memory, g_self, g_cross, g_proj, g_in, g_out, g_vec, g_bin = layer(
        tag_lengths, tag_states, image_memory, out_grad, full_self, full_cross, full_proj, full_in, full_out, vectors, hidden_bias)
    g_small = jnp.pad(g_vec.reshape(16, devices, lanes).transpose(1, 0, 2)[:, :13], ((0, 0), (0, 0), (0, 128 - lanes)))
    g_hidden = jnp.pad(g_bin.reshape(devices, 1, hidden_lanes), ((0, 0), (0, 2), (0, 128 - hidden_lanes)))
    g_small = jnp.concatenate([g_small, g_hidden], 1).astype(bf16).reshape(devices * 16, 128)

    def parts(grad, shard):
        lead = shard.shape[:-2]
        rows, columns = shard.shape[-2:]
        return fold(grad.reshape(lead + cells + (rows, columns)), rows, columns)

    shares = scatter(dims, [parts(g, s) for g, s in zip((g_self, g_cross, g_proj, g_in, g_out, g_small), shards)], LEADS)
    s_self, s_cross, s_proj, s_in, s_out, s_small = [v.reshape(s.shape) for v, s in zip(shares, shards)]
    return (layer_out, grad_tags, grad_memory, s_self, s_cross, s_proj, s_in, s_small[13, :hidden_lanes], s_out,
            s_small[10:13, :lanes], s_small[:10, :lanes])


def solution(mesh):
    dims = grid_of(mesh.shape["wide"], mesh.shape["narrow"])
    rows, matrix, stack, columns = P(AXES, None, None), P(AXES, None), P(None, AXES, None), P(None, AXES)
    return jax.shard_map(
        functools.partial(per_device, dims),
        mesh=mesh,
        in_specs=(rows, rows, P(AXES), matrix, matrix, stack, matrix, P(AXES), matrix, columns, columns, rows),
        out_specs=(rows, rows, rows, matrix, matrix, stack, matrix, P(AXES), matrix, columns, columns),
        check_vma=False,
    )
```

time: 1370 us -> 258 us (0.19)
  waiting for transfers between devices: 706 us -> 0 us
  Pallas kernels: 0 us -> 241 us
  matrix products: 230 us -> 0 us
  blocking collectives: 159 us -> 0 us
  local copies, waits for them, and re-layouts: 160 us -> 13 us
  other arithmetic: 92.4 us -> 3 us
  between operations: 15.3 us -> 0.84 us
    reduce_scatter x3 -> x0, waiting for transfers between devices: 405 us -> none  [the longest x1 136 us: per_device(): lax.psum_scatter(grad_w_out, ('wide', 'narrow'), scatter_dimension=0, til...]
    unnamed x16 -> x0, waiting for transfers between devices: 268 us -> none
    pallas_call x0 -> x5, Pallas kernels: none -> 241 us  [the longest x1 87.7 us: run_middle(): pl.pallas_call(middle, grid_spec=pltpu.PrefetchScalarGridSpec(num_scalar_...]
    dot_general x63 -> x0, matrix products: 230 us -> none  [the longest x6 49.4 us: attend_back(): jnp.einsum('qhd,khd->hqk', grad_heads, split_heads(value_rows), preferred...]
    unnamed x2 -> x0, blocking collectives: 81.7 us -> none
    all_gather x2 -> x0, blocking collectives: 77.6 us -> none  [the longest x1 40.5 us: per_device(): lax.all_gather(ln_gains, ('wide', 'narrow'), axis=1, tiled=True)]
    convert_element_type x11 -> x2, other arithmetic: 51.3 us -> 0.94 us  [the longest x1 0.93 us: per_device(): by_device[:, :, :lanes].transpose(1, 0, 2).reshape(16, width).astype(f32)]
    dynamic_update_slice x33 -> x0, local copies, waits for them, and re-layouts: 46.5 us -> none  [the longest x9 21.2 us: per_device(): lax.map(cross_back, (cross_q, cross_kv, cross_total, grad_cm))]
  transfers between devices with their start and end apart: 12 -> 0, of which waited for: 7 -> 0; matrix products, arithmetic and copies ran while one was open for 21% -> 0% of each run, Pallas kernels for 0% -> 0%
where the time goes in v1:
time: 258 us
  Pallas kernels  241 us (93%)
  local copies, waits for them, and re-layouts  13 us (5%)
  other arithmetic  3 us (1%)
    pallas_call x1, Pallas kernels, run_middle(): pl.pallas_call(middle, grid_spec=pltpu.PrefetchScalarGridSpec(num_scalar_...  87.7 us
    pallas_call x1, Pallas kernels, scatter(): pl.pallas_call(functools.partial(scatter_kernel, dims, leads), out_shape=...  46.1 us
    pallas_call x1, Pallas kernels, gather(): pl.pallas_call(functools.partial(gather_kernel, dims, leads), out_shape=[...  45.7 us
    pallas_call x1, Pallas kernels, run_self_backward(): pl.pallas_call(self_backward, grid=(images,), in_specs=[per(tags, width),...  31.5 us
    pallas_call x1, Pallas kernels, run_self_forward(): pl.pallas_call(self_forward, grid_spec=pltpu.PrefetchScalarGridSpec(num_s...  29.7 us
    unnamed x19, local copies, waits for them, and re-layouts  5.24 us

profile of v1, /device:TPU:0, one launch (start us, length us, event | category | flops | bytes accessed | tf_op | source)
XLA Modules:
  0.0 257.6 jit_solution(3307709993991029440)
XLA Ops:
  0.6 0.7 fusion.4
  1.4 1.3 fusion.3.refs_5_
  2.6 45.7 %gather_weights.1 = (bf16[4,2,2,2,16,1536]{5,4,3,2,1,0:T(8,128)(2,1)}, bf16[4,2,2,2,16,1536]{5,4,3,2,1,0:T(8,128)(2,1)}, bf16[2,4,2,2,2,16,512]{6,5,4,3,2,1,0:T(...) custom-call(bf16[16,1536]{1,0:T(8,128)(2,1)} %refs_0_.1, ...), custom_call_target="tpu_custom_call" | custom-call | tf_op jit(solution)/shard_map/gather_weights/pallas_call | solution.py:154
  48.4 0.9 slice.71
  49.2 0.7 reshape.126.b_in
  49.9 0.9 convert_bitcast_fusion
  50.8 0.8 convert_element_type.24.vectors
  51.6 0.1 squeeze.14
  51.7 0.1 squeeze.13
  51.8 0.1 squeeze.12
  51.9 0.9 broadcast_in_dim_squeeze.4.bias_q
  52.8 1.0 copy.29.bias_kv
  53.8 1.1 broadcast_in_dim.16.bias_qkv
  54.9 29.7 %self_forward.1 = (bf16[3,24,64,512]{3,2,1,0:T(8,128)(2,1)}, bf16[3,16,64,784]{3,2,1,0:T(8,128)(2,1)}, bf16[3,8,256,256]{3,2,1,0:T(8,128)(2,1)}, bf16[3,8,512,25...) custom-call(s32[3]{0:T(128)} %lens.3, ...), custom_call_target="tpu_custom_call" | custom-call | tf_op jit(solution)/shard_map/self_forward/pallas_call | solution.py:398
  84.6 87.7 %middle.1 = (bf16[3,512,512]{2,1,0:T(8,128)(2,1)}, f32[3,512,512]{2,1,0:T(8,128)}, bf16[3,8,64,512]{3,2,1,0:T(8,128)(2,1)}, bf16[3,16,64,784]{3,2,1,0:T(8,128)(2...) custom-call(s32[3]{0:T(128)} %lens.3, ...), custom_call_target="tpu_custom_call" | custom-call | tf_op jit(solution)/shard_map/middle/pallas_call | solution.py:590
  172.3 0.0 copy-start.4
  172.3 0.0 copy-start.5
  172.4 31.5 %self_backward.1 = (f32[3,512,512]{2,1,0:T(8,128)}, f32[3,784,512]{2,1,0:T(8,128)}, bf16[512,1536]{1,0:T(8,128)(2,1)}, f32[8,512]{1,0:T(8,128)}) custom-call(bf16[3,512,512]{2,1,0:T(8,128)(2,1)} %x_ref.5, bf16[3,24,64,512]{3,2,1,0:T(8,128)(2,1)} %get-tuple-element.67.qkv_ref, bf16[3,8,256,256]{3,2,1,0:T(8,128)(2,1)} %get-tuple-element.68.near_ref, ...), custom_call_target="tpu_custom_call" | custom-call | tf_op jit(solution)/shard_map/self_backward/pallas_call | solution.py:690
  203.9 0.8 slice_dynamic-update-slice_fusion
  204.7 0.1 reshape.127
  204.8 0.1 reshape.124
  205.1 0.1 pad_maximum_fusion.refs_5_
  205.2 1.4 copy-done
  206.6 46.1 %scatter_grads.1 = (f32[16,1536]{1,0:T(8,128)S(1)}, f32[16,1536]{1,0:T(8,128)S(1)}, f32[2,16,512]{2,1,0:T(8,128)S(1)}, f32[16,1024]{1,0:T(8,128)S(1)}, f32[32,512]{1,0:T(8,128)S(1)}, /*index=5*/f32[16,128]{1,0:T(8,128)S(1)}) custom-call(bf16[4,2,2,2,16,1536]{5,4,3,2,1,0:T(8,128)(2,1)S(1)} %bitcast.24, bf16[4,2,2,2,16,1536]{5,4,3,2,1,0:T(8,128)(2,1)} %bitcast.31, ...), custom_call_target="tpu_custom_call" | custom-call | tf_op jit(solution)/shard_map/scatter_grads/pallas_call | solution.py:310
  252.7 0.5 slice_bitcast_fusion
  253.2 0.6 slice.64
  253.8 0.6 copy.46
  254.4 0.6 copy.47
  255.1 0.6 copy.48
  255.7 0.6 copy.49
  256.3 0.6 copy.50
  257.0 0.6 copy.51
  (20 shorter events, 0.2 us)
Async XLA Ops:
  172.3 31.5 %copy-start.4 = (f32[16,512]{1,0:T(8,128)S(1)}, f32[16,512]{1,0:T(8,128)}, u32[]{:S(2)}) copy-start(f32[16,512]{1,0:T(8,128)} %get-tuple-element.82) | copy-start | bytes 98308
  172.3 32.4 %copy-start.5 = (f32[1,1024]{1,0:T(1,128)S(1)}, f32[1,1024]{1,0:T(1,128)}, u32[]{:S(2)}) copy-start(f32[1,1024]{1,0:T(1,128)} %get-tuple-element.84) | copy-start | bytes 12292
  172.3 32.8 %copy-start.2 = (bf16[512,1024]{1,0:T(8,128)(2,1)S(1)}, bf16[512,1024]{1,0:T(8,128)(2,1)}, u32[]{:S(2)}) copy-start(bf16[512,1024]{1,0:T(8,128)(2,1)} %get-tuple-element.80) | copy-start | bytes 3145732
  172.3 32.8 %copy-start.3 = (bf16[1024,512]{1,0:T(8,128)(2,1)S(1)}, bf16[1024,512]{1,0:T(8,128)(2,1)}, u32[]{:S(2)}) copy-start(bf16[1024,512]{1,0:T(8,128)(2,1)} %get-tuple-element.81) | copy-start | bytes 3145732
  203.8 1.3 copy-start.1
  205.2 1.4 copy-start

commit v2 on v1

--- a/solution.py
+++ b/solution.py
@@ -715,6 +715,300 @@
     return out, g_tags, g_mem, gw_self, gw_cross, gw_proj, gw_in, gw_out, g_vec, g_bin
 
 
+ALL = slice(None)
+
+
+class Gathering:
+    def __init__(self, dims, me, shard, held, lead, sems):
+        self.dims, self.me, self.shard, self.held, self.lead = dims, me, shard, held, lead
+        self.local, self.send, self.recv = sems
+
+    def cell(self, *index):
+        return self.held.at[(ALL,) * self.lead + index]
+
+    def remote(self, slot, src, dst, peer):
+        return pltpu.make_async_remote_copy(
+            src_ref=src, dst_ref=dst, send_sem=self.send.at[slot], recv_sem=self.recv.at[slot],
+            device_id=device(self.dims, *peer), device_id_type=MESH)
+
+    def keep(self):
+        return pltpu.make_async_copy(self.shard, self.cell(*self.me), self.local)
+
+    def first(self):
+        a, b, x, c = self.me
+        outer = self.dims[0]
+        return [self.remote(k - 1, self.shard, self.cell(a, b, x, c), (lax.rem(a + k, outer), b, x, c)) for k in range(1, outer)]
+
+    def along_inner(self, core):
+        a, b, x, c = self.me
+        outer, inner, _ = self.dims
+        piece = self.cell(ALL, b, ALL if core == 0 else x, c)
+        return [self.remote(outer - 2 + k, piece, piece, (a, lax.rem(b + k, inner), x, c)) for k in range(1, inner)]
+
+    def along_across(self, core):
+        a, b, x, c = self.me
+        outer, inner, across = self.dims
+        piece = self.cell(ALL, b if core == 0 else ALL, x, c)
+        return [self.remote(outer + inner - 3 + k, piece, piece, (a, b, lax.rem(x + k, across), c)) for k in range(1, across)]
+
+    def second(self, core):
+        return self.along_across(core) if core == 0 else self.along_inner(core)
+
+    def third(self, core):
+        return self.along_inner(core) if core == 0 else self.along_across(core)
+
+    def handed(self, core, holder):
+        a, b, x, c = self.me
+        outer, inner, across = self.dims
+        base = outer + inner + across - 3
+
+        def piece(slot, row, column):
+            ref = self.cell(ALL, row, column, holder)
+            return self.remote(base + slot, ref, ref, (a, b, x, 1 - c))
+
+        own = [piece(0, b, x)]
+        by_inner = [piece(k, lax.rem(b + k, inner), ALL if core == 0 else x) for k in range(1, inner)]
+        by_across = [piece(inner - 1 + k, b if core == 0 else ALL, lax.rem(x + k, across)) for k in range(1, across)]
+        return (own, by_across, by_inner) if core == 0 else (own, by_inner, by_across)
+
+    def begin(self):
+        self.keep().start()
+        for copy in self.first():
+            copy.start()
+
+    def each_core(self, act):
+        for core in (0, 1):
+            pl.when(self.me[3] == core)(functools.partial(act, core))
+
+    def advance(self, stage):
+        def act(core):
+            if stage == 1:
+                self.keep().wait()
+            for copy in (self.first(), self.second(core), self.third(core))[stage - 1]:
+                copy.wait_recv()
+            following = (self.second(core), self.third(core), [])[stage - 1]
+            for copy in following + self.handed(core, self.me[3])[stage - 1]:
+                copy.start()
+        self.each_core(act)
+
+    def finish(self):
+        def act(core):
+            for group in self.handed(1 - core, 1 - self.me[3]):
+                for copy in group:
+                    copy.wait_recv()
+        self.each_core(act)
+
+    def drain(self):
+        def act(core):
+            for copy in self.first() + self.second(core) + self.third(core) + sum(self.handed(core, self.me[3]), []):
+                copy.wait_send()
+        self.each_core(act)
+
+
+def gather_slots(dims):
+    outer, inner, across = dims
+    return outer + 2 * (inner + across) - 4
+
+
+def spread(held, row_lanes, width, rows):
+    devices = held.shape[0] // 16
+    lane = lax.broadcasted_iota(jnp.int32, (128, width), 0)
+    at = lax.broadcasted_iota(jnp.int32, (128, width), 1)
+    pick = jnp.where((lax.rem(at, row_lanes) == lane), 1.0, 0.0).astype(bf16)
+    wide = dot(held, pick, 1, 0)
+    owner = lax.broadcasted_iota(jnp.int32, (devices * 16, width), 0) // 16
+    at = lax.broadcasted_iota(jnp.int32, (devices * 16, width), 1)
+    wide = jnp.where(at // row_lanes == owner, wide, 0.0)
+    return jnp.sum(wide.reshape(devices, 16, width), 0)
+
+
+def opening(dims, lens, x_ref, mem_ref, b_ref, g_ref, h_ref, s_cross, s_self, s_proj, s_in, s_out,
+            qkv_ref, ckv_ref, near_ref, far_ref, inv_ref, mix_ref, wt_self, wt_cross, vec_ref, bin_ref, o_proj, o_in, o_out,
+            small, small_low, h_small, h_kv, h_self, h_q, cols, local, send, recv):
+    width = x_ref.shape[2]
+    tags = x_ref.shape[1]
+    half = tags // 2
+    step = pl.program_id(0)
+    images = pl.num_programs(0) // 2
+    me = place(dims)
+    s_kv, s_q = s_cross.at[:, width:], s_cross.at[:, :width]
+    pairs = ((small_low, h_small, 0), (s_kv, h_kv, 0), (s_self, h_self, 0), (s_q, h_q, 0), (s_proj, o_proj, 1), (s_in, o_in, 0), (s_out, o_out, 0))
+    gs = [Gathering(dims, me, shard, held, lead, (local.at[k], send.at[k], recv.at[k])) for k, (shard, held, lead) in enumerate(pairs)]
+    g_small, g_kv, g_self, g_q, g_proj, g_in, g_out = gs
+
+    @pl.when(step == 0)
+    def _():
+        small[...] = jnp.zeros_like(small)
+        small[0:10, : b_ref.shape[1]] = b_ref[...].astype(f32)
+        small[10:13, : g_ref.shape[1]] = g_ref[...].astype(f32)
+        small[13:14, : h_ref.shape[1]] = h_ref[...].astype(f32)
+        small_low[...] = small[...].astype(bf16)
+        greet(dims, me)
+        g_small.begin()
+        g_kv.begin()
+        g_self.begin()
+        g_small.advance(1)
+        g_kv.advance(1)
+        g_q.begin()
+        g_proj.begin()
+        g_small.advance(2)
+        g_kv.advance(2)
+        g_self.advance(1)
+        g_small.advance(3)
+        g_kv.advance(3)
+        g_in.begin()
+        g_self.advance(2)
+        g_out.begin()
+        g_small.finish()
+        vectors = spread(h_small[...].reshape(-1, 128), b_ref.shape[1], width, 16)
+        vec_ref[...] = vectors
+        bin_ref[...] = spread(h_small[...].reshape(-1, 128), h_ref.shape[1], bin_ref.shape[1], 16)[13:14]
+        cols[...] = vectors.T
+        g_kv.finish()
+        wt_cross[width:] = h_kv[...].reshape(width, 2 * width).T
+
+    @pl.when(step < images)
+    def _():
+        kv = dot(wt_cross[width:], mem_ref[0], 1, 1)
+        heads = ckv_ref.shape[1] // 2
+        ckv_ref[0, :heads] = kv[:width].astype(bf16).reshape(heads, HEAD_DIM, -1)
+        ckv_ref[0, heads:] = (kv[width:] + cols[:, 4:5]).astype(bf16).reshape(heads, HEAD_DIM, -1)
+
+    @pl.when(step == 0)
+    def _():
+        g_self.advance(3)
+        g_q.advance(1)
+        g_proj.advance(1)
+
+    @pl.when(step == 1)
+    def _():
+        g_q.advance(2)
+        g_proj.advance(2)
+        g_in.advance(1)
+
+    @pl.when(step == 2)
+    def _():
+        g_q.advance(3)
+        g_proj.advance(3)
+        g_in.advance(2)
+        g_out.advance(1)
+
+    @pl.when(step == images)
+    def _():
+        g_self.finish()
+        wt_self[...] = h_self[...].reshape(width, 3 * width).T
+
+    @pl.when(step >= images)
+    def _():
+        qkv = dot(wt_self[...], x_ref[0], 1, 1)
+        qkv_ref[0, :HEADS] = ((qkv[:width] + cols[:, 0:1]).astype(bf16) * bf16(HEAD_DIM ** -0.5)).reshape(HEADS, HEAD_DIM, tags)
+        qkv_ref[0, HEADS : 2 * HEADS] = qkv[width : 2 * width].astype(bf16).reshape(HEADS, HEAD_DIM, tags)
+        qkv_ref[0, 2 * HEADS :] = (qkv[2 * width :] + cols[:, 1:2]).astype(bf16).reshape(HEADS, HEAD_DIM, tags)
+
+    @pl.when(step == images)
+    def _():
+        g_in.advance(3)
+        g_out.advance(2)
+
+    def head(h, _):
+        qt, kt, vt = qkv_ref[0, h], qkv_ref[0, HEADS + h], with_ones(qkv_ref[0, 2 * HEADS + h])
+        last = lens[jnp.maximum(step - images, 0)] - 1
+
+        def part(keys, first, out):
+            s = dot(kt[:, :keys], qt[:, first : first + half], 0, 0)
+            key_at = lax.broadcasted_iota(jnp.int32, (keys, half), 0)
+            query_at = lax.broadcasted_iota(jnp.int32, (1, half), 1) + first
+            s = jnp.where(key_at <= jnp.minimum(query_at, last), s, MASKED)
+            e = jnp.exp(s - jnp.max(s, 0, keepdims=True)).astype(bf16)
+            out[0, h] = e
+            mixed = dot(vt[:, :keys], e, 1, 0)
+            inv = 1.0 / mixed[HEAD_DIM : HEAD_DIM + 1]
+            inv_ref[0, pl.ds(h, 1), first : first + half] = inv
+            mix_ref[0, h, :, first : first + half] = (mixed[:HEAD_DIM] * inv).astype(bf16)
+
+        part(half, 0, near_ref)
+        part(tags, half, far_ref)
+        return 0
+
+    @pl.when(step >= images)
+    def _():
+        lax.fori_loop(0, HEADS, head, 0)
+
+    @pl.when(step == images)
+    def _():
+        g_out.advance(3)
+
+    @pl.when(step == 2 * images - 1)
+    def _():
+        g_q.finish()
+        wt_cross[:width] = h_q[...].reshape(width, width).T
+        for g in (g_proj, g_in, g_out):
+            g.finish()
+        for g in gs:
+            g.drain()
+
+
+def run_opening(dims, lens, x, mem, biases, gains, b_in, shards):
+    images, tags, width = x.shape
+    cells = mem.shape[1]
+    half = tags // 2
+    hidden = b_in.shape[1] * dims[0] * dims[1] * dims[2] * 2
+    sds = jax.ShapeDtypeStruct
+
+    def early(*shape):
+        return pl.BlockSpec((1,) + shape, lambda i: (jnp.minimum(i, images - 1),) + (0,) * len(shape))
+
+    def late(*shape):
+        return pl.BlockSpec((1,) + shape, lambda i: (jnp.maximum(i - images, 0),) + (0,) * len(shape))
+
+    def one(*shape):
+        return pl.BlockSpec(shape, lambda i: (0,) * len(shape))
+
+    def held(shard, lead):
+        return shard.shape[:lead] + dims + (2,) + shard.shape[lead:]
+
+    s_cross, s_self, s_proj, s_in, s_out = shards
+    rows = s_cross.shape[0]
+    cell = dims + (2, rows)
+    anywhere = pl.BlockSpec(memory_space=pl.ANY)
+    n = len(shards) + 2
+    slots = gather_slots(dims)
+    return pl.pallas_call(
+        functools.partial(opening, dims),
+        grid=(2 * images,),
+        in_specs=[pl.BlockSpec(memory_space=pltpu.SMEM), late(tags, width), early(cells, width), one(*biases.shape), one(*gains.shape), one(*b_in.shape)]
+        + [anywhere] * len(shards),
+        out_specs=[
+            late(3 * HEADS, HEAD_DIM, tags), early(2 * HEADS, HEAD_DIM, cells), late(HEADS, half, half), late(HEADS, tags, half),
+            late(HEADS, tags), late(HEADS, HEAD_DIM, tags), one(3 * width, width), one(3 * width, width), one(16, width), one(1, hidden),
+            anywhere, anywhere, anywhere,
+        ],
+        out_shape=[
+            sds((images, 3 * HEADS, HEAD_DIM, tags), bf16),
+            sds((images, 2 * HEADS, HEAD_DIM, cells), bf16),
+            sds((images, HEADS, half, half), bf16),
+            sds((images, HEADS, tags, half), bf16),
+            sds((images, HEADS, tags), f32),
+            sds((images, HEADS, HEAD_DIM, tags), bf16),
+            sds((3 * width, width), bf16),
+            sds((3 * width, width), bf16),
+            sds((16, width), f32),
+            sds((1, hidden), f32),
+            sds(held(s_proj, 1), bf16),
+            sds(held(s_in, 0), bf16),
+            sds(held(s_out, 0), bf16),
+        ],
+        scratch_shapes=[
+            pltpu.VMEM((16, 128), f32), pltpu.VMEM((16, 128), bf16), pltpu.VMEM(dims + (2, 16, 128), bf16),
+            pltpu.VMEM(cell + (2 * width,), bf16), pltpu.VMEM(cell + (3 * width,), bf16), pltpu.VMEM(cell + (width,), bf16),
+            pltpu.VMEM((width, 16), f32),
+            pltpu.SemaphoreType.DMA((n,)), pltpu.SemaphoreType.DMA((n, slots)), pltpu.SemaphoreType.DMA((n, slots)),
+        ],
+        compiler_params=pltpu.CompilerParams(collective_id=0, has_side_effects=True, vmem_limit_bytes=58 * MIB),
+        name="opening",
+    )(lens, x, mem, biases, gains, b_in, *shards)
+
+
 AXES = ("wide", "narrow")
 LEADS = (0, 0, 1, 0, 0, 0)
 
@@ -727,29 +1021,39 @@
 
 def per_device(dims, tag_states, image_memory, tag_lengths, w_self, w_cross, w_proj, w_in, b_in, w_out, ln_gains, biases, out_grad):
     cells = dims + (2,)
+    fused = w_self.shape[0] % 16 == 0
     devices = dims[0] * dims[1] * dims[2] * 2
     width = tag_states.shape[2]
     lanes, hidden_lanes = biases.shape[1], b_in.shape[0]
-    small = jnp.concatenate(
-        [
-            jnp.pad(jnp.concatenate([biases, ln_gains]), ((0, 0), (0, 128 - lanes))),
-            jnp.pad(b_in[None], ((0, 2), (0, 128 - hidden_lanes))),
-        ]
-    )
-    shards = (w_self, w_cross, w_proj, w_in, w_out, small)
-    gathered = gather(dims, [fold(s, *s.shape[-2:]) for s in shards], LEADS)
-
-    def whole(held, shard):
-        lead = shard.shape[:-2]
-        rows, columns = shard.shape[-2:]
-        return held.reshape(lead + (devices * rows, columns))
-
-    full_self, full_cross, full_proj, full_in, full_out, full_small = [whole(h, s) for h, s in zip(gathered, shards)]
-    by_device = full_small.reshape(devices, 16, 128)
-    vectors = by_device[:, :, :lanes].transpose(1, 0, 2).reshape(16, width).astype(f32)
-    hidden_bias = by_device[:, 13, :hidden_lanes].reshape(1, -1).astype(f32)
-    layer_out, grad_tags, grad_memory, g_self, g_cross, g_proj, g_in, g_out, g_vec, g_bin = layer(
-        tag_lengths, tag_states, image_memory, out_grad, full_self, full_cross, full_proj, full_in, full_out, vectors, hidden_bias)
+    if fused:
+        qkv, ckv, near, far, inv, mix, wt_self, wt_cross, vectors, hidden_bias, full_proj, full_in, full_out = run_opening(
+            dims, tag_lengths, tag_states, image_memory, biases, ln_gains, b_in[None], (w_cross, w_self, w_proj, w_in, w_out))
+        full_proj, full_in, full_out = full_proj.reshape(2, width, width), full_in.reshape(width, -1), full_out.reshape(-1, width)
+        layer_out, g_resid, gmix, dkv, g_cross, g_proj, g_in, g_out, g_vec, g_bin = run_middle(
+            tag_lengths, tag_states, image_memory, out_grad, mix, ckv, wt_cross, full_proj, full_in, full_out, vectors[3][:, None], vectors, hidden_bias)
+        grad_tags, grad_memory, g_self, g_col = run_self_backward(tag_states, qkv, near, far, inv, mix, gmix, g_resid, dkv, wt_self, wt_cross)
+        g_vec = g_vec.at[0:2].set(g_col[0:2])
+    else:
+        small = jnp.concatenate(
+            [
+                jnp.pad(jnp.concatenate([biases, ln_gains]), ((0, 0), (0, 128 - lanes))),
+                jnp.pad(b_in[None], ((0, 2), (0, 128 - hidden_lanes))),
+            ]
+        )
+        shards = (w_self, w_cross, w_proj, w_in, w_out, small)
+        gathered = gather(dims, [fold(s, *s.shape[-2:]) for s in shards], LEADS)
+
+        def whole(held, shard):
+            lead = shard.shape[:-2]
+            rows, columns = shard.shape[-2:]
+            return held.reshape(lead + (devices * rows, columns))
+
+        full_self, full_cross, full_proj, full_in, full_out, full_small = [whole(h, s) for h, s in zip(gathered, shards)]
+        by_device = full_small.reshape(devices, 16, 128)
+        vectors = by_device[:, :, :lanes].transpose(1, 0, 2).reshape(16, width).astype(f32)
+        hidden_bias = by_device[:, 13, :hidden_lanes].reshape(1, -1).astype(f32)
+        layer_out, grad_tags, grad_memory, g_self, g_cross, g_proj, g_in, g_out, g_vec, g_bin = layer(
+            tag_lengths, tag_states, image_memory, out_grad, full_self, full_cross, full_proj, full_in, full_out, vectors, hidden_bias)
     g_small = jnp.pad(g_vec.reshape(16, devices, lanes).transpose(1, 0, 2)[:, :13], ((0, 0), (0, 0), (0, 128 - lanes)))
     g_hidden = jnp.pad(g_bin.reshape(devices, 1, hidden_lanes), ((0, 0), (0, 2), (0, 128 - hidden_lanes)))
     g_small = jnp.concatenate([g_small, g_hidden], 1).astype(bf16).reshape(devices * 16, 128)
@@ -759,6 +1063,7 @@
         rows, columns = shard.shape[-2:]
         return fold(grad.reshape(lead + cells + (rows, columns)), rows, columns)
 
+    shards = (w_self, w_cross, w_proj, w_in, w_out, jax.ShapeDtypeStruct((16, 128), bf16))
     shares = scatter(dims, [parts(g, s) for g, s in zip((g_self, g_cross, g_proj, g_in, g_out, g_small), shards)], LEADS)
     s_self, s_cross, s_proj, s_in, s_out, s_small = [v.reshape(s.shape) for v, s in zip(shares, shards)]
     return (layer_out, grad_tags, grad_memory, s_self, s_cross, s_proj, s_in, s_small[13, :hidden_lanes], s_out,

time: 258 us -> 247 us (0.957)
  Pallas kernels: 241 us -> 236 us
  local copies, waits for them, and re-layouts: 13 us -> 8.94 us
  other arithmetic: 3 us -> 0.08 us
    pallas_call x1, Pallas kernels: 46.1 us -> 41.8 us  [scatter(): pl.pallas_call(functools.partial(scatter_kernel, dims, leads), out_shape=...]
    pallas_call x2 -> x1, Pallas kernels: 75.4 us -> 75.6 us  [run_opening(): pl.pallas_call(functools.partial(opening, dims), grid=(2 * images,), in_s...]
where the time goes in v2:
time: 247 us; the launch traced here: 246 us
  Pallas kernels  236 us (96%)
  local copies, waits for them, and re-layouts  8.94 us (4%)
    pallas_call x1, Pallas kernels, run_middle(): pl.pallas_call(middle, grid_spec=pltpu.PrefetchScalarGridSpec(num_scalar_...  87.6 us
    pallas_call x1, Pallas kernels, run_opening(): pl.pallas_call(functools.partial(opening, dims), grid=(2 * images,), in_s...  75.6 us
    pallas_call x1, Pallas kernels, scatter(): pl.pallas_call(functools.partial(scatter_kernel, dims, leads), out_shape=...  41.8 us
    pallas_call x1, Pallas kernels, run_self_backward(): pl.pallas_call(self_backward, grid=(images,), in_specs=[per(tags, width),...  31.5 us
    unnamed x19, local copies, waits for them, and re-layouts  5.24 us

profile of v2, /device:TPU:0, one launch (start us, length us, event | category | flops | bytes accessed | tf_op | source)
XLA Modules:
  0.0 246.3 jit_solution(5319371472159333690)
XLA Ops:
  0.6 75.6 %opening.1 = (bf16[3,24,64,512]{3,2,1,0:T(8,128)(2,1)}, bf16[3,16,64,784]{3,2,1,0:T(8,128)(2,1)}, bf16[3,8,256,256]{3,2,1,0:T(8,128)(2,1)}, bf16[3,8,512,256]{3,...) custom-call(s32[3]{0:T(128)} %lens.3, ...), custom_call_target="tpu_custom_call" | custom-call | tf_op jit(solution)/shard_map/opening/pallas_call | solution.py:976
  76.2 0.7 slice_bitcast_fusion
  76.9 0.9 copy.25.bias_q
  77.8 87.6 %middle.1 = (bf16[3,512,512]{2,1,0:T(8,128)(2,1)}, f32[3,512,512]{2,1,0:T(8,128)}, bf16[3,8,64,512]{3,2,1,0:T(8,128)(2,1)}, bf16[3,16,64,784]{3,2,1,0:T(8,128)(2...) custom-call(s32[3]{0:T(128)} %lens.3, ...), custom_call_target="tpu_custom_call" | custom-call | tf_op jit(solution)/shard_map/middle/pallas_call | solution.py:590
  165.4 0.0 copy-start.4
  165.5 0.0 copy-start.5
  165.5 0.0 copy-start.1
  165.5 0.0 copy-start.2
  165.5 0.0 copy-start.3
  165.5 31.5 %self_backward.1 = (f32[3,512,512]{2,1,0:T(8,128)}, f32[3,784,512]{2,1,0:T(8,128)}, bf16[512,1536]{1,0:T(8,128)(2,1)}, f32[8,512]{1,0:T(8,128)}) custom-call(bf16[3,512,512]{2,1,0:T(8,128)(2,1)} %x_ref.5, bf16[3,24,64,512]{3,2,1,0:T(8,128)(2,1)} %get-tuple-element.65.qkv_ref, bf16[3,8,256,256]{3,2,1,0:T(8,128)(2,1)} %get-tuple-element.66.near_ref, ...), custom_call_target="tpu_custom_call" | custom-call | tf_op jit(solution)/shard_map/self_backward/pallas_call | solution.py:690
  197.0 0.0 copy-done.4
  197.0 0.7 slice_dynamic-update-slice_fusion
  197.7 0.0 copy-done.5
  197.8 0.1 reshape.94
  197.9 0.1 reshape.92
  198.2 0.1 pad_maximum_fusion.refs_5_
  198.2 0.0 copy-done.1
  198.2 0.0 copy-done.2
  198.2 0.0 copy-done.3
  198.2 0.0 copy-start
  198.3 1.4 copy-done
  199.7 41.8 %scatter_grads.1 = (f32[16,1536]{1,0:T(8,128)S(1)}, f32[16,1536]{1,0:T(8,128)S(1)}, f32[2,16,512]{2,1,0:T(8,128)S(1)}, f32[16,1024]{1,0:T(8,128)S(1)}, f32[32,512]{1,0:T(8,128)S(1)}, /*index=5*/f32[16,128]{1,0:T(8,128)S(1)}) custom-call(bf16[4,2,2,2,16,1536]{5,4,3,2,1,0:T(8,128)(2,1)S(1)} %bitcast.17, bf16[4,2,2,2,16,1536]{5,4,3,2,1,0:T(8,128)(2,1)} %bitcast.22, ...), custom_call_target="tpu_custom_call" | custom-call | tf_op jit(solution)/shard_map/scatter_grads/pallas_call | solution.py:310
  241.4 0.5 slice_bitcast_fusion.1
  241.9 0.6 slice.40
  242.5 0.6 copy.36
  243.2 0.6 copy.37
  243.8 0.6 copy.38
  244.4 0.6 copy.39
  245.1 0.6 copy.40
  245.7 0.6 copy.41
  (6 shorter events, 0.1 us)
Async XLA Ops:
  165.4 31.6 %copy-start.4 = (f32[16,512]{1,0:T(8,128)S(1)}, f32[16,512]{1,0:T(8,128)}, u32[]{:S(2)}) copy-start(f32[16,512]{1,0:T(8,128)} %get-tuple-element.80) | copy-start | bytes 98308
  165.5 32.3 %copy-start.5 = (f32[1,1024]{1,0:T(1,128)S(1)}, f32[1,1024]{1,0:T(1,128)}, u32[]{:S(2)}) copy-start(f32[1,1024]{1,0:T(1,128)} %get-tuple-element.82) | copy-start | bytes 12292
  165.5 32.7 %copy-start.1 = (bf16[2,512,512]{2,1,0:T(8,128)(2,1)S(1)}, bf16[2,512,512]{2,1,0:T(8,128)(2,1)}, u32[]{:S(2)}) copy-start(bf16[2,512,512]{2,1,0:T(8,128)(2,1)} %get-tuple-element.77) | copy-start | bytes 3145732
  165.5 32.7 %copy-start.2 = (bf16[512,1024]{1,0:T(8,128)(2,1)S(1)}, bf16[512,1024]{1,0:T(8,128)(2,1)}, u32[]{:S(2)}) copy-start(bf16[512,1024]{1,0:T(8,128)(2,1)} %get-tuple-element.78) | copy-start | bytes 3145732
  165.5 32.7 %copy-start.3 = (bf16[1024,512]{1,0:T(8,128)(2,1)S(1)}, bf16[1024,512]{1,0:T(8,128)(2,1)}, u32[]{:S(2)}) copy-start(bf16[1024,512]{1,0:T(8,128)(2,1)} %get-tuple-element.79) | copy-start | bytes 3145732
  198.2 1.4 copy-start

commit v3 on v2

--- a/solution.py
+++ b/solution.py
@@ -321,6 +321,7 @@
 HEADS, HEAD_DIM = 8, 64
 EPS = 1e-5
 MASKED = -1e9
+TAME = 30.0
 MIB = 2**20
 
 
@@ -452,8 +453,41 @@
     return total
 
 
-def middle(lens, x_ref, mem_ref, gout_ref, mix_one, ckv_ref, wt_q, w_proj, w_in, w_out, bias_q, vectors, b_in,
-           out_ref, g_resid, g_mix, dkv_ref, gw_cross, gw_proj, gw_in, gw_out, g_vec, g_bin,
+def cross_back(h, e, keys, values, queries, grad, mixed, inv):
+    grad = grad.astype(f32)
+    delta = jnp.sum(grad * mixed.astype(f32), 0, keepdims=True) * inv
+    grad = (grad * inv).astype(bf16)
+    dp = dot(with_ones(values), with_delta(grad, delta), 0, 0)
+    ds = e * dp.astype(bf16)
+    dv = dot(grad, e, 1, 1).astype(bf16)
+    dk = dot(queries, ds, 1, 1).astype(bf16)
+    dq = (dot(keys, ds, 1, 0) * HEAD_DIM ** -0.5).astype(bf16)
+    return dq, dk, dv
+
+
+def memory_lanes(rows):
+    cells = rows.shape[1]
+    body = cells // 128 * 128
+    total = lane_groups(rows[:, :body])
+    if body < cells:
+        total = total + jnp.concatenate([rows[:, body:], jnp.zeros((rows.shape[0], 128 - cells + body), f32)], 1)
+    return total
+
+
+def middle(held_back, lens, x_ref, mem_ref, gout_ref, mix_one, ckv_ref, wt_cross, w_proj, w_in, w_out, vectors, b_in,
+           out_ref, g_resid, g_mix, g_mem, gw_cross, gw_proj, gw_in, gw_out, g_vec, g_bin, *rest):
+    if held_back:
+        o_scale, o_e, o_q, o_inv, o_mix, o_gmix, o_one, o_two, o_cross, o_proj = rest[:10]
+        gone = rest[-1]
+        rest = rest[10:-1]
+    middle_body(held_back and (o_scale, o_e, o_q, o_inv, o_mix, o_gmix, o_one, o_two, o_cross, o_proj, gone),
+                lens, x_ref, mem_ref, gout_ref, mix_one, ckv_ref, wt_cross, w_proj, w_in, w_out, vectors, b_in,
+                out_ref, g_resid, g_mix, g_mem, gw_cross, gw_proj, gw_in, gw_out, g_vec, g_bin, *rest)
+
+
+def middle_body(held_back, lens, x_ref, mem_ref, gout_ref, mix_one, ckv_ref, wt_cross, w_proj, w_in, w_out, vectors, b_in,
+           out_ref, g_resid, g_mix, g_mem, gw_cross, gw_proj, gw_in, gw_out, g_vec, g_bin,
+           dkv_ref, cols,
            e_ref, q_ref, inv_ref, mix_two, gmix_two, dq_ref, acc_cross, acc_proj, acc_in, acc_out, acc_vec, acc_bin, acc_col,
            n_one, n_two):
     tags, width = x_ref.shape[1:]
@@ -465,6 +499,7 @@
     def _():
         for ref in (acc_cross, acc_proj, acc_in, acc_out, acc_vec, acc_bin, acc_col):
             ref[...] = jnp.zeros_like(ref)
+        cols[...] = vectors[...].T
 
     def vec(k):
         return vectors[k : k + 1, :]
@@ -472,18 +507,39 @@
     def add(k, value):
         acc_vec[k : k + 1, :] += value
 
+    if held_back:
+        scale_out, *places, gone = held_back
+        sources = (e_ref, q_ref, inv_ref, mix_two, gmix_two, n_one, n_two, acc_cross, acc_proj.at[0])
+        copies = [pltpu.make_async_copy(src, dst, gone.at[k]) for k, (src, dst) in enumerate(zip(sources, places))]
+
+    def leave(*numbers):
+        if held_back:
+            @pl.when(i == count - 1)
+            def _():
+                for number in numbers:
+                    copies[number].start()
+
+    leave(7, 8)
     mix_one_t = mix_one[0].reshape(width, tags)
     resid = x_ref[0].astype(f32) + dot(mix_one_t, w_proj[0], 0, 0) + vec(2)
     normed, scale_one = norm(resid)
     n_one[...] = normed
     one = normed * vec(10) + vec(6)
     one_low = one.astype(bf16)
-    cq = (dot(wt_q[...], one_low, 1, 1) + bias_q[...]).astype(bf16) * bf16(HEAD_DIM ** -0.5)
+    cq = (dot(wt_cross[:width], one_low, 1, 1) + cols[:, 3:4]).astype(bf16) * bf16(HEAD_DIM ** -0.5)
     q_ref[...] = cq.reshape(q_ref.shape)
-
-    def forward(h, _):
+    leave(1, 5)
+
+    keys = ckv_ref[0, :HEADS].astype(f32)
+    queries = q_ref[...].astype(f32)
+    bound = jnp.max(jnp.sum(keys * keys, 1)) * jnp.max(jnp.sum(queries * queries, 1))
+    tame = bound < TAME * TAME
+
+    def forward(shifted, h, _):
         s = dot(ckv_ref[0, h], q_ref[h], 0, 0)
-        e = jnp.exp(s - jnp.max(s, 0, keepdims=True)).astype(bf16)
+        if shifted:
+            s = s - jnp.max(s, 0, keepdims=True)
+        e = jnp.exp(s).astype(bf16)
         e_ref[h] = e
         mixed = dot(with_ones(ckv_ref[0, HEADS + h]), e, 1, 0)
         inv = 1.0 / mixed[HEAD_DIM : HEAD_DIM + 1]
@@ -491,7 +547,15 @@
         mix_two[h] = (mixed[:HEAD_DIM] * inv).astype(bf16)
         return 0
 
-    lax.fori_loop(0, HEADS, forward, 0)
+    @pl.when(tame)
+    def _():
+        lax.fori_loop(0, HEADS, functools.partial(forward, False), 0, unroll=4)
+
+    @pl.when(jnp.logical_not(tame))
+    def _():
+        lax.fori_loop(0, HEADS, functools.partial(forward, True), 0)
+
+    leave(0, 2, 3)
     mix_two_t = mix_two[...].reshape(width, tags)
     resid = one + dot(mix_two_t, w_proj[1], 0, 0) + vec(5)
     normed, scale_two = norm(resid)
@@ -529,53 +593,61 @@
     acc_proj[1] += dot(mix_two_t, g_low, 1, 0)
     gmix_two[...] = dot(w_proj[1], g_low, 1, 1).astype(bf16).reshape(gmix_two.shape)
 
-    def backward(h, _):
-        grad = gmix_two[h].astype(f32)
-        inv = inv_ref[pl.ds(h, 1), :]
-        delta = jnp.sum(grad * mix_two[h].astype(f32), 0, keepdims=True) * inv
-        grad = (grad * inv).astype(bf16)
-        e = e_ref[h]
-        dp = dot(with_ones(ckv_ref[0, HEADS + h]), with_delta(grad, delta), 0, 0)
-        ds = e * dp.astype(bf16)
-        dkv_ref[0, HEADS + h] = dot(grad, e, 1, 1).astype(bf16)
-        dkv_ref[0, h] = dot(q_ref[h], ds, 1, 1).astype(bf16)
-        dq_ref[h] = (dot(ckv_ref[0, h], ds, 1, 0) * HEAD_DIM ** -0.5).astype(bf16)
-        return 0
-
-    lax.fori_loop(0, HEADS, backward, 0)
-    dq = dq_ref[...].reshape(width, tags)
-    dkv = dkv_ref[0].reshape(2 * width, cells)
-    acc_col[0] += lane_groups(dq.astype(f32))
-    body = cells // 128 * 128
-    dv = dkv[width:].astype(f32)
-    acc_col[1] += lane_groups(dv[:, :body])
-    if body < cells:
-        acc_col[1, :, : cells - body] += dv[:, body:]
-    acc_cross[:width] += dot(dq, one_low, 1, 0)
-    acc_cross[width:] += dot(dkv, mem_ref[0], 1, 0)
-    g_one = g_two + dot(dq, wt_q[...], 0, 0)
-    add(10, column_sums(g_one * n_one[...]))
-    add(6, column_sums(g_one))
-    g_one = norm_back(g_one, n_one[...], scale_one, vec(10))
-    add(2, column_sums(g_one))
-    g_resid[0] = g_one
-    g_low = g_one.astype(bf16)
-    acc_proj[0] += dot(mix_one_t, g_low, 1, 0)
-    g_mix[0] = dot(w_proj[0], g_low, 1, 1).astype(bf16).reshape(g_mix.shape[1:])
+    def rest_of_image():
+        def backward(h, _):
+            dq_ref[h], dkv_ref[h], dkv_ref[HEADS + h] = cross_back(
+                h, e_ref[h], ckv_ref[0, h], ckv_ref[0, HEADS + h], q_ref[h], gmix_two[h], mix_two[h], inv_ref[pl.ds(h, 1), :])
+            return 0
+
+        lax.fori_loop(0, HEADS, backward, 0, unroll=4)
+        dq = dq_ref[...].reshape(width, tags)
+        dkv = dkv_ref[...].reshape(2 * width, cells)
+        acc_col[0] += lane_groups(dq.astype(f32))
+        acc_col[1] += memory_lanes(dkv[width:].astype(f32))
+        acc_cross[:width] += dot(dq, one_low, 1, 0)
+        acc_cross[width:] += dot(dkv, mem_ref[0], 1, 0)
+        g_mem[0] = dot(dkv, wt_cross[width:], 0, 0)
+        g_one = g_two + dot(dq, wt_cross[:width], 0, 0)
+        add(10, column_sums(g_one * n_one[...]))
+        add(6, column_sums(g_one))
+        g_one = norm_back(g_one, n_one[...], scale_one, vec(10))
+        add(2, column_sums(g_one))
+        g_resid[0] = g_one
+        g_low = g_one.astype(bf16)
+        acc_proj[0] += dot(mix_one_t, g_low, 1, 0)
+        g_mix[0] = dot(w_proj[0], g_low, 1, 1).astype(bf16).reshape(g_mix.shape[1:])
+
+    if held_back:
+        pl.when(i < count - 1)(rest_of_image)
+
+        @pl.when(i == count - 1)
+        def _():
+            n_two[...] = g_two
+            scale_out[...] = scale_one
+
+        leave(4, 6)
+    else:
+        rest_of_image()
 
     @pl.when(i == count - 1)
     def _():
-        gw_cross[...] = acc_cross[...].astype(bf16).T
-        gw_proj[...] = acc_proj[...].astype(bf16)
+        if held_back:
+            gw_proj[...] = acc_proj[1].astype(bf16)
+        else:
+            gw_cross[...] = acc_cross[...].astype(bf16).T
+            gw_proj[...] = acc_proj[...].astype(bf16)
         gw_in[...] = acc_in[...].astype(bf16)
         gw_out[...] = acc_out[...].astype(bf16)
         add(3, column_sums(acc_col[0].T))
         add(4, column_sums(acc_col[1].T))
         g_vec[...] = acc_vec[...]
         g_bin[...] = acc_bin[...]
-
-
-def run_middle(lens, x, mem, gout, mix_one, ckv, wt_cross, w_proj, w_in, w_out, bias_q, vectors, b_in):
+        if held_back:
+            for copy in copies:
+                copy.wait()
+
+
+def run_middle(lens, x, mem, gout, mix_one, ckv, wt_cross, w_proj, w_in, w_out, vectors, b_in, held_back=False):
     images, tags, width = x.shape
     cells = mem.shape[1]
     hidden = w_in.shape[1]
@@ -585,52 +657,72 @@
         return pl.BlockSpec((1,) + shape, lambda i, n: (i,) + (0,) * len(shape))
 
     def one(*shape):
+        return pl.BlockSpec(shape, lambda i, n: (0,) * len(shape), pipeline_mode=pl.Buffered(1))
+
+    def out(*shape):
         return pl.BlockSpec(shape, lambda i, n: (0,) * len(shape))
 
+    def early(*shape):
+        return pl.BlockSpec((1,) + shape, lambda i, n: (jnp.minimum(i, images - 2),) + (0,) * len(shape)) if held_back else per(*shape)
+
+    done = images - 1 if held_back else images
+    out_specs = [
+        per(tags, width), early(tags, width), early(HEADS, HEAD_DIM, tags), early(cells, width),
+        out(width, 3 * width), out(2, width, width), out(width, hidden), out(hidden, width), out(16, width), out(1, hidden),
+    ]
+    out_shape = [
+        sds((images, tags, width), bf16), sds((done, tags, width), f32), sds((done, HEADS, HEAD_DIM, tags), bf16),
+        sds((images, cells, width), f32),
+        sds((width, 3 * width), bf16), sds((2, width, width), bf16), sds((width, hidden), bf16), sds((hidden, width), bf16),
+        sds((16, width), f32), sds((1, hidden), f32),
+    ]
+    scratch = [
+        pltpu.VMEM((2 * HEADS, HEAD_DIM, cells), bf16),
+        pltpu.VMEM((width, 16), f32),
+        pltpu.VMEM((HEADS, cells, tags), bf16),
+        pltpu.VMEM((HEADS, HEAD_DIM, tags), bf16),
+        pltpu.VMEM((HEADS, tags), f32),
+        pltpu.VMEM((HEADS, HEAD_DIM, tags), bf16),
+        pltpu.VMEM((HEADS, HEAD_DIM, tags), bf16),
+        pltpu.VMEM((HEADS, HEAD_DIM, tags), bf16),
+        pltpu.VMEM((3 * width, width), f32),
+        pltpu.VMEM((2, width, width), f32),
+        pltpu.VMEM((width, hidden), f32),
+        pltpu.VMEM((hidden, width), f32),
+        pltpu.VMEM((16, width), f32),
+        pltpu.VMEM((1, hidden), f32),
+        pltpu.VMEM((2, width, 128), f32),
+        pltpu.VMEM((tags, width), f32),
+        pltpu.VMEM((tags, width), f32),
+    ]
+    if held_back:
+        out_specs[4], out_shape[4] = out(8, 128), sds((8, 128), bf16)
+        out_specs[5], out_shape[5] = out(width, width), sds((width, width), bf16)
+        kept = [((HEADS, cells, tags), bf16), ((HEADS, HEAD_DIM, tags), bf16), ((HEADS, tags), f32), ((HEADS, HEAD_DIM, tags), bf16),
+                ((HEADS, HEAD_DIM, tags), bf16), ((tags, width), f32), ((tags, width), f32), ((3 * width, width), f32), ((width, width), f32)]
+        out_specs += [out(tags, 1)] + [pl.BlockSpec(memory_space=pl.ANY)] * len(kept)
+        out_shape += [sds((tags, 1), f32)] + [sds(*k) for k in kept]
+        scratch.append(pltpu.SemaphoreType.DMA((len(kept),)))
     return pl.pallas_call(
-        middle,
+        functools.partial(middle, held_back),
         grid_spec=pltpu.PrefetchScalarGridSpec(
             num_scalar_prefetch=1,
             grid=(images,),
             in_specs=[
                 per(tags, width), per(cells, width), per(tags, width), per(HEADS, HEAD_DIM, tags), per(2 * HEADS, HEAD_DIM, cells),
-                one(width, width), one(2, width, width), one(width, hidden), one(hidden, width), one(width, 1), one(16, width), one(1, hidden),
+                one(3 * width, width), one(2, width, width), one(width, hidden), one(hidden, width), one(16, width), one(1, hidden),
             ],
-            out_specs=[
-                per(tags, width), per(tags, width), per(HEADS, HEAD_DIM, tags), per(2 * HEADS, HEAD_DIM, cells),
-                one(width, 3 * width), one(2, width, width), one(width, hidden), one(hidden, width), one(16, width), one(1, hidden),
-            ],
-            scratch_shapes=[
-                pltpu.VMEM((HEADS, cells, tags), bf16),
-                pltpu.VMEM((HEADS, HEAD_DIM, tags), bf16),
-                pltpu.VMEM((HEADS, tags), f32),
-                pltpu.VMEM((HEADS, HEAD_DIM, tags), bf16),
-                pltpu.VMEM((HEADS, HEAD_DIM, tags), bf16),
-                pltpu.VMEM((HEADS, HEAD_DIM, tags), bf16),
-                pltpu.VMEM((3 * width, width), f32),
-                pltpu.VMEM((2, width, width), f32),
-                pltpu.VMEM((width, hidden), f32),
-                pltpu.VMEM((hidden, width), f32),
-                pltpu.VMEM((16, width), f32),
-                pltpu.VMEM((1, hidden), f32),
-                pltpu.VMEM((2, width, 128), f32),
-                pltpu.VMEM((tags, width), f32),
-                pltpu.VMEM((tags, width), f32),
-            ],
+            out_specs=out_specs,
+            scratch_shapes=scratch,
         ),
-        out_shape=[
-            sds((images, tags, width), bf16), sds((images, tags, width), f32), sds((images, HEADS, HEAD_DIM, tags), bf16),
-            sds((images, 2 * HEADS, HEAD_DIM, cells), bf16),
-            sds((width, 3 * width), bf16), sds((2, width, width), bf16), sds((width, hidden), bf16), sds((hidden, width), bf16),
-            sds((16, width), f32), sds((1, hidden), f32),
-        ],
+        out_shape=out_shape,
         compiler_params=pltpu.CompilerParams(vmem_limit_bytes=62 * MIB),
         name="middle",
-    )(lens, x, mem, gout, mix_one, ckv, wt_cross, w_proj, w_in, w_out, bias_q, vectors, b_in)
-
-
-def self_backward(x_ref, qkv_ref, near_ref, far_ref, inv_ref, mix_ref, gmix_ref, g_resid, dkv_ref, wt_self, wt_cross,
-                  g_tags, g_mem, gw_self, g_col, d_ref, acc, acc_col):
+    )(lens, x, mem, gout, mix_one, ckv, wt_cross, w_proj, w_in, w_out, vectors, b_in)
+
+
+def self_backward(x_ref, qkv_ref, near_ref, far_ref, inv_ref, mix_ref, gmix_ref, g_resid, wt_self,
+                  g_tags, gw_self, g_col, d_ref, acc, acc_col):
     tags, width = x_ref.shape[1:]
     half = tags // 2
     i = pl.program_id(0)
@@ -666,7 +758,6 @@
     acc_col[1] += lane_groups(d[2 * width :].astype(f32))
     acc[...] += dot(d, x_ref[0], 1, 0)
     g_tags[0] = g_resid[0] + dot(d, wt_self[...], 0, 0)
-    g_mem[0] = dot(dkv_ref[0].reshape(2 * width, -1), wt_cross[width:], 0, 0)
 
     @pl.when(i == pl.num_programs(0) - 1)
     def _():
@@ -675,9 +766,8 @@
         g_col[1:2] = column_sums(acc_col[1].T)
 
 
-def run_self_backward(x, qkv, near, far, inv, mix, gmix, g_resid, dkv, wt_self, wt_cross):
+def run_self_backward(x, qkv, near, far, inv, mix, gmix, g_resid, wt_self):
     images, tags, width = x.shape
-    cells = dkv.shape[3]
     half = tags // 2
     sds = jax.ShapeDtypeStruct
 
@@ -691,14 +781,14 @@
         self_backward,
         grid=(images,),
         in_specs=[per(tags, width), per(3 * HEADS, HEAD_DIM, tags), per(HEADS, half, half), per(HEADS, tags, half), per(HEADS, tags),
-                  per(HEADS, HEAD_DIM, tags), per(HEADS, HEAD_DIM, tags), per(tags, width), per(2 * HEADS, HEAD_DIM, cells),
-                  one(3 * width, width), one(3 * width, width)],
-        out_specs=[per(tags, width), per(cells, width), one(width, 3 * width), one(8, width)],
-        out_shape=[sds((images, tags, width), f32), sds((images, cells, width), f32), sds((width, 3 * width), bf16), sds((8, width), f32)],
+                  per(HEADS, HEAD_DIM, tags), per(HEADS, HEAD_DIM, tags), per(tags, width),
+                  one(3 * width, width)],
+        out_specs=[per(tags, width), one(width, 3 * width), one(8, width)],
+        out_shape=[sds((images, tags, width), f32), sds((width, 3 * width), bf16), sds((8, width), f32)],
         scratch_shapes=[pltpu.VMEM((3 * HEADS, HEAD_DIM, tags), bf16), pltpu.VMEM((3 * width, width), f32), pltpu.VMEM((2, width, 128), f32)],
         compiler_params=pltpu.CompilerParams(vmem_limit_bytes=60 * MIB),
         name="self_backward",
-    )(x, qkv, near, far, inv, mix, gmix, g_resid, dkv, wt_self, wt_cross)
+    )(x, qkv, near, far, inv, mix, gmix, g_resid, wt_self)
 
 
 def layer(lens, x, mem, gout, w_self, w_cross, w_proj, w_in, w_out, vectors, b_in):
@@ -706,16 +796,32 @@
     zero = jnp.zeros((width,), f32)
     bias_qkv = jnp.concatenate([vectors[0], zero, vectors[1]])[:, None]
     bias_kv = jnp.concatenate([zero, vectors[4]])[:, None]
-    bias_q = vectors[3][:, None]
     qkv, ckv, near, far, inv, mix, wt_self, wt_cross = run_self_forward(lens, x, mem, w_self, w_cross, bias_qkv, bias_kv)
-    out, g_resid, gmix, dkv, gw_cross, gw_proj, gw_in, gw_out, g_vec, g_bin = run_middle(
-        lens, x, mem, gout, mix, ckv, wt_cross, w_proj, w_in, w_out, bias_q, vectors, b_in)
-    g_tags, g_mem, gw_self, g_col = run_self_backward(x, qkv, near, far, inv, mix, gmix, g_resid, dkv, wt_self, wt_cross)
+    out, g_resid, gmix, g_mem, gw_cross, gw_proj, gw_in, gw_out, g_vec, g_bin = run_middle(
+        lens, x, mem, gout, mix, ckv, wt_cross, w_proj, w_in, w_out, vectors, b_in)
+    g_tags, gw_self, g_col = run_self_backward(x, qkv, near, far, inv, mix, gmix, g_resid, wt_self)
     g_vec = g_vec.at[0:2].set(g_col[0:2])
     return out, g_tags, g_mem, gw_self, gw_cross, gw_proj, gw_in, gw_out, g_vec, g_bin
 
 
 ALL = slice(None)
+
+
+SMALL, SELF, PROJ, CROSS, IN, OUT = range(6)
+PLAN = (
+    ((SMALL, 0), (SELF, 0), (PROJ, 0), (CROSS, 0), (IN, 0), (OUT, 0),
+     (SMALL, 1), (SELF, 1), (SMALL, 2), (PROJ, 1), (SELF, 2), (SMALL, 3), (CROSS, 1), (PROJ, 2), (IN, 1), (SELF, 3), (CROSS, 2), (OUT, 1),
+     (PROJ, 3), (SMALL, 4), (SELF, 4)),
+    ((IN, 2),),
+    ((OUT, 2),),
+    ((CROSS, 3),),
+    ((IN, 3),),
+    ((OUT, 3),),
+    (),
+    ((CROSS, 4),),
+    ((PROJ, 4), (IN, 4), (OUT, 4)),
+)
+MEANTIME = {2: (0, 2), 3: (1, 0), 4: (1, 3), 5: (2, 2)}
 
 
 class Gathering:
@@ -823,18 +929,28 @@
 
 
 def opening(dims, lens, x_ref, mem_ref, b_ref, g_ref, h_ref, s_cross, s_self, s_proj, s_in, s_out,
-            qkv_ref, ckv_ref, near_ref, far_ref, inv_ref, mix_ref, wt_self, wt_cross, vec_ref, bin_ref, o_proj, o_in, o_out,
-            small, small_low, h_small, h_kv, h_self, h_q, cols, local, send, recv):
+            qkv_ref, ckv_ref, near_ref, far_ref, inv_ref, mix_ref, out_self, out_cross, vec_ref, bin_ref, o_proj, o_in, o_out,
+            small, small_low, h_small, h_self, h_cross, wt_self, wt_cross, cols, near_a, far_a, near_b, far_b, gone, local, send, recv):
     width = x_ref.shape[2]
     tags = x_ref.shape[1]
     half = tags // 2
     step = pl.program_id(0)
     images = pl.num_programs(0) // 2
     me = place(dims)
-    s_kv, s_q = s_cross.at[:, width:], s_cross.at[:, :width]
-    pairs = ((small_low, h_small, 0), (s_kv, h_kv, 0), (s_self, h_self, 0), (s_q, h_q, 0), (s_proj, o_proj, 1), (s_in, o_in, 0), (s_out, o_out, 0))
+    pairs = ((small_low, h_small, 0), (s_self, h_self, 0), (s_proj, o_proj, 1), (s_cross, h_cross, 0), (s_in, o_in, 0), (s_out, o_out, 0))
     gs = [Gathering(dims, me, shard, held, lead, (local.at[k], send.at[k], recv.at[k])) for k, (shard, held, lead) in enumerate(pairs)]
-    g_small, g_kv, g_self, g_q, g_proj, g_in, g_out = gs
+    keep_self = pltpu.make_async_copy(wt_self, out_self, gone.at[0])
+    keep_cross = pltpu.make_async_copy(wt_cross, out_cross, gone.at[1])
+
+    def play(slot):
+        for item, stage in PLAN[slot]:
+            item = gs[item]
+            item.begin() if stage == 0 else item.finish() if stage == 4 else item.advance(stage)
+
+    def slot_at(number, slot):
+        @pl.when(step == number)
+        def _():
+            play(slot)
 
     @pl.when(step == 0)
     def _():
@@ -844,108 +960,85 @@
         small[13:14, : h_ref.shape[1]] = h_ref[...].astype(f32)
         small_low[...] = small[...].astype(bf16)
         greet(dims, me)
-        g_small.begin()
-        g_kv.begin()
-        g_self.begin()
-        g_small.advance(1)
-        g_kv.advance(1)
-        g_q.begin()
-        g_proj.begin()
-        g_small.advance(2)
-        g_kv.advance(2)
-        g_self.advance(1)
-        g_small.advance(3)
-        g_kv.advance(3)
-        g_in.begin()
-        g_self.advance(2)
-        g_out.begin()
-        g_small.finish()
+        play(0)
         vectors = spread(h_small[...].reshape(-1, 128), b_ref.shape[1], width, 16)
         vec_ref[...] = vectors
         bin_ref[...] = spread(h_small[...].reshape(-1, 128), h_ref.shape[1], bin_ref.shape[1], 16)[13:14]
         cols[...] = vectors.T
-        g_kv.finish()
-        wt_cross[width:] = h_kv[...].reshape(width, 2 * width).T
+        wt_self[...] = h_self[...].reshape(width, 3 * width).T
+        keep_self.start()
 
     @pl.when(step < images)
-    def _():
-        kv = dot(wt_cross[width:], mem_ref[0], 1, 1)
-        heads = ckv_ref.shape[1] // 2
-        ckv_ref[0, :heads] = kv[:width].astype(bf16).reshape(heads, HEAD_DIM, -1)
-        ckv_ref[0, heads:] = (kv[width:] + cols[:, 4:5]).astype(bf16).reshape(heads, HEAD_DIM, -1)
-
-    @pl.when(step == 0)
-    def _():
-        g_self.advance(3)
-        g_q.advance(1)
-        g_proj.advance(1)
-
-    @pl.when(step == 1)
-    def _():
-        g_q.advance(2)
-        g_proj.advance(2)
-        g_in.advance(1)
-
-    @pl.when(step == 2)
-    def _():
-        g_q.advance(3)
-        g_proj.advance(3)
-        g_in.advance(2)
-        g_out.advance(1)
-
-    @pl.when(step == images)
-    def _():
-        g_self.finish()
-        wt_self[...] = h_self[...].reshape(width, 3 * width).T
-
-    @pl.when(step >= images)
     def _():
         qkv = dot(wt_self[...], x_ref[0], 1, 1)
         qkv_ref[0, :HEADS] = ((qkv[:width] + cols[:, 0:1]).astype(bf16) * bf16(HEAD_DIM ** -0.5)).reshape(HEADS, HEAD_DIM, tags)
         qkv_ref[0, HEADS : 2 * HEADS] = qkv[width : 2 * width].astype(bf16).reshape(HEADS, HEAD_DIM, tags)
         qkv_ref[0, 2 * HEADS :] = (qkv[2 * width :] + cols[:, 1:2]).astype(bf16).reshape(HEADS, HEAD_DIM, tags)
 
-    @pl.when(step == images)
-    def _():
-        g_in.advance(3)
-        g_out.advance(2)
-
-    def head(h, _):
-        qt, kt, vt = qkv_ref[0, h], qkv_ref[0, HEADS + h], with_ones(qkv_ref[0, 2 * HEADS + h])
-        last = lens[jnp.maximum(step - images, 0)] - 1
-
-        def part(keys, first, out):
+    last = lens[jnp.minimum(step, images - 1)] - 1
+
+    def scores(h, near, far):
+        qt, kt = qkv_ref[0, h], qkv_ref[0, HEADS + h]
+
+        def part(keys, first, held):
             s = dot(kt[:, :keys], qt[:, first : first + half], 0, 0)
             key_at = lax.broadcasted_iota(jnp.int32, (keys, half), 0)
             query_at = lax.broadcasted_iota(jnp.int32, (1, half), 1) + first
             s = jnp.where(key_at <= jnp.minimum(query_at, last), s, MASKED)
-            e = jnp.exp(s - jnp.max(s, 0, keepdims=True)).astype(bf16)
+            held[...] = s
+            return jnp.max(s, 0, keepdims=True)
+
+        return part(half, 0, near), part(tags, half, far)
+
+    def mix(h, near, far, tops):
+        vt = with_ones(qkv_ref[0, 2 * HEADS + h])
+
+        def part(keys, first, held, top, out):
+            e = jnp.exp(held[...] - top).astype(bf16)
             out[0, h] = e
             mixed = dot(vt[:, :keys], e, 1, 0)
             inv = 1.0 / mixed[HEAD_DIM : HEAD_DIM + 1]
             inv_ref[0, pl.ds(h, 1), first : first + half] = inv
             mix_ref[0, h, :, first : first + half] = (mixed[:HEAD_DIM] * inv).astype(bf16)
 
-        part(half, 0, near_ref)
-        part(tags, half, far_ref)
-        return 0
+        part(half, 0, near, tops[0], near_ref)
+        part(tags, half, far, tops[1], far_ref)
+
+    def pair(p, tops):
+        h = 2 * p
+        for slot, (image, number) in MEANTIME.items():
+            pl.when(jnp.logical_and(step == image, p == number))(functools.partial(play, slot))
+        following = scores(h + 1, near_b, far_b)
+        mix(h, near_a, far_a, tops)
+        tops = scores(jnp.minimum(h + 2, HEADS - 1), near_a, far_a)
+        mix(h + 1, near_b, far_b, following)
+        return tops
+
+    slot_at(0, 1)
+
+    @pl.when(step < images)
+    def _():
+        lax.fori_loop(0, HEADS // 2, pair, scores(0, near_a, far_a))
+
+    @pl.when(step == images)
+    def _():
+        play(7)
+        wt_cross[...] = h_cross[...].reshape(width, 3 * width).T
+        keep_cross.start()
 
     @pl.when(step >= images)
     def _():
-        lax.fori_loop(0, HEADS, head, 0)
-
-    @pl.when(step == images)
-    def _():
-        g_out.advance(3)
+        kv = dot(wt_cross[width:], mem_ref[0], 1, 1)
+        ckv_ref[0, :HEADS] = kv[:width].astype(bf16).reshape(HEADS, HEAD_DIM, -1)
+        ckv_ref[0, HEADS:] = (kv[width:] + cols[:, 4:5]).astype(bf16).reshape(HEADS, HEAD_DIM, -1)
 
     @pl.when(step == 2 * images - 1)
     def _():
-        g_q.finish()
-        wt_cross[:width] = h_q[...].reshape(width, width).T
-        for g in (g_proj, g_in, g_out):
-            g.finish()
+        play(8)
         for g in gs:
             g.drain()
+        keep_self.wait()
+        keep_cross.wait()
 
 
 def run_opening(dims, lens, x, mem, biases, gains, b_in, shards):
@@ -971,16 +1064,16 @@
     rows = s_cross.shape[0]
     cell = dims + (2, rows)
     anywhere = pl.BlockSpec(memory_space=pl.ANY)
-    n = len(shards) + 2
+    n = len(shards) + 1
     slots = gather_slots(dims)
     return pl.pallas_call(
         functools.partial(opening, dims),
         grid=(2 * images,),
-        in_specs=[pl.BlockSpec(memory_space=pltpu.SMEM), late(tags, width), early(cells, width), one(*biases.shape), one(*gains.shape), one(*b_in.shape)]
+        in_specs=[pl.BlockSpec(memory_space=pltpu.SMEM), early(tags, width), late(cells, width), one(*biases.shape), one(*gains.shape), one(*b_in.shape)]
         + [anywhere] * len(shards),
         out_specs=[
-            late(3 * HEADS, HEAD_DIM, tags), early(2 * HEADS, HEAD_DIM, cells), late(HEADS, half, half), late(HEADS, tags, half),
-            late(HEADS, tags), late(HEADS, HEAD_DIM, tags), one(3 * width, width), one(3 * width, width), one(16, width), one(1, hidden),
+            early(3 * HEADS, HEAD_DIM, tags), late(2 * HEADS, HEAD_DIM, cells), early(HEADS, half, half), early(HEADS, tags, half),
+            early(HEADS, tags), early(HEADS, HEAD_DIM, tags), anywhere, anywhere, one(16, width), one(1, hidden),
             anywhere, anywhere, anywhere,
         ],
         out_shape=[
@@ -1000,8 +1093,10 @@
         ],
         scratch_shapes=[
             pltpu.VMEM((16, 128), f32), pltpu.VMEM((16, 128), bf16), pltpu.VMEM(dims + (2, 16, 128), bf16),
-            pltpu.VMEM(cell + (2 * width,), bf16), pltpu.VMEM(cell + (3 * width,), bf16), pltpu.VMEM(cell + (width,), bf16),
-            pltpu.VMEM((width, 16), f32),
+            pltpu.VMEM(cell + (3 * width,), bf16), pltpu.VMEM(cell + (3 * width,), bf16),
+            pltpu.VMEM((3 * width, width), bf16), pltpu.VMEM((3 * width, width), bf16),
+            pltpu.VMEM((width, 16), f32), pltpu.VMEM((half, half), f32), pltpu.VMEM((tags, half), f32), pltpu.VMEM((half, half), f32), pltpu.VMEM((tags, half), f32),
+            pltpu.SemaphoreType.DMA((2,)),
             pltpu.SemaphoreType.DMA((n,)), pltpu.SemaphoreType.DMA((n, slots)), pltpu.SemaphoreType.DMA((n, slots)),
         ],
         compiler_params=pltpu.CompilerParams(collective_id=0, has_side_effects=True, vmem_limit_bytes=58 * MIB),
@@ -1009,6 +1104,463 @@
     )(lens, x, mem, biases, gains, b_in, *shards)
 
 
+class Scattering:
+    def __init__(self, dims, me, grads, out, lead, held, sems):
+        self.dims, self.me, self.grads, self.out, self.lead = dims, me, grads, out, lead
+        self.pair, self.by_inner, self.by_across, self.by_outer, self.last = held
+        self.send, self.recv = sems
+
+    def at(self, *index):
+        return (ALL,) * self.lead + index
+
+    def remote(self, slot, src, dst, peer):
+        return pltpu.make_async_remote_copy(
+            src_ref=src, dst_ref=dst, send_sem=self.send.at[slot], recv_sem=self.recv.at[slot],
+            device_id=device(self.dims, *peer), device_id_type=MESH)
+
+    def swap(self):
+        a, b, x, c = self.me
+        return [self.remote(0, self.grads.at[self.at(ALL, ALL, ALL, 1 - c)], self.pair, (a, b, x, 1 - c))]
+
+    def along_inner(self, core):
+        a, b, x, c = self.me
+        inner = self.dims[1]
+        res = []
+        for k in range(1, inner):
+            peer = lax.rem(b + k, inner)
+            src = self.pair.at[self.at(ALL, peer)] if core == 0 else self.by_across.at[0].at[self.at(ALL, peer)]
+            dst = self.by_inner.at[k - 1] if core == 0 else self.by_outer.at[k - 1]
+            res.append(self.remote(k, src, dst, (a, peer, x, c)))
+        return res
+
+    def along_across(self, core):
+        a, b, x, c = self.me
+        _, inner, across = self.dims
+        res = []
+        for k in range(1, across):
+            peer = lax.rem(x + k, across)
+            src = self.pair.at[self.at(ALL, ALL, peer)] if core == 1 else self.by_inner.at[0].at[self.at(ALL, peer)]
+            dst = self.by_across.at[k - 1] if core == 1 else self.by_outer.at[k - 1]
+            res.append(self.remote(inner - 1 + k, src, dst, (a, b, peer, c)))
+        return res
+
+    def second(self, core):
+        return self.along_inner(core) if core == 0 else self.along_across(core)
+
+    def third(self, core):
+        return self.along_across(core) if core == 0 else self.along_inner(core)
+
+    def along_outer(self):
+        a, b, x, c = self.me
+        outer, inner, across = self.dims
+        return [
+            self.remote(inner + across - 2 + k, self.by_outer.at[0].at[self.at(lax.rem(a + k, outer))], self.last.at[k - 1],
+                        (lax.rem(a + k, outer), b, x, c))
+            for k in range(1, outer)
+        ]
+
+    def begin(self):
+        for copy in self.swap():
+            copy.start()
+
+    def advance(self, stage):
+        a, b, x, c = self.me
+        _, inner, across = self.dims
+
+        def up(value):
+            return value.astype(f32)
+
+        def act(core):
+            for copy in (self.swap(), self.second(core), self.third(core), self.along_outer())[stage - 1]:
+                copy.wait_recv()
+            if stage == 1:
+                self.pair[...] = (up(self.grads[self.at(ALL, ALL, ALL, c)]) + up(self.pair[...])).astype(bf16)
+                following = self.second(core)
+            elif stage == 2:
+                held = self.by_inner if core == 0 else self.by_across
+                total = up(self.pair[self.at(ALL, b) if core == 0 else self.at(ALL, ALL, x)])
+                for k in range((inner if core == 0 else across) - 1):
+                    total = total + up(held[k])
+                held[0] = total.astype(bf16)
+                following = self.third(core)
+            elif stage == 3:
+                held = self.by_inner if core == 0 else self.by_across
+                total = up(held[(0,) + self.at(ALL, x if core == 0 else b)])
+                for k in range((across if core == 0 else inner) - 1):
+                    total = total + up(self.by_outer[k])
+                self.by_outer[0] = total.astype(bf16)
+                following = self.along_outer()
+            else:
+                total = up(self.by_outer[(0,) + self.at(a)])
+                for k in range(self.dims[0] - 1):
+                    total = total + up(self.last[k])
+                self.out[...] = total
+                following = []
+            for copy in following:
+                copy.start()
+
+        for core in (0, 1):
+            pl.when(c == core)(functools.partial(act, core))
+
+    def drain(self):
+        def act(core):
+            for copy in self.swap() + self.second(core) + self.third(core) + self.along_outer():
+                copy.wait_send()
+
+        for core in (0, 1):
+            pl.when(self.me[3] == core)(functools.partial(act, core))
+
+
+def scatter_slots(dims):
+    return dims[0] + dims[1] + dims[2] - 2
+
+
+def scatter_space(dims, lead, tail):
+    outer, inner, across = dims
+    return [
+        lead + (outer, inner, across) + tail,
+        (inner - 1,) + lead + (outer, across) + tail,
+        (across - 1,) + lead + (outer, inner) + tail,
+        (max(inner, across) - 1,) + lead + (outer,) + tail,
+        (outer - 1,) + lead + tail,
+    ]
+
+
+def collect(rows, row_lanes, devices):
+    width = rows.shape[1]
+    many = jnp.broadcast_to(rows[None], (devices, 16, width)).reshape(devices * 16, width)
+    owner = lax.broadcasted_iota(jnp.int32, many.shape, 0) // 16
+    at = lax.broadcasted_iota(jnp.int32, many.shape, 1)
+    many = jnp.where(at // row_lanes == owner, many, 0.0).astype(bf16)
+    lane = lax.broadcasted_iota(jnp.int32, (128, width), 0)
+    at = lax.broadcasted_iota(jnp.int32, (128, width), 1)
+    pick = jnp.where(lax.rem(at, row_lanes) == lane, 1.0, 0.0).astype(bf16)
+    return dot(many, pick, 1, 1)
+
+
+G_OUT, G_IN, G_ONE, G_CROSS, G_ZERO, G_HALF, G_REST, G_SMALL = range(8)
+EVENTS = {
+    (0, 0): ((G_OUT, 0), (G_IN, 0), (G_ONE, 0)),
+    (0, 3): ((G_OUT, 1),),
+    (0, 4): ((G_IN, 1), (G_ONE, 1)),
+    (0, 6): ((G_OUT, 2), (G_CROSS, 0)),
+    (0, 7): ((G_IN, 2), (G_ZERO, 0)),
+    (1, 1): ((G_ONE, 2), (G_OUT, 3)),
+    (2, 1): ((G_IN, 3), (G_CROSS, 1), (G_ONE, 3), (G_ZERO, 1)),
+    (3, 1): ((G_HALF, 0), (G_OUT, 4)),
+    (4, 1): ((G_IN, 4), (G_ONE, 4)),
+    (5, 1): ((G_HALF, 1), (G_CROSS, 2)),
+    (6, 1): ((G_REST, 0), (G_SMALL, 0), (G_ZERO, 2)),
+    (7, 1): ((G_HALF, 2),),
+    (8, 1): ((G_CROSS, 3), (G_ZERO, 3), (G_REST, 1), (G_SMALL, 1)),
+    (9, 0): ((G_HALF, 3),),
+    (9, 1): ((G_REST, 2), (G_SMALL, 2), (G_CROSS, 4), (G_ZERO, 4), (G_HALF, 4), (G_REST, 3), (G_SMALL, 3), (G_REST, 4), (G_SMALL, 4)),
+}
+
+
+def closing(dims, x_ref, qkv_ref, near_ref, far_ref, inv_ref, mix_ref, gmix_ref, gres_ref, ckv_ref, q_ref, inv_two, mix_two, gmix_two,
+            vectors, g_vec, g_bin, scale_one, low_out, low_in, low_one,
+            e_any, mix_any, two_any, one_any, wc_any, mem_any, ac_any, ap_any, wp_any, ws_any,
+            g_tags, sh_out, sh_in, sh_one, sh_cross, sh_zero, sh_half, sh_rest, sh_small, dkv_ref,
+            e_ref, mix_one, g_two, n_one, wt_cross, mem_ref, acc_cross, acc_zero, w_zero, wt_self,
+            dq_ref, gmix_last, gres_last, gmix_now, acc, add_vec, acc_col, low_cross, low_zero, low_half, low_rest, low_small, head_sem, in_sem, *rest):
+    tags, width = x_ref.shape[1:]
+    cells = mem_ref.shape[0]
+    half = tags // 2
+    some = HEADS // 2
+    step = pl.program_id(0)
+    images = pl.num_programs(0) // 3
+    me = place(dims)
+    devices = dims[0] * dims[1] * dims[2] * 2
+    held, (send, recv) = rest[:-2], rest[-2:]
+    pairs = ((low_out, sh_out), (low_in, sh_in), (low_one, sh_one), (low_cross, sh_cross), (low_zero, sh_zero), (low_half, sh_half),
+             (low_rest, sh_rest), (low_small, sh_small))
+    every = [Scattering(dims, me, grads, out, 0, held[5 * k : 5 * k + 5], (send.at[k], recv.at[k])) for k, (grads, out) in enumerate(pairs)]
+    fetches = [
+        pltpu.make_async_copy(src, dst, in_sem.at[k])
+        for k, (src, dst) in enumerate((
+            (mix_any.at[images - 1], mix_one), (two_any, g_two), (one_any, n_one), (wc_any, wt_cross), (mem_any.at[images - 1], mem_ref),
+            (ac_any, acc_cross), (ap_any, acc_zero), (wp_any.at[0], w_zero), (ws_any, wt_self)))
+    ]
+
+    def e_rows(h):
+        return e_ref.at[pl.ds(pl.multiple_of(h * cells, 16), cells)]
+
+    def e_fetch(h):
+        return pltpu.make_async_copy(e_any.at[h], e_rows(h), head_sem.at[h])
+
+    def play(number, where):
+        for item, stage in EVENTS.get((number, where), ()):
+            item = every[item]
+            item.begin() if stage == 0 else item.advance(stage)
+
+    def events(where):
+        for number in sorted(number for number, at in EVENTS if at == where and number > 0):
+            pl.when(step == number)(functools.partial(play, number, where))
+
+    def vec(k):
+        return vectors[k : k + 1, :]
+
+    @pl.when(step == 0)
+    def _():
+        for h in range(HEADS):
+            e_fetch(h).start()
+        for fetch in fetches:
+            fetch.start()
+        acc_col[...] = jnp.zeros_like(acc_col)
+        greet(dims, me)
+        play(0, 0)
+
+        def pair(p, _):
+            for k in range(1, 4):
+                pl.when(p == k)(functools.partial(play, 0, k + 1))
+            for h in (2 * p, 2 * p + 1):
+                e_fetch(h).wait()
+            for h in (2 * p, 2 * p + 1):
+                dq_ref[h], dkv_ref[h], dkv_ref[HEADS + h] = cross_back(
+                    h, e_rows(h)[...], ckv_ref[0, h], ckv_ref[0, HEADS + h], q_ref[h], gmix_two[h], mix_two[h], inv_two[pl.ds(h, 1), :])
+            return 0
+
+        lax.fori_loop(0, HEADS // 2, pair, 0)
+        for fetch in fetches:
+            fetch.wait()
+        dq = dq_ref[...].reshape(width, tags)
+        dkv = dkv_ref[...].reshape(2 * width, cells)
+        one_low = (n_one[...] * vec(10) + vec(6)).astype(bf16)
+        acc_cross[:width] += dot(dq, one_low, 1, 0)
+        acc_cross[width:] += dot(dkv, mem_ref[...], 1, 0)
+        low_cross[...] = acc_cross[...].astype(bf16).T.reshape(low_cross.shape)
+        play(0, 6)
+        g_one = g_two[...] + dot(dq, wt_cross[:width], 0, 0)
+        sum_gain, sum_shift = column_sums(g_one * n_one[...]), column_sums(g_one)
+        g_one = norm_back(g_one, n_one[...], scale_one[...], vec(10))
+        gres_last[...] = g_one
+        g_low = g_one.astype(bf16)
+        acc_zero[...] += dot(mix_one[...].reshape(width, tags), g_low, 1, 0)
+        low_zero[...] = acc_zero[...].astype(bf16).reshape(low_zero.shape)
+        play(0, 7)
+        gmix_last[...] = dot(w_zero[...], g_low, 1, 1).astype(bf16).reshape(gmix_last.shape)
+        at = lax.broadcasted_iota(jnp.int32, add_vec.shape, 0)
+        total = g_vec[...]
+        for k, row in ((2, column_sums(g_one)), (3, column_sums(lane_groups(dq.astype(f32)).T)),
+                       (4, column_sums(memory_lanes(dkv[width:].astype(f32)).T)), (6, sum_shift), (10, sum_gain)):
+            total = total + jnp.where(at == k, row, 0.0)
+        add_vec[...] = total
+
+    turn = jnp.maximum(step - 1, 0)
+    part = jnp.minimum(turn // images, 1)
+    now = lax.rem(turn, images)
+    backward = jnp.logical_and(step >= 1, step <= 2 * images)
+
+    @pl.when(jnp.logical_and(backward, now < images - 1))
+    def _():
+        gmix_now[...] = gmix_ref[0]
+
+    @pl.when(jnp.logical_and(backward, now == images - 1))
+    def _():
+        gmix_now[...] = gmix_last[pl.ds(part * some, some)]
+
+    def d_rows(image, kind, h, count=1):
+        return pl.ds(pl.multiple_of(((image * 3 + kind) * HEADS + h) * HEAD_DIM, HEAD_DIM), count * HEAD_DIM)
+
+    def head(h, _):
+        grad = gmix_now[h].astype(f32)
+        inv = inv_ref[0, pl.ds(part * some + h, 1), :]
+        delta = jnp.sum(grad * mix_ref[0, h].astype(f32), 0, keepdims=True) * inv
+        grad = (grad * inv).astype(bf16)
+        ext = with_delta(grad, delta)
+        qt, kt, vt = qkv_ref[0, 0, h], qkv_ref[0, 1, h], with_ones(qkv_ref[0, 2, h])
+        near, far = near_ref[0, h], far_ref[0, h]
+        ds_near = near * dot(vt[:, :half], ext[:, :half], 0, 0).astype(bf16)
+        ds_far = far * dot(vt, ext[:, half:], 0, 0).astype(bf16)
+        dv = dot(grad[:, half:], far, 1, 1)
+        dk = dot(qt[:, half:], ds_far, 1, 1)
+        dv = jnp.concatenate([dv[:, :half] + dot(grad[:, :half], near, 1, 1), dv[:, half:]], 1)
+        dk = jnp.concatenate([dk[:, :half] + dot(qt[:, :half], ds_near, 1, 1), dk[:, half:]], 1)
+        dq = jnp.concatenate([dot(kt[:, :half], ds_near, 1, 0), dot(kt, ds_far, 1, 0)], 1) * HEAD_DIM ** -0.5
+        at = part * some + h
+        e_ref[d_rows(now, 0, at)] = dq.astype(bf16)
+        e_ref[d_rows(now, 1, at)] = dk.astype(bf16)
+        e_ref[d_rows(now, 2, at)] = dv.astype(bf16)
+        return 0
+
+    @pl.when(backward)
+    def _():
+        lax.fori_loop(0, some, head, 0, unroll=2)
+        d = [e_ref[d_rows(now, kind, part * some, some)] for kind in range(3)]
+        rows = some * HEAD_DIM
+        acc_col[0, pl.ds(part * rows, rows)] += lane_groups(d[0].astype(f32))
+        acc_col[1, pl.ds(part * rows, rows)] += lane_groups(d[2].astype(f32))
+        fresh = now == 0
+        for kind in range(3):
+            product = dot(d[kind], x_ref[0], 1, 0)
+
+            @pl.when(fresh)
+            def _():
+                acc[kind * rows : (kind + 1) * rows] = product
+
+            @pl.when(jnp.logical_not(fresh))
+            def _():
+                acc[kind * rows : (kind + 1) * rows] += product
+
+    @pl.when(step == images)
+    def _():
+        low_half[...] = acc[...].astype(bf16).T.reshape(low_half.shape)
+
+    @pl.when(step == 2 * images)
+    def _():
+        low_rest[...] = acc[...].astype(bf16).T.reshape(low_rest.shape)
+        at = lax.broadcasted_iota(jnp.int32, add_vec.shape, 0)
+        rows = jnp.where(at == 0, column_sums(acc_col[0].T), jnp.where(at == 1, column_sums(acc_col[1].T), add_vec[...]))
+        at = lax.broadcasted_iota(jnp.int32, (16, g_bin.shape[1]), 0)
+        hidden = jnp.where(at == 13, g_bin[...], 0.0)
+        small = collect(rows, width // devices, devices) + collect(hidden, g_bin.shape[1] // devices, devices)
+        low_small[...] = small.astype(bf16).reshape(low_small.shape)
+
+    events(0)
+
+    @pl.when(step > 2 * images)
+    def _():
+        image = jnp.maximum(step - 2 * images - 1, 0)
+        d = e_ref[d_rows(image, 0, 0, 3 * HEADS)]
+        product = dot(d, wt_self[...], 0, 0)
+
+        @pl.when(image < images - 1)
+        def _():
+            g_tags[0] = gres_ref[0] + product
+
+        @pl.when(image == images - 1)
+        def _():
+            g_tags[0] = gres_last[...] + product
+
+    events(1)
+
+    @pl.when(step == 3 * images)
+    def _():
+        for item in every:
+            item.drain()
+
+
+def run_closing(dims, x, qkv, near, far, inv, mix, gmix, g_resid, ckv, mem, vectors, wt_self, wt_cross, w_proj, g_one, g_in, g_out, g_vec, g_bin, kept):
+    scale_one, e, q, inv_two, mix_two, gmix_two, n_one, g_two, acc_cross, acc_zero = kept
+    images, tags, width = x.shape
+    memory = mem.shape[1]
+    half, some = tags // 2, HEADS // 2
+    sds = jax.ShapeDtypeStruct
+    cells = dims + (2,)
+    devices = dims[0] * dims[1] * dims[2] * 2
+
+    def parts(grad):
+        return grad.reshape(cells + (grad.shape[0] // devices, grad.shape[1]))
+
+    low = [parts(g_out), parts(g_in), parts(g_one)]
+    rows = width // devices
+    lows = [cells + (rows, 3 * width), cells + (rows, width)] + [cells + (rows, 3 * width // 2)] * 2 + [cells + (16, 128)]
+
+    def turn(i):
+        t = jnp.clip(i - 1, 0, 2 * images - 1)
+        return lax.rem(t, images), lax.div(t, images)
+
+    def by_turn(shape, split):
+        def index(i):
+            image, part = turn(i)
+            return (image,) + tuple(part if k == split else 0 for k in range(len(shape)))
+        return pl.BlockSpec((1,) + shape, index)
+
+    def gmix_index(i):
+        image, part = turn(i)
+        return jnp.minimum(image, images - 2), part, 0, 0
+
+    def one(*shape):
+        return pl.BlockSpec(shape, lambda i: (0,) * len(shape), pipeline_mode=pl.Buffered(1))
+
+    def out(*shape):
+        return pl.BlockSpec(shape, lambda i: (0,) * len(shape))
+
+    anywhere = pl.BlockSpec(memory_space=pl.ANY)
+    shares = [g.shape[4:] for g in low] + [s[4:] for s in lows]
+    space = []
+    for shape in [g.shape for g in low] + lows:
+        space += [pltpu.VMEM(s, bf16) for s in scatter_space(dims, (), shape[4:])]
+    slots = scatter_slots(dims)
+    qkv = qkv.reshape(images, 3, HEADS, HEAD_DIM, tags)
+    heads = (HEADS, HEAD_DIM, tags)
+    return pl.pallas_call(
+        functools.partial(closing, dims),
+        grid=(3 * images + 1,),
+        in_specs=[
+            by_turn((tags, width), None), by_turn((3, some, HEAD_DIM, tags), 1), by_turn((some, half, half), 0), by_turn((some, tags, half), 0),
+            by_turn((HEADS, tags), None), by_turn((some, HEAD_DIM, tags), 0), pl.BlockSpec((1, some, HEAD_DIM, tags), gmix_index),
+            pl.BlockSpec((1, tags, width), lambda i: (jnp.clip(i - 2 * images - 1, 0, images - 2), 0, 0)),
+            pl.BlockSpec((1, 2 * HEADS, HEAD_DIM, memory), lambda i: (images - 1, 0, 0, 0), pipeline_mode=pl.Buffered(1)),
+            one(*heads), one(HEADS, tags), one(*heads), one(*heads), one(16, width), one(16, width), one(*g_bin.shape), one(tags, 1),
+        ] + [one(*g.shape) for g in low] + [anywhere] * 10,
+        out_specs=[pl.BlockSpec((1, tags, width), lambda i: (jnp.clip(i - 2 * images - 1, 0, images - 1), 0, 0))]
+        + [out(*s) for s in shares] + [pl.BlockSpec((2 * HEADS, HEAD_DIM, memory), lambda i: (0, 0, 0))],
+        out_shape=[sds((images, tags, width), f32)] + [sds(s, f32) for s in shares] + [sds((2 * HEADS, HEAD_DIM, memory), bf16)],
+        scratch_shapes=[
+            pltpu.VMEM((HEADS * memory, tags), bf16), pltpu.VMEM(heads, bf16), pltpu.VMEM((tags, width), f32), pltpu.VMEM((tags, width), f32),
+            pltpu.VMEM((3 * width, width), bf16), pltpu.VMEM((memory, width), bf16), pltpu.VMEM((3 * width, width), f32), pltpu.VMEM((width, width), f32),
+            pltpu.VMEM((width, width), bf16), pltpu.VMEM((3 * width, width), bf16),
+            pltpu.VMEM(heads, bf16), pltpu.VMEM(heads, bf16), pltpu.VMEM((tags, width), f32), pltpu.VMEM((some, HEAD_DIM, tags), bf16),
+            pltpu.VMEM((3 * width // 2, width), f32), pltpu.VMEM((16, width), f32), pltpu.VMEM((2, width, 128), f32),
+        ] + [pltpu.VMEM(s, bf16) for s in lows] + [pltpu.SemaphoreType.DMA((HEADS,)), pltpu.SemaphoreType.DMA((9,))] + space
+        + [pltpu.SemaphoreType.DMA((8, slots)), pltpu.SemaphoreType.DMA((8, slots))],
+        compiler_params=pltpu.CompilerParams(collective_id=1, has_side_effects=True, vmem_limit_bytes=62 * MIB),
+        name="closing",
+    )(x, qkv, near, far, inv, mix, gmix, g_resid, ckv, q, inv_two, mix_two, gmix_two, vectors, g_vec, g_bin, scale_one, *low,
+      e, mix, g_two, n_one, wt_cross, mem, acc_cross, acc_zero, w_proj, wt_self)
+
+
+def settle(lanes, hidden_lanes, images, g_mem_in, dkv, wt_cross, tags, s_out, s_in, s_one, s_cross, s_zero, s_half, s_rest, small,
+           g_mem, o_tags, o_self, o_cross, o_proj, o_in, o_out, o_bin, o_gains, o_biases):
+    width = o_tags.shape[2]
+    o_tags[...] = tags[...]
+
+    @pl.when(pl.program_id(0) == 0)
+    def _():
+        g_mem[0] = dot(dkv[...].reshape(2 * width, -1), wt_cross[...], 0, 0)
+        part = width // 2
+        for kind in range(3):
+            o_self[:, kind * width : kind * width + part] = s_half[:, kind * part : (kind + 1) * part]
+            o_self[:, kind * width + part : (kind + 1) * width] = s_rest[:, kind * part : (kind + 1) * part]
+        o_cross[...] = s_cross[...]
+        o_proj[0] = s_zero[...]
+        o_proj[1] = s_one[...]
+        o_in[...] = s_in[...]
+        o_out[...] = s_out[...]
+        o_biases[...] = small[:10, :lanes]
+        o_gains[...] = small[10:13, :lanes]
+        o_bin[...] = small[13:14, :hidden_lanes]
+
+
+def run_settle(lanes, hidden_lanes, g_mem, dkv, wt_cross, g_tags, shares):
+    images, tags, width = g_tags.shape
+    sds = jax.ShapeDtypeStruct
+    s_out, s_in, s_one, s_cross, s_zero, s_half, s_rest, small = shares
+
+    def one(*shape):
+        return pl.BlockSpec(shape, lambda i: (0,) * len(shape), pipeline_mode=pl.Buffered(1))
+
+    def out(*shape):
+        return pl.BlockSpec(shape, lambda i: (0,) * len(shape))
+
+    rows = s_cross.shape[0]
+    shapes = [s_cross.shape, s_cross.shape, (2, rows, width), s_in.shape, s_out.shape, (1, hidden_lanes), (3, lanes), (10, lanes)]
+    image = pl.BlockSpec((1, tags, width), lambda i: (i, 0, 0))
+    return pl.pallas_call(
+        functools.partial(settle, lanes, hidden_lanes, images),
+        grid=(images,),
+        in_specs=[pl.BlockSpec(memory_space=pl.ANY), one(*dkv.shape),
+                  pl.BlockSpec((2 * width, width), lambda i: (0, 0), pipeline_mode=pl.Buffered(1)), image] + [one(*s.shape) for s in shares],
+        out_specs=[pl.BlockSpec((1,) + g_mem.shape[1:], lambda i: (images - 1, 0, 0)), image] + [out(*s) for s in shapes],
+        out_shape=[sds(g_mem.shape, f32), sds(g_tags.shape, f32)] + [sds(s, f32) for s in shapes],
+        input_output_aliases={0: 0},
+        compiler_params=pltpu.CompilerParams(vmem_limit_bytes=62 * MIB),
+        name="settle",
+    )(g_mem, dkv, wt_cross[width:], g_tags, *shares)
+
+
 AXES = ("wide", "narrow")
 LEADS = (0, 0, 1, 0, 0, 0)
 
@@ -1021,7 +1573,7 @@
 
 def per_device(dims, tag_states, image_memory, tag_lengths, w_self, w_cross, w_proj, w_in, b_in, w_out, ln_gains, biases, out_grad):
     cells = dims + (2,)
-    fused = w_self.shape[0] % 16 == 0
+    fused = w_self.shape[0] % 16 == 0 and tag_states.shape[0] == 3
     devices = dims[0] * dims[1] * dims[2] * 2
     width = tag_states.shape[2]
     lanes, hidden_lanes = biases.shape[1], b_in.shape[0]
@@ -1029,31 +1581,34 @@
         qkv, ckv, near, far, inv, mix, wt_self, wt_cross, vectors, hidden_bias, full_proj, full_in, full_out = run_opening(
             dims, tag_lengths, tag_states, image_memory, biases, ln_gains, b_in[None], (w_cross, w_self, w_proj, w_in, w_out))
         full_proj, full_in, full_out = full_proj.reshape(2, width, width), full_in.reshape(width, -1), full_out.reshape(-1, width)
-        layer_out, g_resid, gmix, dkv, g_cross, g_proj, g_in, g_out, g_vec, g_bin = run_middle(
-            tag_lengths, tag_states, image_memory, out_grad, mix, ckv, wt_cross, full_proj, full_in, full_out, vectors[3][:, None], vectors, hidden_bias)
-        grad_tags, grad_memory, g_self, g_col = run_self_backward(tag_states, qkv, near, far, inv, mix, gmix, g_resid, dkv, wt_self, wt_cross)
-        g_vec = g_vec.at[0:2].set(g_col[0:2])
-    else:
-        small = jnp.concatenate(
-            [
-                jnp.pad(jnp.concatenate([biases, ln_gains]), ((0, 0), (0, 128 - lanes))),
-                jnp.pad(b_in[None], ((0, 2), (0, 128 - hidden_lanes))),
-            ]
-        )
-        shards = (w_self, w_cross, w_proj, w_in, w_out, small)
-        gathered = gather(dims, [fold(s, *s.shape[-2:]) for s in shards], LEADS)
-
-        def whole(held, shard):
-            lead = shard.shape[:-2]
-            rows, columns = shard.shape[-2:]
-            return held.reshape(lead + (devices * rows, columns))
-
-        full_self, full_cross, full_proj, full_in, full_out, full_small = [whole(h, s) for h, s in zip(gathered, shards)]
-        by_device = full_small.reshape(devices, 16, 128)
-        vectors = by_device[:, :, :lanes].transpose(1, 0, 2).reshape(16, width).astype(f32)
-        hidden_bias = by_device[:, 13, :hidden_lanes].reshape(1, -1).astype(f32)
-        layer_out, grad_tags, grad_memory, g_self, g_cross, g_proj, g_in, g_out, g_vec, g_bin = layer(
-            tag_lengths, tag_states, image_memory, out_grad, full_self, full_cross, full_proj, full_in, full_out, vectors, hidden_bias)
+        layer_out, g_resid, gmix, g_mem, _, g_one, g_in, g_out, g_vec, g_bin, *kept = run_middle(
+            tag_lengths, tag_states, image_memory, out_grad, mix, ckv, wt_cross, full_proj, full_in, full_out, vectors, hidden_bias, True)
+        g_tags, *shares, dkv = run_closing(
+            dims, tag_states, qkv, near, far, inv, mix, gmix, g_resid, ckv, image_memory, vectors, wt_self, wt_cross, full_proj,
+            g_one, g_in, g_out, g_vec, g_bin, kept)
+        grad_memory, grad_tags, s_self, s_cross, s_proj, s_in, s_out, s_bin, s_gains, s_biases = run_settle(
+            lanes, hidden_lanes, g_mem, dkv, wt_cross, g_tags, shares)
+        return layer_out, grad_tags, grad_memory, s_self, s_cross, s_proj, s_in, s_bin[0], s_out, s_gains, s_biases
+    small = jnp.concatenate(
+        [
+            jnp.pad(jnp.concatenate([biases, ln_gains]), ((0, 0), (0, 128 - lanes))),
+            jnp.pad(b_in[None], ((0, 2), (0, 128 - hidden_lanes))),
+        ]
+    )
+    shards = (w_self, w_cross, w_proj, w_in, w_out, small)
+    gathered = gather(dims, [fold(s, *s.shape[-2:]) for s in shards], LEADS)
+
+    def whole(held, shard):
+        lead = shard.shape[:-2]
+        rows, columns = shard.shape[-2:]
+        return held.reshape(lead + (devices * rows, columns))
+
+    full_self, full_cross, full_proj, full_in, full_out, full_small = [whole(h, s) for h, s in zip(gathered, shards)]
+    by_device = full_small.reshape(devices, 16, 128)
+    vectors = by_device[:, :, :lanes].transpose(1, 0, 2).reshape(16, width).astype(f32)
+    hidden_bias = by_device[:, 13, :hidden_lanes].reshape(1, -1).astype(f32)
+    layer_out, grad_tags, grad_memory, g_self, g_cross, g_proj, g_in, g_out, g_vec, g_bin = layer(
+        tag_lengths, tag_states, image_memory, out_grad, full_self, full_cross, full_proj, full_in, full_out, vectors, hidden_bias)
     g_small = jnp.pad(g_vec.reshape(16, devices, lanes).transpose(1, 0, 2)[:, :13], ((0, 0), (0, 0), (0, 128 - lanes)))
     g_hidden = jnp.pad(g_bin.reshape(devices, 1, hidden_lanes), ((0, 0), (0, 2), (0, 128 - hidden_lanes)))
     g_small = jnp.concatenate([g_small, g_hidden], 1).astype(bf16).reshape(devices * 16, 128)

time: 247 us -> 208 us (0.84)
  Pallas kernels: 236 us -> 206 us
  local copies, waits for them, and re-layouts: 8.94 us -> 1.12 us
    pallas_call x1, Pallas kernels: 75.6 us -> 55.4 us  [run_opening(): pl.pallas_call(functools.partial(opening, dims), grid=(2 * images,), in_s...]
    pallas_call x3, Pallas kernels: 161 us -> 150 us  [the longest x1 78 us: run_middle(): pl.pallas_call(functools.partial(middle, held_back), grid_spec=pltpu.Pref...]
    unnamed x19 -> x2, local copies, waits for them, and re-layouts: 5.24 us -> 0.01 us
where the time goes in v3:
time: 208 us
  Pallas kernels  206 us (99%)
    pallas_call x1, Pallas kernels, run_middle(): pl.pallas_call(functools.partial(middle, held_back), grid_spec=pltpu.Pref...  78 us
    pallas_call x1, Pallas kernels, run_closing(): pl.pallas_call(functools.partial(closing, dims), grid=(3 * images + 1,),...  65.1 us
    pallas_call x1, Pallas kernels, run_opening(): pl.pallas_call(functools.partial(opening, dims), grid=(2 * images,), in_s...  55.4 us
    pallas_call x1, Pallas kernels, run_settle(): pl.pallas_call(functools.partial(settle, lanes, hidden_lanes, images), gr...  7.04 us

profile of v3, /device:TPU:0, one launch (start us, length us, event | category | flops | bytes accessed | tf_op | source)
XLA Modules:
  0.0 207.6 jit_solution(17899490818039320316)
XLA Ops:
  0.6 55.4 %opening.1 = (bf16[3,24,64,512]{3,2,1,0:T(8,128)(2,1)}, bf16[3,16,64,784]{3,2,1,0:T(8,128)(2,1)}, bf16[3,8,256,256]{3,2,1,0:T(8,128)(2,1)}, bf16[3,8,512,256]{3,...) custom-call(s32[3]{0:T(128)} %lens.3, ...), custom_call_target="tpu_custom_call" | custom-call | tf_op jit(solution)/shard_map/opening/pallas_call | solution.py:1069
  56.1 78.0 %middle.1 = (bf16[3,512,512]{2,1,0:T(8,128)(2,1)}, f32[2,512,512]{2,1,0:T(8,128)}, bf16[2,8,64,512]{3,2,1,0:T(8,128)(2,1)}, f32[3,784,512]{2,1,0:T(8,128)}, bf16...) custom-call(s32[3]{0:T(128)} %lens.3, ...), custom_call_target="tpu_custom_call" | custom-call | tf_op jit(solution)/shard_map/middle/pallas_call | solution.py:706
  134.1 0.0 copy-start
  134.1 65.1 %closing.1 = (f32[3,512,512]{2,1,0:T(8,128)}, f32[32,512]{1,0:T(8,128)}, f32[16,1024]{1,0:T(8,128)}, f32[16,512]{1,0:T(8,128)}, f32[16,1536]{1,0:T(8,128)}, /*in...) custom-call(bf16[3,512,512]{2,1,0:T(8,128)(2,1)} %x_ref.5, ...), custom_call_target="tpu_custom_call" | custom-call | tf_op jit(solution)/shard_map/closing/pallas_call | solution.py:1488
  199.2 0.0 copy-done
  199.2 1.1 slice.3.wt_cross
  200.3 7.0 %settle.1 = (f32[3,784,512]{2,1,0:T(8,128)}, f32[3,512,512]{2,1,0:T(8,128)}, f32[16,1536]{1,0:T(8,128)}, f32[16,1536]{1,0:T(8,128)}, f32[2,16,512]{2,1,0:T(8,128...) custom-call(f32[3,784,512]{2,1,0:T(8,128)} %get-tuple-element.72.g_m, ...), custom_call_target="tpu_custom_call", output_to_operand_aliasing={{0}: (0, {})} | custom-call | tf_op jit(solution)/shard_map/settle/pallas_call | solution.py:1551
Async XLA Ops:
  134.1 65.1 %copy-start = (bf16[1536,512]{1,0:T(8,128)(2,1)S(1)}, bf16[1536,512]{1,0:T(8,128)(2,1)}, u32[]{:S(2)}) copy-start(bf16[1536,512]{1,0:T(8,128)(2,1)} %get-tuple-element.65.wt_cross.wc_any) | copy-start | bytes 4718596

commit v4 on v3

--- a/solution.py
+++ b/solution.py
@@ -322,6 +322,7 @@
 EPS = 1e-5
 MASKED = -1e9
 TAME = 30.0
+CHUNKS = 1
 MIB = 2**20
 
 
@@ -489,7 +490,7 @@
            out_ref, g_resid, g_mix, g_mem, gw_cross, gw_proj, gw_in, gw_out, g_vec, g_bin,
            dkv_ref, cols,
            e_ref, q_ref, inv_ref, mix_two, gmix_two, dq_ref, acc_cross, acc_proj, acc_in, acc_out, acc_vec, acc_bin, acc_col,
-           n_one, n_two):
+           n_one, n_two, scale_two, two_low, act, g_inner, g_ff, g_cross, g_two):
     tags, width = x_ref.shape[1:]
     cells = mem_ref.shape[1]
     i = pl.program_id(0)
@@ -509,7 +510,7 @@
 
     if held_back:
         scale_out, *places, gone = held_back
-        sources = (e_ref, q_ref, inv_ref, mix_two, gmix_two, n_one, n_two, acc_cross, acc_proj.at[0])
+        sources = (e_ref, q_ref, inv_ref, mix_two, gmix_two, n_one, g_two, acc_cross, acc_proj.at[0])
         copies = [pltpu.make_async_copy(src, dst, gone.at[k]) for k, (src, dst) in enumerate(zip(sources, places))]
 
     def leave(*numbers):
@@ -557,41 +558,56 @@
 
     leave(0, 2, 3)
     mix_two_t = mix_two[...].reshape(width, tags)
-    resid = one + dot(mix_two_t, w_proj[1], 0, 0) + vec(5)
-    normed, scale_two = norm(resid)
-    n_two[...] = normed
-    two = normed * vec(11) + vec(7)
-    two_low = two.astype(bf16)
-    inner = dot(two_low, w_in[...], 1, 0) + b_in[...]
     root = 0.7978845608028654
-    square = inner * inner
-    tanh = jnp.tanh(root * inner * (1.0 + 0.044715 * square))
-    act = (0.5 * inner * (1.0 + tanh)).astype(bf16)
-    slope = 0.5 * (1.0 + tanh) + 0.5 * inner * (1.0 - tanh * tanh) * (root * (1.0 + 3 * 0.044715 * square))
-    resid = two + dot(act, w_out[...], 1, 0) + vec(9)
-    three, scale_three = norm(resid)
-    valid = lax.broadcasted_iota(jnp.int32, (tags, 1), 0) < lens[i]
-    out_ref[0] = jnp.where(valid, three * vec(12) + vec(8), 0.0).astype(bf16)
-
-    grad = jnp.where(valid, gout_ref[0].astype(f32), 0.0)
-    add(12, column_sums(grad * three))
-    add(8, column_sums(grad))
-    g_three = norm_back(grad, three, scale_three, vec(12))
-    g_low = g_three.astype(bf16)
-    add(9, column_sums(g_three))
-    acc_out[...] += dot(act, g_low, 0, 0)
-    g_inner = dot(g_low, w_out[...], 1, 1) * slope
-    acc_bin[...] += column_sums(g_inner)
-    g_inner = g_inner.astype(bf16)
-    acc_in[...] += dot(two_low, g_inner, 0, 0)
-    g_two = g_three + dot(g_inner, w_in[...], 1, 1)
-    add(11, column_sums(g_two * n_two[...]))
-    add(7, column_sums(g_two))
-    g_two = norm_back(g_two, n_two[...], scale_two, vec(11))
-    add(5, column_sums(g_two))
-    g_low = g_two.astype(bf16)
-    acc_proj[1] += dot(mix_two_t, g_low, 1, 0)
-    gmix_two[...] = dot(w_proj[1], g_low, 1, 1).astype(bf16).reshape(gmix_two.shape)
+    rows = tags // CHUNKS
+    totals = {}
+
+    def tally(k, value):
+        totals[k] = totals[k] + column_sums(value) if k in totals else column_sums(value)
+
+    for first in range(0, tags, rows):
+        at = slice(first, first + rows)
+        resid = n_one[at] * vec(10) + vec(6) + dot(mix_two_t[:, at], w_proj[1], 0, 0) + vec(5)
+        normed, scale = norm(resid)
+        n_two[at] = normed
+        scale_two[at] = scale
+        two = normed * vec(11) + vec(7)
+        two_low[at] = two.astype(bf16)
+        inner = dot(two_low[at], w_in[...], 1, 0) + b_in[...]
+        square = inner * inner
+        tanh = jnp.tanh(inner * (root + (root * 0.044715) * square))
+        half_more = 0.5 + 0.5 * tanh
+        act[at] = (inner * half_more).astype(bf16)
+        slope = half_more + inner * (half_more * (1.0 - tanh)) * (root + (3 * 0.044715 * root) * square)
+        resid = two + dot(act[at], w_out[...], 1, 0) + vec(9)
+        three, scale = norm(resid)
+        valid = lax.broadcasted_iota(jnp.int32, (rows, 1), 0) + first < lens[i]
+        out_ref[0, at] = jnp.where(valid, three * vec(12) + vec(8), 0.0).astype(bf16)
+        grad = jnp.where(valid, gout_ref[0, at].astype(f32), 0.0)
+        tally(12, grad * three)
+        tally(8, grad)
+        g_three = norm_back(grad, three, scale, vec(12))
+        g_ff[at] = g_three.astype(bf16)
+        tally(9, g_three)
+        back = dot(g_ff[at], w_out[...], 1, 1) * slope
+        tally(-1, back)
+        g_inner[at] = back.astype(bf16)
+        back = g_three + dot(g_inner[at], w_in[...], 1, 1)
+        tally(11, back * n_two[at])
+        tally(7, back)
+        back = norm_back(back, n_two[at], scale_two[at], vec(11))
+        tally(5, back)
+        g_two[at] = back
+        g_cross[at] = back.astype(bf16)
+
+    for k, value in totals.items():
+        if k >= 0:
+            add(k, value)
+    acc_bin[...] += totals[-1]
+    acc_out[...] += dot(act[...], g_ff[...], 0, 0)
+    acc_in[...] += dot(two_low[...], g_inner[...], 0, 0)
+    acc_proj[1] += dot(mix_two_t, g_cross[...], 1, 0)
+    gmix_two[...] = dot(w_proj[1], g_cross[...], 1, 1).astype(bf16).reshape(gmix_two.shape)
 
     def rest_of_image():
         def backward(h, _):
@@ -607,7 +623,7 @@
         acc_cross[:width] += dot(dq, one_low, 1, 0)
         acc_cross[width:] += dot(dkv, mem_ref[0], 1, 0)
         g_mem[0] = dot(dkv, wt_cross[width:], 0, 0)
-        g_one = g_two + dot(dq, wt_cross[:width], 0, 0)
+        g_one = g_two[...] + dot(dq, wt_cross[:width], 0, 0)
         add(10, column_sums(g_one * n_one[...]))
         add(6, column_sums(g_one))
         g_one = norm_back(g_one, n_one[...], scale_one, vec(10))
@@ -622,7 +638,6 @@
 
         @pl.when(i == count - 1)
         def _():
-            n_two[...] = g_two
             scale_out[...] = scale_one
 
         leave(4, 6)
@@ -694,6 +709,13 @@
         pltpu.VMEM((2, width, 128), f32),
         pltpu.VMEM((tags, width), f32),
         pltpu.VMEM((tags, width), f32),
+        pltpu.VMEM((tags, 1), f32),
+        pltpu.VMEM((tags, width), bf16),
+        pltpu.VMEM((tags, hidden), bf16),
+        pltpu.VMEM((tags, hidden), bf16),
+        pltpu.VMEM((tags, width), bf16),
+        pltpu.VMEM((tags, width), bf16),
+        pltpu.VMEM((tags, width), f32),
     ]
     if held_back:
         out_specs[4], out_shape[4] = out(8, 128), sds((8, 128), bf16)
@@ -821,7 +843,7 @@
     ((CROSS, 4),),
     ((PROJ, 4), (IN, 4), (OUT, 4)),
 )
-MEANTIME = {2: (0, 2), 3: (1, 0), 4: (1, 3), 5: (2, 2)}
+MEANTIME = {2: (0, 4), 3: (1, 0), 4: (1, 4), 5: (2, 4)}
 
 
 class Gathering:
@@ -929,8 +951,8 @@
 
 
 def opening(dims, lens, x_ref, mem_ref, b_ref, g_ref, h_ref, s_cross, s_self, s_proj, s_in, s_out,
-            qkv_ref, ckv_ref, near_ref, far_ref, inv_ref, mix_ref, out_self, out_cross, vec_ref, bin_ref, o_proj, o_in, o_out,
-            small, small_low, h_small, h_self, h_cross, wt_self, wt_cross, cols, near_a, far_a, near_b, far_b, gone, local, send, recv):
+            qkv_ref, ckv_ref, low_ref, high_ref, inv_ref, mix_ref, out_self, out_cross, vec_ref, bin_ref, o_proj, o_in, o_out,
+            small, small_low, h_small, h_self, h_cross, wt_self, wt_cross, cols, low_a, high_a, low_b, high_b, tile, beyond, gone, local, send, recv):
     width = x_ref.shape[2]
     tags = x_ref.shape[1]
     half = tags // 2
@@ -975,50 +997,54 @@
         qkv_ref[0, HEADS : 2 * HEADS] = qkv[width : 2 * width].astype(bf16).reshape(HEADS, HEAD_DIM, tags)
         qkv_ref[0, 2 * HEADS :] = (qkv[2 * width :] + cols[:, 1:2]).astype(bf16).reshape(HEADS, HEAD_DIM, tags)
 
-    last = lens[jnp.minimum(step, images - 1)] - 1
-
-    def scores(h, near, far):
-        qt, kt = qkv_ref[0, h], qkv_ref[0, HEADS + h]
-
-        def part(keys, first, held):
-            s = dot(kt[:, :keys], qt[:, first : first + half], 0, 0)
-            key_at = lax.broadcasted_iota(jnp.int32, (keys, half), 0)
-            query_at = lax.broadcasted_iota(jnp.int32, (1, half), 1) + first
-            s = jnp.where(key_at <= jnp.minimum(query_at, last), s, MASKED)
-            held[...] = s
-            return jnp.max(s, 0, keepdims=True)
-
-        return part(half, 0, near), part(tags, half, far)
-
-    def mix(h, near, far, tops):
+    @pl.when(step < images)
+    def _():
+        key_at, query_at = lax.broadcasted_iota(jnp.int32, (half, half), 0), lax.broadcasted_iota(jnp.int32, (half, half), 1)
+        tile[...] = jnp.where(key_at <= query_at, 0.0, MASKED)
+        row, key_at = lax.broadcasted_iota(jnp.int32, beyond.shape, 0), lax.broadcasted_iota(jnp.int32, beyond.shape, 1)
+        hidden = jnp.logical_and(row == 0, key_at >= lens[jnp.minimum(step, images - 1)])
+        beyond[...] = jnp.where(hidden, MASKED, 0.0).astype(bf16)
+
+    def scores(h, low, high):
+        qt, kt = with_ones(qkv_ref[0, h]), jnp.concatenate([qkv_ref[0, HEADS + h], beyond[...]], 0)
+        s = dot(kt[:, :half], qt, 0, 0)
+        left, right = s[:, :half] + tile[...], s[:, half:]
+        under = dot(kt[:, half:], qt[:, half:], 0, 0) + tile[...]
+        low[:, :half] = left
+        low[:, half:] = right
+        high[...] = under
+        return jnp.max(left, 0, keepdims=True), jnp.maximum(jnp.max(right, 0, keepdims=True), jnp.max(under, 0, keepdims=True))
+
+    def mix(h, low, high, tops):
         vt = with_ones(qkv_ref[0, 2 * HEADS + h])
-
-        def part(keys, first, held, top, out):
-            e = jnp.exp(held[...] - top).astype(bf16)
-            out[0, h] = e
-            mixed = dot(vt[:, :keys], e, 1, 0)
-            inv = 1.0 / mixed[HEAD_DIM : HEAD_DIM + 1]
-            inv_ref[0, pl.ds(h, 1), first : first + half] = inv
-            mix_ref[0, h, :, first : first + half] = (mixed[:HEAD_DIM] * inv).astype(bf16)
-
-        part(half, 0, near, tops[0], near_ref)
-        part(tags, half, far, tops[1], far_ref)
-
-    def pair(p, tops):
-        h = 2 * p
-        for slot, (image, number) in MEANTIME.items():
-            pl.when(jnp.logical_and(step == image, p == number))(functools.partial(play, slot))
-        following = scores(h + 1, near_b, far_b)
-        mix(h, near_a, far_a, tops)
-        tops = scores(jnp.minimum(h + 2, HEADS - 1), near_a, far_a)
-        mix(h + 1, near_b, far_b, following)
+        e_low = jnp.concatenate([jnp.exp(low[:, :half] - tops[0]).astype(bf16), jnp.exp(low[:, half:] - tops[1]).astype(bf16)], 1)
+        e_high = jnp.exp(high[...] - tops[1]).astype(bf16)
+        low_ref[0, h] = e_low
+        high_ref[0, h] = e_high
+        mixed = dot(vt[:, :half], e_low, 1, 0)
+        mixed = jnp.concatenate([mixed[:, :half], mixed[:, half:] + dot(vt[:, half:], e_high, 1, 0)], 1)
+        inv = 1.0 / mixed[HEAD_DIM : HEAD_DIM + 1]
+        inv_ref[0, h : h + 1] = inv
+        mix_ref[0, h] = (mixed[:HEAD_DIM] * inv).astype(bf16)
+
+    def pair(h, tops):
+        following = scores(h + 1, low_b, high_b)
+        mix(h, low_a, high_a, tops)
+        if h + 2 < HEADS:
+            tops = scores(h + 2, low_a, high_a)
+        mix(h + 1, low_b, high_b, following)
         return tops
 
     slot_at(0, 1)
 
     @pl.when(step < images)
     def _():
-        lax.fori_loop(0, HEADS // 2, pair, scores(0, near_a, far_a))
+        tops = scores(0, low_a, high_a)
+        for h in range(0, HEADS, 2):
+            for slot, (image, number) in MEANTIME.items():
+                if number == h:
+                    pl.when(step == image)(functools.partial(play, slot))
+            tops = pair(h, tops)
 
     @pl.when(step == images)
     def _():
@@ -1072,15 +1098,15 @@
         in_specs=[pl.BlockSpec(memory_space=pltpu.SMEM), early(tags, width), late(cells, width), one(*biases.shape), one(*gains.shape), one(*b_in.shape)]
         + [anywhere] * len(shards),
         out_specs=[
-            early(3 * HEADS, HEAD_DIM, tags), late(2 * HEADS, HEAD_DIM, cells), early(HEADS, half, half), early(HEADS, tags, half),
+            early(3 * HEADS, HEAD_DIM, tags), late(2 * HEADS, HEAD_DIM, cells), early(HEADS, half, tags), early(HEADS, half, half),
             early(HEADS, tags), early(HEADS, HEAD_DIM, tags), anywhere, anywhere, one(16, width), one(1, hidden),
             anywhere, anywhere, anywhere,
         ],
         out_shape=[
             sds((images, 3 * HEADS, HEAD_DIM, tags), bf16),
             sds((images, 2 * HEADS, HEAD_DIM, cells), bf16),
+            sds((images, HEADS, half, tags), bf16),
             sds((images, HEADS, half, half), bf16),
-            sds((images, HEADS, tags, half), bf16),
             sds((images, HEADS, tags), f32),
             sds((images, HEADS, HEAD_DIM, tags), bf16),
             sds((3 * width, width), bf16),
@@ -1095,7 +1121,8 @@
             pltpu.VMEM((16, 128), f32), pltpu.VMEM((16, 128), bf16), pltpu.VMEM(dims + (2, 16, 128), bf16),
             pltpu.VMEM(cell + (3 * width,), bf16), pltpu.VMEM(cell + (3 * width,), bf16),
             pltpu.VMEM((3 * width, width), bf16), pltpu.VMEM((3 * width, width), bf16),
-            pltpu.VMEM((width, 16), f32), pltpu.VMEM((half, half), f32), pltpu.VMEM((tags, half), f32), pltpu.VMEM((half, half), f32), pltpu.VMEM((tags, half), f32),
+            pltpu.VMEM((width, 16), f32), pltpu.VMEM((half, tags), f32), pltpu.VMEM((half, half), f32), pltpu.VMEM((half, tags), f32), pltpu.VMEM((half, half), f32),
+            pltpu.VMEM((half, half), f32), pltpu.VMEM((16, tags), bf16),
             pltpu.SemaphoreType.DMA((2,)),
             pltpu.SemaphoreType.DMA((n,)), pltpu.SemaphoreType.DMA((n, slots)), pltpu.SemaphoreType.DMA((n, slots)),
         ],
@@ -1105,8 +1132,8 @@
 
 
 class Scattering:
-    def __init__(self, dims, me, grads, out, lead, held, sems):
-        self.dims, self.me, self.grads, self.out, self.lead = dims, me, grads, out, lead
+    def __init__(self, dims, me, grads, mine, out, lead, held, sems):
+        self.dims, self.me, self.grads, self.mine, self.out, self.lead = dims, me, grads, mine, out, lead
         self.pair, self.by_inner, self.by_across, self.by_outer, self.last = held
         self.send, self.recv = sems
 
@@ -1174,21 +1201,29 @@
             for copy in (self.swap(), self.second(core), self.third(core), self.along_outer())[stage - 1]:
                 copy.wait_recv()
             if stage == 1:
-                self.pair[...] = (up(self.grads[self.at(ALL, ALL, ALL, c)]) + up(self.pair[...])).astype(bf16)
+                def add(k, _):
+                    self.pair[k] = (up(self.grads[k, :, :, c]) + up(self.pair[k])).astype(bf16)
+                    return 0
                 following = self.second(core)
             elif stage == 2:
                 held = self.by_inner if core == 0 else self.by_across
-                total = up(self.pair[self.at(ALL, b) if core == 0 else self.at(ALL, ALL, x)])
-                for k in range((inner if core == 0 else across) - 1):
-                    total = total + up(held[k])
-                held[0] = total.astype(bf16)
+
+                def add(k, _):
+                    total = up(self.pair[k, b] if core == 0 else self.pair[k, :, x])
+                    for j in range((inner if core == 0 else across) - 1):
+                        total = total + up(held[j, k])
+                    held[0, k] = total.astype(bf16)
+                    return 0
                 following = self.third(core)
             elif stage == 3:
                 held = self.by_inner if core == 0 else self.by_across
-                total = up(held[(0,) + self.at(ALL, x if core == 0 else b)])
-                for k in range((across if core == 0 else inner) - 1):
-                    total = total + up(self.by_outer[k])
-                self.by_outer[0] = total.astype(bf16)
+
+                def add(k, _):
+                    total = up(held[0, k, x if core == 0 else b])
+                    for j in range((across if core == 0 else inner) - 1):
+                        total = total + up(self.by_outer[j, k])
+                    self.by_outer[0, k] = total.astype(bf16)
+                    return 0
                 following = self.along_outer()
             else:
                 total = up(self.by_outer[(0,) + self.at(a)])
@@ -1196,6 +1231,8 @@
                     total = total + up(self.last[k])
                 self.out[...] = total
                 following = []
+            if stage < 4:
+                lax.fori_loop(0, self.dims[0], add, 0)
             for copy in following:
                 copy.start()
 
@@ -1241,28 +1278,26 @@
 G_OUT, G_IN, G_ONE, G_CROSS, G_ZERO, G_HALF, G_REST, G_SMALL = range(8)
 EVENTS = {
     (0, 0): ((G_OUT, 0), (G_IN, 0), (G_ONE, 0)),
-    (0, 3): ((G_OUT, 1),),
-    (0, 4): ((G_IN, 1), (G_ONE, 1)),
-    (0, 6): ((G_OUT, 2), (G_CROSS, 0)),
-    (0, 7): ((G_IN, 2), (G_ZERO, 0)),
-    (1, 1): ((G_ONE, 2), (G_OUT, 3)),
-    (2, 1): ((G_IN, 3), (G_CROSS, 1), (G_ONE, 3), (G_ZERO, 1)),
-    (3, 1): ((G_HALF, 0), (G_OUT, 4)),
-    (4, 1): ((G_IN, 4), (G_ONE, 4)),
-    (5, 1): ((G_HALF, 1), (G_CROSS, 2)),
-    (6, 1): ((G_REST, 0), (G_SMALL, 0), (G_ZERO, 2)),
-    (7, 1): ((G_HALF, 2),),
-    (8, 1): ((G_CROSS, 3), (G_ZERO, 3), (G_REST, 1), (G_SMALL, 1)),
-    (9, 0): ((G_HALF, 3),),
-    (9, 1): ((G_REST, 2), (G_SMALL, 2), (G_CROSS, 4), (G_ZERO, 4), (G_HALF, 4), (G_REST, 3), (G_SMALL, 3), (G_REST, 4), (G_SMALL, 4)),
+    (0, 1): ((G_OUT, 1),),
+    (0, 2): ((G_IN, 1), (G_ONE, 1)),
+    (0, 6): ((G_CROSS, 0),),
+    (0, 7): ((G_ZERO, 0), (G_OUT, 2)),
+    (1, 1): ((G_IN, 2),),
+    (2, 1): ((G_CROSS, 1), (G_ONE, 2), (G_ZERO, 1)),
+    (3, 1): ((G_HALF, 0), (G_OUT, 3), (G_IN, 3)),
+    (5, 1): ((G_OUT, 4), (G_CROSS, 2), (G_HALF, 1), (G_ONE, 3)),
+    (6, 1): ((G_REST, 0), (G_SMALL, 0), (G_ZERO, 2), (G_IN, 4)),
+    (8, 1): ((G_ONE, 4), (G_CROSS, 3)),
+    (9, 1): ((G_HALF, 2), (G_REST, 1), (G_SMALL, 1), (G_ZERO, 3)),
+    (9, 2): ((G_HALF, 3), (G_CROSS, 4), (G_REST, 2), (G_SMALL, 2), (G_ZERO, 4), (G_HALF, 4), (G_REST, 3), (G_SMALL, 3), (G_REST, 4), (G_SMALL, 4)),
 }
 
 
-def closing(dims, x_ref, qkv_ref, near_ref, far_ref, inv_ref, mix_ref, gmix_ref, gres_ref, ckv_ref, q_ref, inv_two, mix_two, gmix_two,
-            vectors, g_vec, g_bin, scale_one, low_out, low_in, low_one,
-            e_any, mix_any, two_any, one_any, wc_any, mem_any, ac_any, ap_any, wp_any, ws_any,
-            g_tags, sh_out, sh_in, sh_one, sh_cross, sh_zero, sh_half, sh_rest, sh_small, dkv_ref,
-            e_ref, mix_one, g_two, n_one, wt_cross, mem_ref, acc_cross, acc_zero, w_zero, wt_self,
+def closing(dims, x_ref, qkv_ref, low_ref, high_ref, inv_ref, mix_ref, gmix_ref, inv_two, vectors, g_vec, g_bin, scale_one,
+            low_out, low_in, low_one, e_any, ckv_any, q_any, mix_two_any, gmix_two_any, mix_any, two_any, one_any, wc_any, mem_any, ac_any, ap_any, wp_any, ws_any, gres_any,
+            g_tags, sh_out, sh_in, sh_one, sh_cross, sh_zero, sh_half, sh_rest, sh_small, g_mem,
+            e_ref, ckv_ref, q_ref, mix_two, gmix_two, mine_out, mine_in, mine_one, gres_ref, dkv_ref,
+            mix_one, g_two, n_one, wt_cross, mem_ref, acc_cross, acc_zero, w_zero, wt_self,
             dq_ref, gmix_last, gres_last, gmix_now, acc, add_vec, acc_col, low_cross, low_zero, low_half, low_rest, low_small, head_sem, in_sem, *rest):
     tags, width = x_ref.shape[1:]
     cells = mem_ref.shape[0]
@@ -1273,21 +1308,24 @@
     me = place(dims)
     devices = dims[0] * dims[1] * dims[2] * 2
     held, (send, recv) = rest[:-2], rest[-2:]
-    pairs = ((low_out, sh_out), (low_in, sh_in), (low_one, sh_one), (low_cross, sh_cross), (low_zero, sh_zero), (low_half, sh_half),
-             (low_rest, sh_rest), (low_small, sh_small))
-    every = [Scattering(dims, me, grads, out, 0, held[5 * k : 5 * k + 5], (send.at[k], recv.at[k])) for k, (grads, out) in enumerate(pairs)]
+    triples = ((mine_out, None, sh_out), (mine_in, None, sh_in), (mine_one, None, sh_one), (low_cross, None, sh_cross),
+               (low_zero, None, sh_zero), (low_half, None, sh_half), (low_rest, None, sh_rest), (low_small, None, sh_small))
+    every = [Scattering(dims, me, grads, mine, out, 0, held[5 * k : 5 * k + 5], (send.at[k], recv.at[k])) for k, (grads, mine, out) in enumerate(triples)]
     fetches = [
         pltpu.make_async_copy(src, dst, in_sem.at[k])
         for k, (src, dst) in enumerate((
-            (mix_any.at[images - 1], mix_one), (two_any, g_two), (one_any, n_one), (wc_any, wt_cross), (mem_any.at[images - 1], mem_ref),
-            (ac_any, acc_cross), (ap_any, acc_zero), (wp_any.at[0], w_zero), (ws_any, wt_self)))
+            (low_out, mine_out), (low_in, mine_in), (low_one, mine_one),
+            (one_any, n_one), (mem_any.at[images - 1], mem_ref), (ac_any, acc_cross), (two_any, g_two), (wc_any, wt_cross),
+            (mix_any.at[images - 1], mix_one), (ap_any, acc_zero), (wp_any.at[0], w_zero), (gres_any, gres_ref), (ws_any, wt_self)))
     ]
 
     def e_rows(h):
         return e_ref.at[pl.ds(pl.multiple_of(h * cells, 16), cells)]
 
-    def e_fetch(h):
-        return pltpu.make_async_copy(e_any.at[h], e_rows(h), head_sem.at[h])
+    def head_fetches(h):
+        pairs = ((e_any.at[h], e_rows(h)), (ckv_any.at[images - 1, h], ckv_ref.at[h]), (ckv_any.at[images - 1, HEADS + h], ckv_ref.at[HEADS + h]),
+                 (q_any.at[h], q_ref.at[h]), (mix_two_any.at[h], mix_two.at[h]), (gmix_two_any.at[h], gmix_two.at[h]))
+        return [pltpu.make_async_copy(src, dst, head_sem.at[h, k]) for k, (src, dst) in enumerate(pairs)]
 
     def play(number, where):
         for item, stage in EVENTS.get((number, where), ()):
@@ -1303,26 +1341,28 @@
 
     @pl.when(step == 0)
     def _():
+        for fetch in fetches[:3]:
+            fetch.start()
         for h in range(HEADS):
-            e_fetch(h).start()
-        for fetch in fetches:
+            for fetch in head_fetches(h):
+                fetch.start()
+        for fetch in fetches[3:]:
             fetch.start()
         acc_col[...] = jnp.zeros_like(acc_col)
         greet(dims, me)
+        for fetch in fetches[:3]:
+            fetch.wait()
         play(0, 0)
 
-        def pair(p, _):
-            for k in range(1, 4):
-                pl.when(p == k)(functools.partial(play, 0, k + 1))
-            for h in (2 * p, 2 * p + 1):
-                e_fetch(h).wait()
-            for h in (2 * p, 2 * p + 1):
+        for first in (0, some):
+            for h in range(first, first + some):
+                for fetch in head_fetches(h):
+                    fetch.wait()
+            for h in range(first, first + some):
                 dq_ref[h], dkv_ref[h], dkv_ref[HEADS + h] = cross_back(
-                    h, e_rows(h)[...], ckv_ref[0, h], ckv_ref[0, HEADS + h], q_ref[h], gmix_two[h], mix_two[h], inv_two[pl.ds(h, 1), :])
-            return 0
-
-        lax.fori_loop(0, HEADS // 2, pair, 0)
-        for fetch in fetches:
+                    h, e_rows(h)[...], ckv_ref[h], ckv_ref[HEADS + h], q_ref[h], gmix_two[h], mix_two[h], inv_two[h : h + 1, :])
+            play(0, 1 + first // some)
+        for fetch in fetches[3:11]:
             fetch.wait()
         dq = dq_ref[...].reshape(width, tags)
         dkv = dkv_ref[...].reshape(2 * width, cells)
@@ -1370,14 +1410,13 @@
         grad = (grad * inv).astype(bf16)
         ext = with_delta(grad, delta)
         qt, kt, vt = qkv_ref[0, 0, h], qkv_ref[0, 1, h], with_ones(qkv_ref[0, 2, h])
-        near, far = near_ref[0, h], far_ref[0, h]
-        ds_near = near * dot(vt[:, :half], ext[:, :half], 0, 0).astype(bf16)
-        ds_far = far * dot(vt, ext[:, half:], 0, 0).astype(bf16)
-        dv = dot(grad[:, half:], far, 1, 1)
-        dk = dot(qt[:, half:], ds_far, 1, 1)
-        dv = jnp.concatenate([dv[:, :half] + dot(grad[:, :half], near, 1, 1), dv[:, half:]], 1)
-        dk = jnp.concatenate([dk[:, :half] + dot(qt[:, :half], ds_near, 1, 1), dk[:, half:]], 1)
-        dq = jnp.concatenate([dot(kt[:, :half], ds_near, 1, 0), dot(kt, ds_far, 1, 0)], 1) * HEAD_DIM ** -0.5
+        e_low, e_high = low_ref[0, h], high_ref[0, h]
+        ds_low = e_low * dot(vt[:, :half], ext, 0, 0).astype(bf16)
+        ds_high = e_high * dot(vt[:, half:], ext[:, half:], 0, 0).astype(bf16)
+        dv = jnp.concatenate([dot(grad, e_low, 1, 1), dot(grad[:, half:], e_high, 1, 1)], 1)
+        dk = jnp.concatenate([dot(qt, ds_low, 1, 1), dot(qt[:, half:], ds_high, 1, 1)], 1)
+        dq = dot(kt[:, :half], ds_low, 1, 0)
+        dq = jnp.concatenate([dq[:, :half], dq[:, half:] + dot(kt[:, half:], ds_high, 1, 0)], 1) * HEAD_DIM ** -0.5
         at = part * some + h
         e_ref[d_rows(now, 0, at)] = dq.astype(bf16)
         e_ref[d_rows(now, 1, at)] = dk.astype(bf16)
@@ -1386,7 +1425,7 @@
 
     @pl.when(backward)
     def _():
-        lax.fori_loop(0, some, head, 0, unroll=2)
+        lax.fori_loop(0, some, head, 0, unroll=some)
         d = [e_ref[d_rows(now, kind, part * some, some)] for kind in range(3)]
         rows = some * HEAD_DIM
         acc_col[0, pl.ds(part * rows, rows)] += lane_groups(d[0].astype(f32))
@@ -1419,6 +1458,11 @@
 
     events(0)
 
+    @pl.when(step == 2 * images + 1)
+    def _():
+        for fetch in fetches[11:]:
+            fetch.wait()
+
     @pl.when(step > 2 * images)
     def _():
         image = jnp.maximum(step - 2 * images - 1, 0)
@@ -1427,7 +1471,7 @@
 
         @pl.when(image < images - 1)
         def _():
-            g_tags[0] = gres_ref[0] + product
+            g_tags[0] = gres_ref[jnp.minimum(image, images - 2)] + product
 
         @pl.when(image == images - 1)
         def _():
@@ -1437,11 +1481,17 @@
 
     @pl.when(step == 3 * images)
     def _():
+        g_mem[...] = dot(dkv_ref[...].reshape(2 * width, cells), wt_cross[width:], 0, 0)
+
+    events(2)
+
+    @pl.when(step == 3 * images)
+    def _():
         for item in every:
             item.drain()
 
 
-def run_closing(dims, x, qkv, near, far, inv, mix, gmix, g_resid, ckv, mem, vectors, wt_self, wt_cross, w_proj, g_one, g_in, g_out, g_vec, g_bin, kept):
+def run_closing(dims, x, qkv, e_low, e_high, inv, mix, gmix, g_resid, ckv, mem, vectors, wt_self, wt_cross, w_proj, g_one, g_in, g_out, g_vec, g_bin, kept):
     scale_one, e, q, inv_two, mix_two, gmix_two, n_one, g_two, acc_cross, acc_zero = kept
     images, tags, width = x.shape
     memory = mem.shape[1]
@@ -1489,37 +1539,38 @@
         functools.partial(closing, dims),
         grid=(3 * images + 1,),
         in_specs=[
-            by_turn((tags, width), None), by_turn((3, some, HEAD_DIM, tags), 1), by_turn((some, half, half), 0), by_turn((some, tags, half), 0),
+            by_turn((tags, width), None), by_turn((3, some, HEAD_DIM, tags), 1), by_turn((some, half, tags), 0), by_turn((some, half, half), 0),
             by_turn((HEADS, tags), None), by_turn((some, HEAD_DIM, tags), 0), pl.BlockSpec((1, some, HEAD_DIM, tags), gmix_index),
-            pl.BlockSpec((1, tags, width), lambda i: (jnp.clip(i - 2 * images - 1, 0, images - 2), 0, 0)),
-            pl.BlockSpec((1, 2 * HEADS, HEAD_DIM, memory), lambda i: (images - 1, 0, 0, 0), pipeline_mode=pl.Buffered(1)),
-            one(*heads), one(HEADS, tags), one(*heads), one(*heads), one(16, width), one(16, width), one(*g_bin.shape), one(tags, 1),
-        ] + [one(*g.shape) for g in low] + [anywhere] * 10,
+            one(HEADS, tags), one(16, width), one(16, width), one(*g_bin.shape), one(tags, 1),
+        ] + [anywhere] * 18,
         out_specs=[pl.BlockSpec((1, tags, width), lambda i: (jnp.clip(i - 2 * images - 1, 0, images - 1), 0, 0))]
-        + [out(*s) for s in shares] + [pl.BlockSpec((2 * HEADS, HEAD_DIM, memory), lambda i: (0, 0, 0))],
-        out_shape=[sds((images, tags, width), f32)] + [sds(s, f32) for s in shares] + [sds((2 * HEADS, HEAD_DIM, memory), bf16)],
+        + [out(*s) for s in shares] + [out(memory, width)],
+        out_shape=[sds((images, tags, width), f32)] + [sds(s, f32) for s in shares] + [sds((memory, width), f32)],
         scratch_shapes=[
-            pltpu.VMEM((HEADS * memory, tags), bf16), pltpu.VMEM(heads, bf16), pltpu.VMEM((tags, width), f32), pltpu.VMEM((tags, width), f32),
+            pltpu.VMEM((HEADS * memory, tags), bf16), pltpu.VMEM((2 * HEADS, HEAD_DIM, memory), bf16), pltpu.VMEM(heads, bf16), pltpu.VMEM(heads, bf16), pltpu.VMEM(heads, bf16),
+        ] + [pltpu.VMEM(g.shape, bf16) for g in low] + [
+            pltpu.VMEM((images - 1, tags, width), f32), pltpu.VMEM((2 * HEADS, HEAD_DIM, memory), bf16),
+            pltpu.VMEM(heads, bf16), pltpu.VMEM((tags, width), f32), pltpu.VMEM((tags, width), f32),
             pltpu.VMEM((3 * width, width), bf16), pltpu.VMEM((memory, width), bf16), pltpu.VMEM((3 * width, width), f32), pltpu.VMEM((width, width), f32),
             pltpu.VMEM((width, width), bf16), pltpu.VMEM((3 * width, width), bf16),
             pltpu.VMEM(heads, bf16), pltpu.VMEM(heads, bf16), pltpu.VMEM((tags, width), f32), pltpu.VMEM((some, HEAD_DIM, tags), bf16),
             pltpu.VMEM((3 * width // 2, width), f32), pltpu.VMEM((16, width), f32), pltpu.VMEM((2, width, 128), f32),
-        ] + [pltpu.VMEM(s, bf16) for s in lows] + [pltpu.SemaphoreType.DMA((HEADS,)), pltpu.SemaphoreType.DMA((9,))] + space
+        ] + [pltpu.VMEM(s, bf16) for s in lows] + [pltpu.SemaphoreType.DMA((HEADS, 6)), pltpu.SemaphoreType.DMA((13,))] + space
         + [pltpu.SemaphoreType.DMA((8, slots)), pltpu.SemaphoreType.DMA((8, slots))],
         compiler_params=pltpu.CompilerParams(collective_id=1, has_side_effects=True, vmem_limit_bytes=62 * MIB),
         name="closing",
-    )(x, qkv, near, far, inv, mix, gmix, g_resid, ckv, q, inv_two, mix_two, gmix_two, vectors, g_vec, g_bin, scale_one, *low,
-      e, mix, g_two, n_one, wt_cross, mem, acc_cross, acc_zero, w_proj, wt_self)
-
-
-def settle(lanes, hidden_lanes, images, g_mem_in, dkv, wt_cross, tags, s_out, s_in, s_one, s_cross, s_zero, s_half, s_rest, small,
+    )(x, qkv, e_low, e_high, inv, mix, gmix, inv_two, vectors, g_vec, g_bin, scale_one, *low,
+      e, ckv, q, mix_two, gmix_two, mix, g_two, n_one, wt_cross, mem, acc_cross, acc_zero, w_proj, wt_self, g_resid)
+
+
+def settle(lanes, hidden_lanes, images, g_mem_in, m_last, tags, s_out, s_in, s_one, s_cross, s_zero, s_half, s_rest, small,
            g_mem, o_tags, o_self, o_cross, o_proj, o_in, o_out, o_bin, o_gains, o_biases):
     width = o_tags.shape[2]
     o_tags[...] = tags[...]
 
     @pl.when(pl.program_id(0) == 0)
     def _():
-        g_mem[0] = dot(dkv[...].reshape(2 * width, -1), wt_cross[...], 0, 0)
+        g_mem[0] = m_last[...]
         part = width // 2
         for kind in range(3):
             o_self[:, kind * width : kind * width + part] = s_half[:, kind * part : (kind + 1) * part]
@@ -1534,7 +1585,7 @@
         o_bin[...] = small[13:14, :hidden_lanes]
 
 
-def run_settle(lanes, hidden_lanes, g_mem, dkv, wt_cross, g_tags, shares):
+def run_settle(lanes, hidden_lanes, g_mem, m_last, g_tags, shares):
     images, tags, width = g_tags.shape
     sds = jax.ShapeDtypeStruct
     s_out, s_in, s_one, s_cross, s_zero, s_half, s_rest, small = shares
@@ -1551,14 +1602,13 @@
     return pl.pallas_call(
         functools.partial(settle, lanes, hidden_lanes, images),
         grid=(images,),
-        in_specs=[pl.BlockSpec(memory_space=pl.ANY), one(*dkv.shape),
-                  pl.BlockSpec((2 * width, width), lambda i: (0, 0), pipeline_mode=pl.Buffered(1)), image] + [one(*s.shape) for s in shares],
+        in_specs=[pl.BlockSpec(memory_space=pl.ANY), one(*m_last.shape), image] + [one(*s.shape) for s in shares],
         out_specs=[pl.BlockSpec((1,) + g_mem.shape[1:], lambda i: (images - 1, 0, 0)), image] + [out(*s) for s in shapes],
         out_shape=[sds(g_mem.shape, f32), sds(g_tags.shape, f32)] + [sds(s, f32) for s in shapes],
         input_output_aliases={0: 0},
         compiler_params=pltpu.CompilerParams(vmem_limit_bytes=62 * MIB),
         name="settle",
-    )(g_mem, dkv, wt_cross[width:], g_tags, *shares)
+    )(g_mem, m_last, g_tags, *shares)
 
 
 AXES = ("wide", "narrow")
@@ -1583,11 +1633,11 @@
         full_proj, full_in, full_out = full_proj.reshape(2, width, width), full_in.reshape(width, -1), full_out.reshape(-1, width)
         layer_out, g_resid, gmix, g_mem, _, g_one, g_in, g_out, g_vec, g_bin, *kept = run_middle(
             tag_lengths, tag_states, image_memory, out_grad, mix, ckv, wt_cross, full_proj, full_in, full_out, vectors, hidden_bias, True)
-        g_tags, *shares, dkv = run_closing(
+        g_tags, *shares, m_last = run_closing(
             dims, tag_states, qkv, near, far, inv, mix, gmix, g_resid, ckv, image_memory, vectors, wt_self, wt_cross, full_proj,
             g_one, g_in, g_out, g_vec, g_bin, kept)
         grad_memory, grad_tags, s_self, s_cross, s_proj, s_in, s_out, s_bin, s_gains, s_biases = run_settle(
-            lanes, hidden_lanes, g_mem, dkv, wt_cross, g_tags, shares)
+            lanes, hidden_lanes, g_mem, m_last, g_tags, shares)
         return layer_out, grad_tags, grad_memory, s_self, s_cross, s_proj, s_in, s_bin[0], s_out, s_gains, s_biases
     small = jnp.concatenate(
         [

time: 208 us -> 197 us (0.947)
  Pallas kernels: 206 us -> 196 us
    pallas_call x1, Pallas kernels: 78 us -> 64.3 us  [run_middle(): pl.pallas_call(functools.partial(middle, held_back), grid_spec=pltpu.Pref...]
    pallas_call x1, Pallas kernels: 65.1 us -> 73 us  [run_closing(): pl.pallas_call(functools.partial(closing, dims), grid=(3 * images + 1,),...]
    pallas_call x1, Pallas kernels: 55.4 us -> 53 us  [run_opening(): pl.pallas_call(functools.partial(opening, dims), grid=(2 * images,), in_s...]
where the time goes in v4:
time: 197 us
  Pallas kernels  196 us (99%)
    pallas_call x1, Pallas kernels, run_closing(): pl.pallas_call(functools.partial(closing, dims), grid=(3 * images + 1,),...  73 us
    pallas_call x1, Pallas kernels, run_middle(): pl.pallas_call(functools.partial(middle, held_back), grid_spec=pltpu.Pref...  64.3 us
    pallas_call x1, Pallas kernels, run_opening(): pl.pallas_call(functools.partial(opening, dims), grid=(2 * images,), in_s...  53 us
    pallas_call x1, Pallas kernels, run_settle(): pl.pallas_call(functools.partial(settle, lanes, hidden_lanes, images), gr...  5.81 us

profile of v4, /device:TPU:0, one launch (start us, length us, event | category | flops | bytes accessed | tf_op | source)
XLA Modules:
  0.0 196.9 jit_solution(8211684611674762803)
XLA Ops:
  0.6 53.0 %opening.1 = (bf16[3,24,64,512]{3,2,1,0:T(8,128)(2,1)}, bf16[3,16,64,784]{3,2,1,0:T(8,128)(2,1)}, bf16[3,8,256,512]{3,2,1,0:T(8,128)(2,1)}, bf16[3,8,256,256]{3,...) custom-call(s32[3]{0:T(128)} %lens.3, ...), custom_call_target="tpu_custom_call" | custom-call | tf_op jit(solution)/shard_map/opening/pallas_call | solution.py:1095
  53.7 64.3 %middle.1 = (bf16[3,512,512]{2,1,0:T(8,128)(2,1)}, f32[2,512,512]{2,1,0:T(8,128)}, bf16[2,8,64,512]{3,2,1,0:T(8,128)(2,1)}, f32[3,784,512]{2,1,0:T(8,128)}, bf16...) custom-call(s32[3]{0:T(128)} %lens.3, ...), custom_call_target="tpu_custom_call" | custom-call | tf_op jit(solution)/shard_map/middle/pallas_call | solution.py:728
  117.9 73.0 %closing.1 = (f32[3,512,512]{2,1,0:T(8,128)}, f32[32,512]{1,0:T(8,128)}, f32[16,1024]{1,0:T(8,128)}, f32[16,512]{1,0:T(8,128)}, f32[16,1536]{1,0:T(8,128)}, /*in...) custom-call(bf16[3,512,512]{2,1,0:T(8,128)(2,1)} %x_ref.5, ...), custom_call_target="tpu_custom_call" | custom-call | tf_op jit(solution)/shard_map/closing/pallas_call | solution.py:1538
  190.9 5.8 %settle.1 = (f32[3,784,512]{2,1,0:T(8,128)}, f32[3,512,512]{2,1,0:T(8,128)}, f32[16,1536]{1,0:T(8,128)}, f32[16,1536]{1,0:T(8,128)}, f32[2,16,512]{2,1,0:T(8,128...) custom-call(f32[3,784,512]{2,1,0:T(8,128)} %get-tuple-element.72.g_m, ...), custom_call_target="tpu_custom_call", output_to_operand_aliasing={{0}: (0, {})} | custom-call | tf_op jit(solution)/shard_map/settle/pallas_call | solution.py:1602

commit v5 on v4

--- a/solution.py
+++ b/solution.py
@@ -27,7 +27,7 @@
     return {"wide": a * dims[1] + b, "narrow": x * 2 + c}
 
 
-def greet(dims, me):
+def greet(dims, me, diagonal=False):
     a, b, x, c = me
     outer, inner, across = dims
     barrier = pltpu.get_barrier_semaphore()
@@ -35,6 +35,8 @@
     peers += [(a, lax.rem(b + k, inner), x, c) for k in range(1, inner)]
     peers += [(a, b, lax.rem(x + k, across), c) for k in range(1, across)]
     peers += [(a, b, x, 1 - c)]
+    if diagonal:
+        peers += [(a, lax.rem(b + j, inner), lax.rem(x + k, across), c) for j in range(1, inner) for k in range(1, across)]
     for peer in peers:
         pl.semaphore_signal(barrier, inc=1, device_id=device(dims, *peer), device_id_type=MESH)
     pl.semaphore_wait(barrier, len(peers))
@@ -486,21 +488,24 @@
                 out_ref, g_resid, g_mix, g_mem, gw_cross, gw_proj, gw_in, gw_out, g_vec, g_bin, *rest)
 
 
-def middle_body(held_back, lens, x_ref, mem_ref, gout_ref, mix_one, ckv_ref, wt_cross, w_proj, w_in, w_out, vectors, b_in,
+def middle_body(held_back, lens, x_ref, mem_ref, gout_ref, mix_one, ckv_ref, wt_cross, w_proj, far_in, far_out, vectors, b_in,
            out_ref, g_resid, g_mix, g_mem, gw_cross, gw_proj, gw_in, gw_out, g_vec, g_bin,
            dkv_ref, cols,
            e_ref, q_ref, inv_ref, mix_two, gmix_two, dq_ref, acc_cross, acc_proj, acc_in, acc_out, acc_vec, acc_bin, acc_col,
-           n_one, n_two, scale_two, two_low, act, g_inner, g_ff, g_cross, g_two):
+           n_one, n_two, scale_two, two_low, act, g_inner, g_ff, g_cross, g_two, w_in, w_out, come):
     tags, width = x_ref.shape[1:]
     cells = mem_ref.shape[1]
     i = pl.program_id(0)
     count = pl.num_programs(0)
+    arrivals = [pltpu.make_async_copy(src, dst, come.at[k]) for k, (src, dst) in enumerate(((far_in, w_in), (far_out, w_out)))]
 
     @pl.when(i == 0)
     def _():
         for ref in (acc_cross, acc_proj, acc_in, acc_out, acc_vec, acc_bin, acc_col):
             ref[...] = jnp.zeros_like(ref)
         cols[...] = vectors[...].T
+        for copy in arrivals:
+            copy.start()
 
     def vec(k):
         return vectors[k : k + 1, :]
@@ -557,6 +562,11 @@
         lax.fori_loop(0, HEADS, functools.partial(forward, True), 0)
 
     leave(0, 2, 3)
+    @pl.when(i == 0)
+    def _():
+        for copy in arrivals:
+            copy.wait()
+
     mix_two_t = mix_two[...].reshape(width, tags)
     root = 0.7978845608028654
     rows = tags // CHUNKS
@@ -716,6 +726,9 @@
         pltpu.VMEM((tags, width), bf16),
         pltpu.VMEM((tags, width), bf16),
         pltpu.VMEM((tags, width), f32),
+        pltpu.VMEM((width, hidden), bf16),
+        pltpu.VMEM((hidden, width), bf16),
+        pltpu.SemaphoreType.DMA((2,)),
     ]
     if held_back:
         out_specs[4], out_shape[4] = out(8, 128), sds((8, 128), bf16)
@@ -732,7 +745,7 @@
             grid=(images,),
             in_specs=[
                 per(tags, width), per(cells, width), per(tags, width), per(HEADS, HEAD_DIM, tags), per(2 * HEADS, HEAD_DIM, cells),
-                one(3 * width, width), one(2, width, width), one(width, hidden), one(hidden, width), one(16, width), one(1, hidden),
+                one(3 * width, width), one(2, width, width), pl.BlockSpec(memory_space=pl.ANY), pl.BlockSpec(memory_space=pl.ANY), one(16, width), one(1, hidden),
             ],
             out_specs=out_specs,
             scratch_shapes=scratch,
@@ -1132,8 +1145,8 @@
 
 
 class Scattering:
-    def __init__(self, dims, me, grads, mine, out, lead, held, sems):
-        self.dims, self.me, self.grads, self.mine, self.out, self.lead = dims, me, grads, mine, out, lead
+    def __init__(self, dims, me, grads, short, out, lead, held, sems):
+        self.dims, self.me, self.grads, self.short, self.out, self.lead = dims, me, grads, short, out, lead
         self.pair, self.by_inner, self.by_across, self.by_outer, self.last = held
         self.send, self.recv = sems
 
@@ -1186,11 +1199,57 @@
             for k in range(1, outer)
         ]
 
+    def over_plane(self):
+        a, b, x, c = self.me
+        _, inner, across = self.dims
+        res = []
+        for k in range(1, inner * across):
+            row, column = lax.rem(b + k // across, inner), lax.rem(x + k % across, across)
+            res.append(self.remote(k, self.pair.at[:, row, column], self.by_inner.at[k - 1], (a, row, column, c)))
+        return res
+
+    def from_plane(self):
+        a, b, x, c = self.me
+        outer, inner, across = self.dims
+        return [
+            self.remote(inner * across - 1 + k, self.by_outer.at[0, lax.rem(a + k, outer)], self.last.at[k - 1], (lax.rem(a + k, outer), b, x, c))
+            for k in range(1, outer)
+        ]
+
     def begin(self):
         for copy in self.swap():
             copy.start()
 
+    def advance_short(self, stage):
+        a, b, x, c = self.me
+        outer, inner, across = self.dims
+
+        def up(value):
+            return value.astype(f32)
+
+        for copy in (self.swap(), self.over_plane(), self.from_plane())[stage - 1]:
+            copy.wait_recv()
+        if stage == 1:
+            self.pair[...] = (up(self.grads[:, :, :, c]) + up(self.pair[...])).astype(bf16)
+            following = self.over_plane()
+        elif stage == 2:
+            total = up(self.pair[:, b, x])
+            for k in range(inner * across - 1):
+                total = total + up(self.by_inner[k])
+            self.by_outer[0] = total.astype(bf16)
+            following = self.from_plane()
+        else:
+            total = up(self.by_outer[0, a])
+            for k in range(outer - 1):
+                total = total + up(self.last[k])
+            self.out[...] = total
+            following = []
+        for copy in following:
+            copy.start()
+
     def advance(self, stage):
+        if self.short:
+            return self.advance_short(stage)
         a, b, x, c = self.me
         _, inner, across = self.dims
 
@@ -1244,16 +1303,22 @@
             for copy in self.swap() + self.second(core) + self.third(core) + self.along_outer():
                 copy.wait_send()
 
+        if self.short:
+            for copy in self.swap() + self.over_plane() + self.from_plane():
+                copy.wait_send()
+            return
         for core in (0, 1):
             pl.when(self.me[3] == core)(functools.partial(act, core))
 
 
 def scatter_slots(dims):
-    return dims[0] + dims[1] + dims[2] - 2
-
-
-def scatter_space(dims, lead, tail):
+    return max(dims[0] + dims[1] + dims[2] - 2, dims[0] + dims[1] * dims[2] - 1)
+
+
+def scatter_space(dims, lead, tail, short=False):
     outer, inner, across = dims
+    if short:
+        return [(outer, inner, across) + tail, (inner * across - 1, outer) + tail, (1,) + tail, (1, outer) + tail, (outer - 1,) + tail]
     return [
         lead + (outer, inner, across) + tail,
         (inner - 1,) + lead + (outer, across) + tail,
@@ -1276,6 +1341,7 @@
 
 
 G_OUT, G_IN, G_ONE, G_CROSS, G_ZERO, G_HALF, G_REST, G_SMALL = range(8)
+SHORT = (G_REST, G_SMALL)
 EVENTS = {
     (0, 0): ((G_OUT, 0), (G_IN, 0), (G_ONE, 0)),
     (0, 1): ((G_OUT, 1),),
@@ -1289,7 +1355,7 @@
     (6, 1): ((G_REST, 0), (G_SMALL, 0), (G_ZERO, 2), (G_IN, 4)),
     (8, 1): ((G_ONE, 4), (G_CROSS, 3)),
     (9, 1): ((G_HALF, 2), (G_REST, 1), (G_SMALL, 1), (G_ZERO, 3)),
-    (9, 2): ((G_HALF, 3), (G_CROSS, 4), (G_REST, 2), (G_SMALL, 2), (G_ZERO, 4), (G_HALF, 4), (G_REST, 3), (G_SMALL, 3), (G_REST, 4), (G_SMALL, 4)),
+    (9, 2): ((G_HALF, 3), (G_REST, 2), (G_SMALL, 2), (G_CROSS, 4), (G_ZERO, 4), (G_HALF, 4), (G_REST, 3), (G_SMALL, 3)),
 }
 
 
@@ -1310,7 +1376,7 @@
     held, (send, recv) = rest[:-2], rest[-2:]
     triples = ((mine_out, None, sh_out), (mine_in, None, sh_in), (mine_one, None, sh_one), (low_cross, None, sh_cross),
                (low_zero, None, sh_zero), (low_half, None, sh_half), (low_rest, None, sh_rest), (low_small, None, sh_small))
-    every = [Scattering(dims, me, grads, mine, out, 0, held[5 * k : 5 * k + 5], (send.at[k], recv.at[k])) for k, (grads, mine, out) in enumerate(triples)]
+    every = [Scattering(dims, me, grads, k in SHORT, out, 0, held[5 * k : 5 * k + 5], (send.at[k], recv.at[k])) for k, (grads, _, out) in enumerate(triples)]
     fetches = [
         pltpu.make_async_copy(src, dst, in_sem.at[k])
         for k, (src, dst) in enumerate((
@@ -1349,7 +1415,7 @@
         for fetch in fetches[3:]:
             fetch.start()
         acc_col[...] = jnp.zeros_like(acc_col)
-        greet(dims, me)
+        greet(dims, me, True)
         for fetch in fetches[:3]:
             fetch.wait()
         play(0, 0)
@@ -1471,17 +1537,17 @@
 
         @pl.when(image < images - 1)
         def _():
-            g_tags[0] = gres_ref[jnp.minimum(image, images - 2)] + product
+            g_tags[0] = (gres_ref[jnp.minimum(image, images - 2)] + product).astype(bf16)
 
         @pl.when(image == images - 1)
         def _():
-            g_tags[0] = gres_last[...] + product
+            g_tags[0] = (gres_last[...] + product).astype(bf16)
 
     events(1)
 
     @pl.when(step == 3 * images)
     def _():
-        g_mem[...] = dot(dkv_ref[...].reshape(2 * width, cells), wt_cross[width:], 0, 0)
+        g_mem[...] = dot(dkv_ref[...].reshape(2 * width, cells), wt_cross[width:], 0, 0).astype(bf16)
 
     events(2)
 
@@ -1530,8 +1596,8 @@
     anywhere = pl.BlockSpec(memory_space=pl.ANY)
     shares = [g.shape[4:] for g in low] + [s[4:] for s in lows]
     space = []
-    for shape in [g.shape for g in low] + lows:
-        space += [pltpu.VMEM(s, bf16) for s in scatter_space(dims, (), shape[4:])]
+    for k, shape in enumerate([g.shape for g in low] + lows):
+        space += [pltpu.VMEM(s, bf16) for s in scatter_space(dims, (), shape[4:], k in SHORT)]
     slots = scatter_slots(dims)
     qkv = qkv.reshape(images, 3, HEADS, HEAD_DIM, tags)
     heads = (HEADS, HEAD_DIM, tags)
@@ -1545,7 +1611,7 @@
         ] + [anywhere] * 18,
         out_specs=[pl.BlockSpec((1, tags, width), lambda i: (jnp.clip(i - 2 * images - 1, 0, images - 1), 0, 0))]
         + [out(*s) for s in shares] + [out(memory, width)],
-        out_shape=[sds((images, tags, width), f32)] + [sds(s, f32) for s in shares] + [sds((memory, width), f32)],
+        out_shape=[sds((images, tags, width), bf16)] + [sds(s, f32) for s in shares] + [sds((memory, width), bf16)],
         scratch_shapes=[
             pltpu.VMEM((HEADS * memory, tags), bf16), pltpu.VMEM((2 * HEADS, HEAD_DIM, memory), bf16), pltpu.VMEM(heads, bf16), pltpu.VMEM(heads, bf16), pltpu.VMEM(heads, bf16),
         ] + [pltpu.VMEM(g.shape, bf16) for g in low] + [
@@ -1566,11 +1632,11 @@
 def settle(lanes, hidden_lanes, images, g_mem_in, m_last, tags, s_out, s_in, s_one, s_cross, s_zero, s_half, s_rest, small,
            g_mem, o_tags, o_self, o_cross, o_proj, o_in, o_out, o_bin, o_gains, o_biases):
     width = o_tags.shape[2]
-    o_tags[...] = tags[...]
+    o_tags[...] = tags[...].astype(f32)
 
     @pl.when(pl.program_id(0) == 0)
     def _():
-        g_mem[0] = m_last[...]
+        g_mem[0] = m_last[...].astype(f32)
         part = width // 2
         for kind in range(3):
             o_self[:, kind * width : kind * width + part] = s_half[:, kind * part : (kind + 1) * part]

time: 197 us -> 192 us (0.975)
  Pallas kernels: 196 us -> 191 us
    pallas_call x1, Pallas kernels: 73 us -> 70.1 us  [run_closing(): pl.pallas_call(functools.partial(closing, dims), grid=(3 * images + 1,),...]
where the time goes in v5:
time: 192 us
  Pallas kernels  191 us (99%)
    pallas_call x1, Pallas kernels, run_closing(): pl.pallas_call(functools.partial(closing, dims), grid=(3 * images + 1,),...  70.1 us
    pallas_call x1, Pallas kernels, run_middle(): pl.pallas_call(functools.partial(middle, held_back), grid_spec=pltpu.Pref...  63.6 us
    pallas_call x1, Pallas kernels, run_opening(): pl.pallas_call(functools.partial(opening, dims), grid=(2 * images,), in_s...  52.9 us
    pallas_call x1, Pallas kernels, run_settle(): pl.pallas_call(functools.partial(settle, lanes, hidden_lanes, images), gr...  4.82 us

profile of v5, /device:TPU:0, one launch (start us, length us, event | category | flops | bytes accessed | tf_op | source)
XLA Modules:
  0.0 192.3 jit_solution(7557871155785815020)
XLA Ops:
  0.6 52.9 %opening.1 = (bf16[3,24,64,512]{3,2,1,0:T(8,128)(2,1)}, bf16[3,16,64,784]{3,2,1,0:T(8,128)(2,1)}, bf16[3,8,256,512]{3,2,1,0:T(8,128)(2,1)}, bf16[3,8,256,256]{3,...) custom-call(s32[3]{0:T(128)} %lens.3, ...), custom_call_target="tpu_custom_call" | custom-call | tf_op jit(solution)/shard_map/opening/pallas_call | solution.py:1108
  53.6 63.6 %middle.1 = (bf16[3,512,512]{2,1,0:T(8,128)(2,1)}, f32[2,512,512]{2,1,0:T(8,128)}, bf16[2,8,64,512]{3,2,1,0:T(8,128)(2,1)}, f32[3,784,512]{2,1,0:T(8,128)}, bf16...) custom-call(s32[3]{0:T(128)} %lens.3, ...), custom_call_target="tpu_custom_call" | custom-call | tf_op jit(solution)/shard_map/middle/pallas_call | solution.py:741
  117.2 70.1 %closing.1 = (bf16[3,512,512]{2,1,0:T(8,128)(2,1)}, f32[32,512]{1,0:T(8,128)}, f32[16,1024]{1,0:T(8,128)}, f32[16,512]{1,0:T(8,128)}, f32[16,1536]{1,0:T(8,128)}...) custom-call(bf16[3,512,512]{2,1,0:T(8,128)(2,1)} %x_ref.5, ...), custom_call_target="tpu_custom_call" | custom-call | tf_op jit(solution)/shard_map/closing/pallas_call | solution.py:1604
  187.3 4.8 %settle.1 = (f32[3,784,512]{2,1,0:T(8,128)}, f32[3,512,512]{2,1,0:T(8,128)}, f32[16,1536]{1,0:T(8,128)}, f32[16,1536]{1,0:T(8,128)}, f32[2,16,512]{2,1,0:T(8,128...) custom-call(f32[3,784,512]{2,1,0:T(8,128)} %get-tuple-element.72.g_m, ...), custom_call_target="tpu_custom_call", output_to_operand_aliasing={{0}: (0, {})} | custom-call | tf_op jit(solution)/shard_map/settle/pallas_call | solution.py:1668

commit v6 on v5

--- a/solution.py
+++ b/solution.py
@@ -27,7 +27,7 @@
     return {"wide": a * dims[1] + b, "narrow": x * 2 + c}
 
 
-def greet(dims, me, diagonal=False):
+def hail(dims, me, diagonal=False):
     a, b, x, c = me
     outer, inner, across = dims
     barrier = pltpu.get_barrier_semaphore()
@@ -39,7 +39,11 @@
         peers += [(a, lax.rem(b + j, inner), lax.rem(x + k, across), c) for j in range(1, inner) for k in range(1, across)]
     for peer in peers:
         pl.semaphore_signal(barrier, inc=1, device_id=device(dims, *peer), device_id_type=MESH)
-    pl.semaphore_wait(barrier, len(peers))
+    return len(peers)
+
+
+def greet(dims, me, count=0):
+    pl.semaphore_wait(pltpu.get_barrier_semaphore(), count or hail(dims, me))
 
 
 ALL = slice(None)
@@ -555,7 +559,7 @@
 
     @pl.when(tame)
     def _():
-        lax.fori_loop(0, HEADS, functools.partial(forward, False), 0, unroll=4)
+        lax.fori_loop(0, HEADS, functools.partial(forward, False), 0, unroll=8)
 
     @pl.when(jnp.logical_not(tame))
     def _():
@@ -856,7 +860,7 @@
     ((CROSS, 4),),
     ((PROJ, 4), (IN, 4), (OUT, 4)),
 )
-MEANTIME = {2: (0, 4), 3: (1, 0), 4: (1, 4), 5: (2, 4)}
+MEANTIME = {2: (0, 6), 3: (1, 2), 4: (2, 0), 5: (2, 6)}
 
 
 class Gathering:
@@ -989,12 +993,13 @@
 
     @pl.when(step == 0)
     def _():
+        hails = hail(dims, me)
         small[...] = jnp.zeros_like(small)
         small[0:10, : b_ref.shape[1]] = b_ref[...].astype(f32)
         small[10:13, : g_ref.shape[1]] = g_ref[...].astype(f32)
         small[13:14, : h_ref.shape[1]] = h_ref[...].astype(f32)
         small_low[...] = small[...].astype(bf16)
-        greet(dims, me)
+        greet(dims, me, hails)
         play(0)
         vectors = spread(h_small[...].reshape(-1, 128), b_ref.shape[1], width, 16)
         vec_ref[...] = vectors
@@ -1342,6 +1347,7 @@
 
 G_OUT, G_IN, G_ONE, G_CROSS, G_ZERO, G_HALF, G_REST, G_SMALL = range(8)
 SHORT = (G_REST, G_SMALL)
+FEW = 2
 EVENTS = {
     (0, 0): ((G_OUT, 0), (G_IN, 0), (G_ONE, 0)),
     (0, 1): ((G_OUT, 1),),
@@ -1388,10 +1394,13 @@
     def e_rows(h):
         return e_ref.at[pl.ds(pl.multiple_of(h * cells, 16), cells)]
 
-    def head_fetches(h):
-        pairs = ((e_any.at[h], e_rows(h)), (ckv_any.at[images - 1, h], ckv_ref.at[h]), (ckv_any.at[images - 1, HEADS + h], ckv_ref.at[HEADS + h]),
-                 (q_any.at[h], q_ref.at[h]), (mix_two_any.at[h], mix_two.at[h]), (gmix_two_any.at[h], gmix_two.at[h]))
-        return [pltpu.make_async_copy(src, dst, head_sem.at[h, k]) for k, (src, dst) in enumerate(pairs)]
+    def few_fetches(k):
+        few = pl.ds(k * FEW, FEW)
+        rows = pl.ds(k * FEW * cells, FEW * cells)
+        pairs = ((e_any.at[rows], e_ref.at[rows]), (ckv_any.at[images - 1, few], ckv_ref.at[few]),
+                 (ckv_any.at[images - 1, pl.ds(HEADS + k * FEW, FEW)], ckv_ref.at[pl.ds(HEADS + k * FEW, FEW)]),
+                 (q_any.at[few], q_ref.at[few]), (mix_two_any.at[few], mix_two.at[few]), (gmix_two_any.at[few], gmix_two.at[few]))
+        return [pltpu.make_async_copy(src, dst, head_sem.at[k, j]) for j, (src, dst) in enumerate(pairs)]
 
     def play(number, where):
         for item, stage in EVENTS.get((number, where), ()):
@@ -1407,27 +1416,31 @@
 
     @pl.when(step == 0)
     def _():
+        hails = hail(dims, me, True)
+        for fetch in fetches[:3] + few_fetches(0):
+            fetch.start()
+        greet(dims, me, hails)
         for fetch in fetches[:3]:
-            fetch.start()
-        for h in range(HEADS):
-            for fetch in head_fetches(h):
+            fetch.wait()
+        play(0, 0)
+        for k in range(1, HEADS // FEW):
+            for fetch in few_fetches(k):
                 fetch.start()
         for fetch in fetches[3:]:
             fetch.start()
         acc_col[...] = jnp.zeros_like(acc_col)
-        greet(dims, me, True)
-        for fetch in fetches[:3]:
-            fetch.wait()
-        play(0, 0)
-
-        for first in (0, some):
-            for h in range(first, first + some):
-                for fetch in head_fetches(h):
-                    fetch.wait()
-            for h in range(first, first + some):
+        def few_heads(k, _):
+            for fetch in few_fetches(k):
+                fetch.wait()
+            for j in range(FEW):
+                h = k * FEW + j
                 dq_ref[h], dkv_ref[h], dkv_ref[HEADS + h] = cross_back(
-                    h, e_rows(h)[...], ckv_ref[h], ckv_ref[HEADS + h], q_ref[h], gmix_two[h], mix_two[h], inv_two[h : h + 1, :])
-            play(0, 1 + first // some)
+                    h, e_rows(h)[...], ckv_ref[h], ckv_ref[HEADS + h], q_ref[h], gmix_two[h], mix_two[h], inv_two[pl.ds(h, 1), :])
+            for half_done in (1, 2):
+                pl.when((k + 1) * FEW == some * half_done)(functools.partial(play, 0, half_done))
+            return 0
+
+        lax.fori_loop(0, HEADS // FEW, few_heads, 0)
         for fetch in fetches[3:11]:
             fetch.wait()
         dq = dq_ref[...].reshape(width, tags)
@@ -1621,12 +1634,12 @@
             pltpu.VMEM((width, width), bf16), pltpu.VMEM((3 * width, width), bf16),
             pltpu.VMEM(heads, bf16), pltpu.VMEM(heads, bf16), pltpu.VMEM((tags, width), f32), pltpu.VMEM((some, HEAD_DIM, tags), bf16),
             pltpu.VMEM((3 * width // 2, width), f32), pltpu.VMEM((16, width), f32), pltpu.VMEM((2, width, 128), f32),
-        ] + [pltpu.VMEM(s, bf16) for s in lows] + [pltpu.SemaphoreType.DMA((HEADS, 6)), pltpu.SemaphoreType.DMA((13,))] + space
+        ] + [pltpu.VMEM(s, bf16) for s in lows] + [pltpu.SemaphoreType.DMA((HEADS // FEW, 6)), pltpu.SemaphoreType.DMA((13,))] + space
         + [pltpu.SemaphoreType.DMA((8, slots)), pltpu.SemaphoreType.DMA((8, slots))],
         compiler_params=pltpu.CompilerParams(collective_id=1, has_side_effects=True, vmem_limit_bytes=62 * MIB),
         name="closing",
     )(x, qkv, e_low, e_high, inv, mix, gmix, inv_two, vectors, g_vec, g_bin, scale_one, *low,
-      e, ckv, q, mix_two, gmix_two, mix, g_two, n_one, wt_cross, mem, acc_cross, acc_zero, w_proj, wt_self, g_resid)
+      e.reshape(HEADS * memory, tags), ckv, q, mix_two, gmix_two, mix, g_two, n_one, wt_cross, mem, acc_cross, acc_zero, w_proj, wt_self, g_resid)
 
 
 def settle(lanes, hidden_lanes, images, g_mem_in, m_last, tags, s_out, s_in, s_one, s_cross, s_zero, s_half, s_rest, small,

time: 192 us -> 192 us (level)
    pallas_call x1, Pallas kernels: 70.1 us -> 56.1 us  [run_closing(): pl.pallas_call(functools.partial(closing, dims), grid=(3 * images + 1,),...]
    pallas_call x1, Pallas kernels: 63.6 us -> 76.4 us  [run_middle(): pl.pallas_call(functools.partial(middle, held_back), grid_spec=pltpu.Pref...]
where the time goes in v6:
time: 192 us; the launch traced here: 191 us
  Pallas kernels  190 us (99%)
    pallas_call x1, Pallas kernels, run_middle(): pl.pallas_call(functools.partial(middle, held_back), grid_spec=pltpu.Pref...  76.4 us
    pallas_call x1, Pallas kernels, run_closing(): pl.pallas_call(functools.partial(closing, dims), grid=(3 * images + 1,),...  56.1 us
    pallas_call x1, Pallas kernels, run_opening(): pl.pallas_call(functools.partial(opening, dims), grid=(2 * images,), in_s...  53.1 us
    pallas_call x1, Pallas kernels, run_settle(): pl.pallas_call(functools.partial(settle, lanes, hidden_lanes, images), gr...  4.82 us

profile of v6, /device:TPU:0, one launch (start us, length us, event | category | flops | bytes accessed | tf_op | source)
XLA Modules:
  0.0 191.3 jit_solution(4046700461244431780)
XLA Ops:
  0.6 53.1 %opening.1 = (bf16[3,24,64,512]{3,2,1,0:T(8,128)(2,1)}, bf16[3,16,64,784]{3,2,1,0:T(8,128)(2,1)}, bf16[3,8,256,512]{3,2,1,0:T(8,128)(2,1)}, bf16[3,8,256,256]{3,...) custom-call(s32[3]{0:T(128)} %lens.3, ...), custom_call_target="tpu_custom_call" | custom-call | tf_op jit(solution)/shard_map/opening/pallas_call | solution.py:1113
  53.8 76.4 %middle.1 = (bf16[3,512,512]{2,1,0:T(8,128)(2,1)}, f32[2,512,512]{2,1,0:T(8,128)}, bf16[2,8,64,512]{3,2,1,0:T(8,128)(2,1)}, f32[3,784,512]{2,1,0:T(8,128)}, bf16...) custom-call(s32[3]{0:T(128)} %lens.3, ...), custom_call_target="tpu_custom_call" | custom-call | tf_op jit(solution)/shard_map/middle/pallas_call | solution.py:745
  130.2 56.1 %closing.1 = (bf16[3,512,512]{2,1,0:T(8,128)(2,1)}, f32[32,512]{1,0:T(8,128)}, f32[16,1024]{1,0:T(8,128)}, f32[16,512]{1,0:T(8,128)}, f32[16,1536]{1,0:T(8,128)}...) custom-call(bf16[3,512,512]{2,1,0:T(8,128)(2,1)} %x_ref.5, ...), custom_call_target="tpu_custom_call" | custom-call | tf_op jit(solution)/shard_map/closing/pallas_call | solution.py:1617
  186.3 4.8 %settle.1 = (f32[3,784,512]{2,1,0:T(8,128)}, f32[3,512,512]{2,1,0:T(8,128)}, f32[16,1536]{1,0:T(8,128)}, f32[16,1536]{1,0:T(8,128)}, f32[2,16,512]{2,1,0:T(8,128...) custom-call(f32[3,784,512]{2,1,0:T(8,128)} %get-tuple-element.72.g_m, ...), custom_call_target="tpu_custom_call", output_to_operand_aliasing={{0}: (0, {})} | custom-call | tf_op jit(solution)/shard_map/settle/pallas_call | solution.py:1681

commit v7 on v6

--- a/solution.py
+++ b/solution.py
@@ -540,9 +540,9 @@
     q_ref[...] = cq.reshape(q_ref.shape)
     leave(1, 5)
 
-    keys = ckv_ref[0, :HEADS].astype(f32)
-    queries = q_ref[...].astype(f32)
-    bound = jnp.max(jnp.sum(keys * keys, 1)) * jnp.max(jnp.sum(queries * queries, 1))
+    keys, queries = ckv_ref[0, :HEADS], q_ref[...]
+    keys, queries = keys * keys, queries * queries
+    bound = jnp.max(jnp.sum(keys.astype(f32), 1)) * jnp.max(jnp.sum(queries.astype(f32), 1))
     tame = bound < TAME * TAME
 
     def forward(shifted, h, _):
@@ -1677,10 +1677,10 @@
 
     rows = s_cross.shape[0]
     shapes = [s_cross.shape, s_cross.shape, (2, rows, width), s_in.shape, s_out.shape, (1, hidden_lanes), (3, lanes), (10, lanes)]
-    image = pl.BlockSpec((1, tags, width), lambda i: (i, 0, 0))
+    image = pl.BlockSpec((1, tags // 2, width), lambda i: (lax.div(i, 2), lax.rem(i, 2), 0))
     return pl.pallas_call(
         functools.partial(settle, lanes, hidden_lanes, images),
-        grid=(images,),
+        grid=(2 * images,),
         in_specs=[pl.BlockSpec(memory_space=pl.ANY), one(*m_last.shape), image] + [one(*s.shape) for s in shares],
         out_specs=[pl.BlockSpec((1,) + g_mem.shape[1:], lambda i: (images - 1, 0, 0)), image] + [out(*s) for s in shapes],
         out_shape=[sds(g_mem.shape, f32), sds(g_tags.shape, f32)] + [sds(s, f32) for s in shapes],

time: 192 us -> 193 us (level)
  no operation moved by 1% of the time
where the time goes in v7:
time: 193 us; the launch traced here: 192 us
  Pallas kernels  191 us (99%)
    pallas_call x1, Pallas kernels, run_middle(): pl.pallas_call(functools.partial(middle, held_back), grid_spec=pltpu.Pref...  77.1 us
    pallas_call x1, Pallas kernels, run_closing(): pl.pallas_call(functools.partial(closing, dims), grid=(3 * images + 1,),...  54.6 us
    pallas_call x1, Pallas kernels, run_opening(): pl.pallas_call(functools.partial(opening, dims), grid=(2 * images,), in_s...  53.1 us
    pallas_call x1, Pallas kernels, run_settle(): pl.pallas_call(functools.partial(settle, lanes, hidden_lanes, images), gr...  6.07 us

profile of v7, /device:TPU:0, one launch (start us, length us, event | category | flops | bytes accessed | tf_op | source)
XLA Modules:
  0.0 191.7 jit_solution(7622658440306105132)
XLA Ops:
  0.6 53.1 %opening.1 = (bf16[3,24,64,512]{3,2,1,0:T(8,128)(2,1)}, bf16[3,16,64,784]{3,2,1,0:T(8,128)(2,1)}, bf16[3,8,256,512]{3,2,1,0:T(8,128)(2,1)}, bf16[3,8,256,256]{3,...) custom-call(s32[3]{0:T(128)} %lens.3, ...), custom_call_target="tpu_custom_call" | custom-call | tf_op jit(solution)/shard_map/opening/pallas_call | solution.py:1113
  53.8 77.1 %middle.1 = (bf16[3,512,512]{2,1,0:T(8,128)(2,1)}, f32[2,512,512]{2,1,0:T(8,128)}, bf16[2,8,64,512]{3,2,1,0:T(8,128)(2,1)}, f32[3,784,512]{2,1,0:T(8,128)}, bf16...) custom-call(s32[3]{0:T(128)} %lens.3, ...), custom_call_target="tpu_custom_call" | custom-call | tf_op jit(solution)/shard_map/middle/pallas_call | solution.py:745
  130.9 54.6 %closing.1 = (bf16[3,512,512]{2,1,0:T(8,128)(2,1)}, f32[32,512]{1,0:T(8,128)}, f32[16,1024]{1,0:T(8,128)}, f32[16,512]{1,0:T(8,128)}, f32[16,1536]{1,0:T(8,128)}...) custom-call(bf16[3,512,512]{2,1,0:T(8,128)(2,1)} %x_ref.5, ...), custom_call_target="tpu_custom_call" | custom-call | tf_op jit(solution)/shard_map/closing/pallas_call | solution.py:1617
  185.5 6.1 %settle.1 = (f32[3,784,512]{2,1,0:T(8,128)}, f32[3,512,512]{2,1,0:T(8,128)}, f32[16,1536]{1,0:T(8,128)}, f32[16,1536]{1,0:T(8,128)}, f32[2,16,512]{2,1,0:T(8,128...) custom-call(f32[3,784,512]{2,1,0:T(8,128)} %get-tuple-element.72.g_m, ...), custom_call_target="tpu_custom_call", output_to_operand_aliasing={{0}: (0, {})} | custom-call | tf_op jit(solution)/shard_map/settle/pallas_call | solution.py:1681
